TPU v7x, 32 devices: a whole 2x2x4 slice. The times are simulated.
32 devices in a mesh: batch: 4 (over y, core), seq: 8 (over z, x).
Axes of the slice: x: 2, y: 2, z: 4, core: 2. Of those that a mesh axis runs over, the one named last changes fastest.
Arguments:
- block_input: bfloat16 [8, 1024, 512], P('batch', 'seq'), may hold values from -6 to 6
- cotangent: bfloat16 [8, 1024, 512], P('batch', 'seq'), may hold values from -6 to 6
- groups: int32 [8], P('batch'), may hold values from 0 to 7
- lengths: int32 [8], P('batch'), may hold values from 128 to 1024, as said below
- pair_table: float32 [8, 512], replicated, may hold values from -5 to 5
- qkv_weight: bfloat16 [512, 1536], replicated, may hold values from -0.25 to 0.25
- q_bias: float32 [512], replicated, may hold values from -3 to 3
- v_bias: float32 [512], replicated, may hold values from -3 to 3
- out_weight: bfloat16 [512, 512], replicated, may hold values from -0.5 to 0.5
- out_bias: float32 [512], replicated, may hold values from -2 to 2
- norm1_gain: float32 [512], replicated, may hold values from 0.5 to 1.5
- norm1_bias: float32 [512], replicated, may hold values from -2 to 2
- up_weight: bfloat16 [512, 2048], replicated, may hold values from -0.25 to 0.25
- up_bias: float32 [2048], replicated, may hold values from -3 to 3
- down_weight: bfloat16 [2048, 512], replicated, may hold values from -0.125 to 0.125
- down_bias: float32 [512], replicated, may hold values from -2 to 2
- norm2_gain: float32 [512], replicated, may hold values from 0.5 to 1.5
- norm2_bias: float32 [512], replicated, may hold values from -2 to 2
Outputs:
- layer_out: float32 [8, 1024, 512], P('batch', 'seq')
- input_grad: float32 [8, 1024, 512], P('batch', 'seq')
- pair_table_grad: float32 [8, 512], replicated
- qkv_weight_grad: float32 [512, 1536], replicated
- q_bias_grad: float32 [512], replicated
- v_bias_grad: float32 [512], replicated
- out_weight_grad: float32 [512, 512], replicated
- out_bias_grad: float32 [512], replicated
- norm1_gain_grad: float32 [512], replicated
- norm1_bias_grad: float32 [512], replicated
- up_weight_grad: float32 [512, 2048], replicated
- up_bias_grad: float32 [2048], replicated
- down_weight_grad: float32 [2048, 512], replicated
- down_bias_grad: float32 [512], replicated
- norm2_gain_grad: float32 [512], replicated
- norm2_bias_grad: float32 [512], replicated
Inputs may be any that keep to these rules, and one draw needn't show every extreme that they name: `lengths`: in each aligned block of 2 rows (the rows of one index of batch), one row, chosen by the seed, has length 1024.
All inputs are finite; a program needn't handle non-finite values.
Results may differ from a plain program's by a relative error of at most 0.014.
The roundings to bfloat16 on the way count: a program that leaves them out, or rounds other values in their place, can miss the bound.
Values may be sent and summed in bfloat16 or wider, within the bound.
A program may use at most 192 MiB of HBM per device.

v0:
```python
import jax
import jax.numpy as jnp
from jax import lax
from jax.sharding import PartitionSpec as P

HEADS = 8


highest = lax.Precision.HIGHEST
eps_norm = 1e-05


def layer_norm(hidden, norm_gain, norm_shift):
    row_mean = jnp.mean(hidden, axis=-1, keepdims=True)
    centred = hidden - row_mean
    spread = jnp.mean(centred * centred, axis=-1, keepdims=True)
    return centred * lax.rsqrt(spread + eps_norm) * norm_gain + norm_shift


def exact_gelu(pre_act):
    return jax.nn.gelu(pre_act, approximate=False)


def block_size():
    return 512


def to_heads(flat_rows, head_count):
    return flat_rows.reshape(
        flat_rows.shape[0], flat_rows.shape[1], head_count, flat_rows.shape[2] // head_count
    )


def masked_exp(query_block, key_block, key_first, row_lengths, score_scale):
    scores = (
        jnp.einsum("rihd,rjhd->rhij", query_block, key_block, preferred_element_type=jnp.float32)
        * score_scale
    )
    places = key_first + jnp.arange(key_block.shape[1], dtype=jnp.int32)
    usable = places[None, :] < row_lengths[:, None]
    return jnp.where(usable[:, None, None, :], jnp.exp(scores), 0.0)


def forward_piece(
    running, key_piece, value_piece, query_heads, row_lengths, score_scale, head_count
):
    piece_len = key_piece.shape[1]
    block_len = block_size()
    key_all = to_heads(key_piece, head_count)
    value_all = to_heads(value_piece, head_count)

    def forward_one_block(block_index, partial_sums):
        numerator, denominator = partial_sums
        block_first = block_index * block_len
        key_block = lax.dynamic_slice_in_dim(key_all, block_first, block_len, 1)
        value_block = lax.dynamic_slice_in_dim(value_all, block_first, block_len, 1)
        exp_scores = masked_exp(query_heads, key_block, block_first, row_lengths, score_scale)
        denominator = denominator + jnp.sum(exp_scores, axis=-1)
        numerator = numerator + jnp.einsum(
            "rhij,rjhd->rihd",
            exp_scores.astype(jnp.bfloat16),
            value_block,
            preferred_element_type=jnp.float32,
        )
        return (numerator, denominator)

    return lax.fori_loop(0, piece_len // block_len, forward_one_block, running)


def key_side(
    running,
    query_piece,
    grad_piece,
    total_piece,
    key_heads,
    value_heads,
    key_first,
    row_lengths,
    score_scale,
    head_count,
):
    piece_len = query_piece.shape[1]
    block_len = block_size()
    query_all = to_heads(query_piece.astype(jnp.bfloat16), head_count)
    grad_all = to_heads(grad_piece, head_count)
    value_wide = value_heads.astype(jnp.float32)

    def key_one_block(block_index, partial_grads):
        key_grad, value_grad = partial_grads
        block_first = block_index * block_len
        query_block = lax.dynamic_slice_in_dim(query_all, block_first, block_len, 1)
        grad_block = lax.dynamic_slice_in_dim(grad_all, block_first, block_len, 1)
        total_block = lax.dynamic_slice_in_dim(total_piece, block_first, block_len, 1)
        exp_scores = masked_exp(query_block, key_heads, key_first, row_lengths, score_scale)
        prob_grad = jnp.einsum(
            "rihd,rjhd->rhij",
            grad_block,
            value_wide,
            precision=highest,
            preferred_element_type=jnp.float32,
        )
        shift_grad = jnp.transpose(total_block, (0, 2, 1))[..., None]
        score_grad = (exp_scores * (prob_grad + shift_grad)).astype(jnp.bfloat16)
        key_grad = (
            key_grad
            + jnp.einsum(
                "rhij,rihd->rjhd", score_grad, query_block, preferred_element_type=jnp.float32
            )
            * score_scale
        )
        exp_low = exp_scores.astype(jnp.bfloat16).astype(jnp.float32)
        value_grad = value_grad + jnp.einsum(
            "rhij,rihd->rjhd",
            exp_low,
            grad_block,
            precision=highest,
            preferred_element_type=jnp.float32,
        )
        return (key_grad, value_grad)

    return lax.fori_loop(0, piece_len // block_len, key_one_block, running)


def query_side(
    running,
    key_piece,
    value_piece,
    query_heads,
    grad_heads,
    total_here,
    row_lengths,
    score_scale,
    head_count,
):
    piece_len = key_piece.shape[1]
    block_len = block_size()
    key_all = to_heads(key_piece, head_count)
    value_all = to_heads(value_piece, head_count)

    def query_one_block(block_index, query_grad):
        block_first = block_index * block_len
        key_block = lax.dynamic_slice_in_dim(key_all, block_first, block_len, 1)
        value_block = lax.dynamic_slice_in_dim(value_all, block_first, block_len, 1)
        exp_scores = masked_exp(query_heads, key_block, block_first, row_lengths, score_scale)
        prob_grad = jnp.einsum(
            "rihd,rjhd->rhij",
            grad_heads,
            value_block.astype(jnp.float32),
            precision=highest,
            preferred_element_type=jnp.float32,
        )
        score_grad = (exp_scores * (prob_grad + total_here[..., None])).astype(jnp.bfloat16)
        return (
            query_grad
            + jnp.einsum(
                "rhij,rjhd->rihd", score_grad, key_block, preferred_element_type=jnp.float32
            )
            * score_scale
        )

    return lax.fori_loop(0, piece_len // block_len, query_one_block, running)


def local(
    block_input,
    cotangent,
    groups,
    lengths,
    pair_table,
    qkv_weight,
    q_bias,
    v_bias,
    out_weight,
    out_bias,
    norm1_gain,
    norm1_bias,
    up_weight,
    up_bias,
    down_weight,
    down_bias,
    norm2_gain,
    norm2_bias,
):
    row_count, shard_len, model_width = block_input.shape
    head_count = HEADS
    head_size = model_width // head_count
    score_scale = head_size ** (-0.5)
    key_offset = lax.axis_index("seq") * shard_len
    pair_onehot = (
        groups[:, None] == jnp.arange(pair_table.shape[0], dtype=jnp.int32)[None, :]
    ).astype(jnp.float32)
    lifted = jnp.dot(pair_onehot, pair_table, precision=highest)
    start_x = block_input.astype(jnp.float32) + lifted[:, None, :]
    lowered = start_x.astype(jnp.bfloat16)
    projected = jnp.einsum("rtd,de->rte", lowered, qkv_weight, preferred_element_type=jnp.float32)
    query_rows = (projected[:, :, :model_width] + q_bias).astype(jnp.bfloat16)
    key_rows = projected[:, :, model_width : 2 * model_width].astype(jnp.bfloat16)
    value_rows = (projected[:, :, 2 * model_width :] + v_bias).astype(jnp.bfloat16)
    query_heads = to_heads(query_rows, head_count)
    key_heads = to_heads(key_rows, head_count)
    value_heads = to_heads(value_rows, head_count)
    zero_heads = jnp.zeros((row_count, shard_len, head_count, head_size), jnp.float32)
    zero_totals = jnp.zeros((row_count, head_count, shard_len), jnp.float32)
    incoming = (
        lax.all_gather(key_rows, "seq", axis=1, tiled=True),
        lax.all_gather(value_rows, "seq", axis=1, tiled=True),
    )
    numerator, denominator = forward_piece(
        (zero_heads, zero_totals),
        incoming[0],
        incoming[1],
        query_heads,
        lengths,
        score_scale,
        head_count,
    )
    inverse = 1.0 / jnp.transpose(denominator, (0, 2, 1))[..., None]
    attended = numerator * inverse
    attended_low = attended.reshape(row_count, shard_len, model_width).astype(jnp.bfloat16)
    attn_out = (
        jnp.einsum("rtd,de->rte", attended_low, out_weight, preferred_element_type=jnp.float32)
        + out_bias
    )
    normed, norm1_back = jax.vjp(layer_norm, start_x + attn_out, norm1_gain, norm1_bias)
    normed_low = normed.astype(jnp.bfloat16)
    pre_act = (
        jnp.einsum("rtd,df->rtf", normed_low, up_weight, preferred_element_type=jnp.float32)
        + up_bias
    )
    activated, gelu_back = jax.vjp(exact_gelu, pre_act)
    activated_low = activated.astype(jnp.bfloat16)
    ffn_out = (
        jnp.einsum("rtf,fd->rtd", activated_low, down_weight, preferred_element_type=jnp.float32)
        + down_bias
    )
    layer_out, norm2_back = jax.vjp(layer_norm, ffn_out + normed + start_x, norm2_gain, norm2_bias)
    second_grad, norm2_gain_grad, norm2_bias_grad = norm2_back(cotangent.astype(jnp.float32))
    ffn_grad = second_grad.astype(jnp.bfloat16)
    down_bias_grad = jnp.sum(ffn_grad.astype(jnp.float32), axis=(0, 1))
    down_weight_grad = jnp.einsum(
        "rtf,rtd->fd", activated_low, ffn_grad, preferred_element_type=jnp.float32
    )
    act_grad = jnp.einsum("rtd,fd->rtf", ffn_grad, down_weight, preferred_element_type=jnp.float32)
    pre_grad = gelu_back(act_grad)[0].astype(jnp.bfloat16)
    up_bias_grad = jnp.sum(pre_grad.astype(jnp.float32), axis=(0, 1))
    up_weight_grad = jnp.einsum(
        "rtd,rtf->df", normed_low, pre_grad, preferred_element_type=jnp.float32
    )
    normed_grad = second_grad + jnp.einsum(
        "rtf,df->rtd", pre_grad, up_weight, preferred_element_type=jnp.float32
    )
    first_grad, norm1_gain_grad, norm1_bias_grad = norm1_back(normed_grad)
    attn_grad = first_grad.astype(jnp.bfloat16)
    out_bias_grad = jnp.sum(attn_grad.astype(jnp.float32), axis=(0, 1))
    out_weight_grad = jnp.einsum(
        "rtd,rte->de", attended_low, attn_grad, preferred_element_type=jnp.float32
    )
    attended_grad = to_heads(
        jnp.einsum("rte,de->rtd", attn_grad, out_weight, preferred_element_type=jnp.float32),
        head_count,
    )
    numer_grad = attended_grad * inverse
    total_grad = -jnp.sum(attended_grad * attended, axis=-1) * inverse[..., 0]
    grad_rows = numer_grad.reshape(row_count, shard_len, model_width)
    total_here = jnp.transpose(total_grad, (0, 2, 1))
    incoming = (
        lax.all_gather(query_rows.astype(jnp.float32), "seq", axis=1, tiled=True),
        lax.all_gather(grad_rows, "seq", axis=1, tiled=True),
        lax.all_gather(total_grad, "seq", axis=1, tiled=True),
    )
    key_grad, value_grad = key_side(
        (zero_heads, zero_heads),
        incoming[0],
        incoming[1],
        incoming[2],
        key_heads,
        value_heads,
        key_offset,
        lengths,
        score_scale,
        head_count,
    )
    incoming = (
        lax.all_gather(key_rows, "seq", axis=1, tiled=True),
        lax.all_gather(value_rows, "seq", axis=1, tiled=True),
    )
    query_grad = query_side(
        zero_heads,
        incoming[0],
        incoming[1],
        query_heads,
        numer_grad,
        total_here,
        lengths,
        score_scale,
        head_count,
    )
    flat_shape = (row_count, shard_len, model_width)
    query_low = query_grad.reshape(flat_shape).astype(jnp.bfloat16)
    key_low = key_grad.reshape(flat_shape).astype(jnp.bfloat16)
    value_low = value_grad.reshape(flat_shape).astype(jnp.bfloat16)
    qkv_grad = jnp.concatenate([query_low, key_low, value_low], axis=-1)
    qkv_weight_grad = jnp.einsum(
        "rtd,rte->de", lowered, qkv_grad, preferred_element_type=jnp.float32
    )
    q_bias_grad = jnp.sum(query_low.astype(jnp.float32), axis=(0, 1))
    v_bias_grad = jnp.sum(value_low.astype(jnp.float32), axis=(0, 1))
    input_grad = (
        jnp.einsum("rte,de->rtd", qkv_grad, qkv_weight, preferred_element_type=jnp.float32)
        + first_grad
        + second_grad
    )
    pair_table_grad = jnp.dot(
        jnp.transpose(pair_onehot), jnp.sum(input_grad, axis=1), precision=highest
    )
    summed = lax.psum(
        (
            pair_table_grad,
            qkv_weight_grad,
            q_bias_grad,
            v_bias_grad,
            out_weight_grad,
            out_bias_grad,
            norm1_gain_grad,
            norm1_bias_grad,
            up_weight_grad,
            up_bias_grad,
            down_weight_grad,
            down_bias_grad,
            norm2_gain_grad,
            norm2_bias_grad,
        ),
        ("batch", "seq"),
    )
    return (
        layer_out,
        input_grad,
        summed[0],
        summed[1],
        summed[2],
        summed[3],
        summed[4],
        summed[5],
        summed[6],
        summed[7],
        summed[8],
        summed[9],
        summed[10],
        summed[11],
        summed[12],
        summed[13],
    )


def solution(mesh):
    in_specs = (
        P("batch", "seq", None),
        P("batch", "seq", None),
        P("batch"),
        P("batch"),
        P(),
        P(),
        P(),
        P(),
        P(),
        P(),
        P(),
        P(),
        P(),
        P(),
        P(),
        P(),
        P(),
        P(),
    )
    out_specs = (
        P("batch", "seq", None),
        P("batch", "seq", None),
        P(),
        P(),
        P(),
        P(),
        P(),
        P(),
        P(),
        P(),
        P(),
        P(),
        P(),
        P(),
        P(),
        P(),
    )
    return jax.shard_map(local, mesh=mesh, in_specs=in_specs, out_specs=out_specs, check_vma=False)
```

profile of v0, /device:TPU:1, one launch (start us, length us, event | category | flops | bytes accessed | tf_op | source)
XLA Modules:
  0.0 525.2 jit_solution(14312206927684130852)
XLA Ops:
  8.3 2.1 fusion.71
  17.0 45.9 %all-gather.5.cloned.1.call-done = bf16[2,1024,512]{2,1,0:T(8,128)(2,1)} async-done(((bf16[2,128,512]{2,1,0:T(8,128)(2,1)}), bf16[2,1024,512]{2,1,0:T(8,128)(2,1)}) %all-gather.5.cloned.1.call-update) | async-done | bytes 2097168 | tf_op jit(solution)/shard_map/all_gather | solution.py:206
  62.9 3.9 copy.52
  66.8 46.1 %all-gather.7.cloned.1.call-done = bf16[2,1024,512]{2,1,0:T(8,128)(2,1)} async-done(((bf16[2,128,512]{2,1,0:T(8,128)(2,1)}), bf16[2,1024,512]{2,1,0:T(8,128)(2,1)}) %all-gather.7.cloned.1.call-update) | async-done | bytes 2097168 | tf_op jit(solution)/shard_map/all_gather | solution.py:205
  112.9 3.9 copy.53
  116.8 8.1 %while.46 = (s32[]{:T(128)}, f32[2,128,8,64]{1,3,2,0:T(8,128)S(1)}, f32[2,8,128]{2,1,0:T(8,128)S(1)}, bf16[2,1024,8,64]{1,3,2,0:T(8,128)(2,1)}, s32[2]{0:T(128)S...) while((s32[]{:T(128)}, f32[2,128,8,64]{1,3,2,0:T(8,128)S(1)}, ...), condition=%wide.region_2.3_spmd.clone, body=%wide.region_0.2_spmd.clone.sunk | while | flops 274992640 | bytes 20226268 | solution.py:67
  116.9 2.7 bitcast_reduce_fusion.2
  121.0 2.8 bitcast_reduce_fusion.2
  131.1 4.8 multiply_convert_fusion.2
  152.1 16.0 %while.47 = (s32[]{:T(128)}, f32[2,128,8,64]{1,3,2,0:T(8,128)}, bf16[2,1024,8,64]{1,3,2,0:T(8,128)(2,1)}, s32[2]{0:T(128)S(1)}, bf16[2,128,8,64]{3,2,1,0:T(8,128...) while((s32[]{:T(128)}, f32[2,128,8,64]{1,3,2,0:T(8,128)}, ...), condition=%wide.region_13.14_spmd.clone, body=%wide.region_12.13_spmd.clone.sunk | while | flops 1079379456 | bytes 30686496 | solution.py:161
  152.2 2.2 fusion.172
  154.4 3.0 multiply_convert_fusion.6
  160.2 2.2 fusion.172
  162.4 3.0 multiply_convert_fusion.6
  170.2 4.1 copy.60
  174.3 24.6 %all_gather.21 = f32[2,1024,8]{1,2,0:T(8,128)S(1)} all-gather(f32[2,128,8]{1,2,0:T(8,128)S(1)} %negate_multiply_fusion.1), channel_id=1, replica_groups=mesh['batch'=4,'seq'=8] {'seq'}, dimensions={1}, use_global_device_ids=true | all-gather | bytes 73728 | tf_op jit(solution)/shard_map/all_gather | solution.py:269
  200.2 3.8 convolution_bitcast_fusion.1
  204.0 2.9 convolution_bitcast_fusion.2
  206.8 30.3 %all-gather.11.cloned.1.call-done = f32[2,1024,512]{2,1,0:T(8,128)} async-done(((f32[2,128,512]{2,1,0:T(8,128)}), f32[2,1024,512]{2,1,0:T(8,128)}) %all-gather.11.cloned.1.call-update) | async-done | bytes 4194320 | tf_op jit(solution)/shard_map/all_gather | solution.py:268
  237.2 5.3 %copy.63 = f32[2,1024,512]{1,2,0:T(8,128)} copy(f32[2,1024,512]{2,1,0:T(8,128)} %all-gather.11.cloned.1.call-done) | data formatting | bytes 8388608 | tf_op jit(solution)/shard_map/all_gather | solution.py:268
  242.5 28.5 %while.48 = (s32[]{:T(128)}, f32[2,128,8,64]{1,3,2,0:T(8,128)S(1)}, f32[2,128,8,64]{1,3,2,0:T(8,128)S(1)}, bf16[2,1024,8,64]{1,3,2,0:T(8,128)(2,1)}, s32[]{:T(12...) while((s32[]{:T(128)}, f32[2,128,8,64]{1,3,2,0:T(8,128)S(1)}, ...), condition=%wide.region_15.16_spmd.clone, body=%wide.region_14.15_spmd.clone.sunk | while | flops 1888092544 | bytes 43354624 | solution.py:121
  242.6 2.2 fusion.182
  246.9 7.9 %multiply_convert_fusion.7 = bf16[2,8,512,128]{3,2,1,0:T(8,128)(2,1)S(1)} fusion(f32[2,8,512,128]{3,2,1,0:T(8,128)S(1)} %fusion.182, f32[2,8,512]{2,1,0:T(8,128)S(1)} %dynamic-slice_bitcast_fusion.2, pred[2,128]{1,0:T(4,128)(4,1)S(1)} %broadcast_compare_fusion.8, f32[2,1024,8,64]{1,3,2,0:T(8,128)S(1)} %copy-done.2, s32[]{:T(128)S(6)} %select_n.95, ...), kind=kOutput, calls=%fused_computation.34.clone.1 | convolution fusion | flops 810549248 | bytes 9470468 | tf_op jit(solution)/shard_map/while/body/eval_jaxpr/rihd,rjhd->rhij/dot_general | solution.py:95
  256.9 2.2 fusion.182
  261.1 7.9 %multiply_convert_fusion.7 = bf16[2,8,512,128]{3,2,1,0:T(8,128)(2,1)S(1)} fusion(f32[2,8,512,128]{3,2,1,0:T(8,128)S(1)} %fusion.182, f32[2,8,512]{2,1,0:T(8,128)S(1)} %dynamic-slice_bitcast_fusion.2, pred[2,128]{1,0:T(4,128)(4,1)S(1)} %broadcast_compare_fusion.8, f32[2,1024,8,64]{1,3,2,0:T(8,128)S(1)} %copy-done.2, s32[]{:T(128)S(6)} %select_n.95, ...), kind=kOutput, calls=%fused_computation.34.clone.1 | convolution fusion | flops 810549248 | bytes 9470468 | tf_op jit(solution)/shard_map/while/body/eval_jaxpr/rihd,rjhd->rhij/dot_general | solution.py:95
  272.1 2.3 convolution_bitcast_fusion
  275.6 2.8 fusion.124
  278.7 42.7 %all-reduce = (f32[8,512]{1,0:T(8,128)}, f32[512]{0:T(512)}, f32[512]{0:T(512)}, f32[512]{0:T(512)}, f32[512]{0:T(512)}, /*index=5*/f32[512]{0:T(512)}, f32[2048...) all-reduce(f32[8,512]{1,0:T(8,128)S(1)} %fusion.110, ...), channel_id=1, replica_groups=mesh['batch'=4,'seq'=8] {'batch','seq'}, use_global_device_ids=true, to_apply=%region_17.18 | all-reduce | flops 10240 | bytes 81920 | tf_op jit(solution)/shard_map/psum | solution.py:316
  321.4 185.6 %all-reduce.4.cloned.1.call-done = (f32[512,1536]{1,0:T(8,128)}, f32[512,512]{1,0:T(8,128)}, f32[512,2048]{1,0:T(8,128)}, f32[2048,512]{1,0:T(8,128)}) async-done(((f32[512,1536]{1,0:T(8,128)}, f32[512,512]{1,0:T(8,128)}, f32[512,2048]{1,0:T(8,128)}, f32[2048,512]{1,0:T(8,128)}), (f32[512,1536]{1,0:T(8,128)}, f32[512,512]{1,0:T(8,128)}, f32[512,2048]{1,0:T(8,128)}, ...) | async-done | bytes 12582928 | tf_op jit(solution)/shard_map/psum | solution.py:316
  507.0 3.9 copy.122
  511.9 2.1 copy.124
  515.6 2.1 copy.125
  (195 shorter events, 55.2 us)
Async XLA Ops:
  7.2 122.5 %copy-start = (bf16[512,2048]{1,0:T(8,128)(2,1)S(1)}, bf16[512,2048]{1,0:T(8,128)(2,1)}, u32[]{:S(2)}) copy-start(bf16[512,2048]{1,0:T(8,128)(2,1)} %param.36) | copy-start | bytes 6291460
  7.2 4.4 copy-start.41
  7.2 4.3 copy-start.40
  7.2 55.7 %all-gather.5.cloned.1.call-start = ((), (), s32[]{:S(2)}) async-start(), calls=%async_computation | async-start | bytes 2359296 | tf_op jit(solution)/shard_map/all_gather | solution.py:206
  12.5 100.4 %all-gather.7.cloned.1.call-start = ((), (), s32[]{:S(2)}) async-start(), calls=%async_computation.1 | async-start | bytes 2359296 | tf_op jit(solution)/shard_map/all_gather | solution.py:205
  14.4 155.8 %all-gather.9.cloned.1.call-start = ((), (), s32[]{:S(2)}) async-start(), calls=%async_computation.2 | async-start | bytes 2359296 | tf_op jit(solution)/shard_map/all_gather | solution.py:267
  15.1 222.0 %all-gather.11.cloned.1.call-start = ((), (), s32[]{:S(2)}) async-start(), calls=%async_computation.3 | async-start | bytes 4718592 | tf_op jit(solution)/shard_map/all_gather | solution.py:268
  66.8 50.0 %copy-start.37 = (s32[2]{0:T(128)S(1)}, s32[2]{0:T(128)}, u32[]{:S(2)}) copy-start(s32[2]{0:T(128)} %param.27) | copy-start | bytes 28
  125.0 3.0 copy-start.17
  125.0 4.7 copy-start.36
  125.0 4.7 copy-start.38
  125.0 4.7 copy-start.46
  125.1 5.9 %copy-start.25 = (bf16[2,128,8,64]{1,3,2,0:T(8,128)(2,1)}, bf16[2,128,8,64]{1,3,2,0:T(8,128)(2,1)S(1)}, u32[]{:S(2)}) copy-start(bf16[2,128,8,64]{1,3,2,0:T(8,128)(2,1)S(1)} %multiply_convert_fusion.3) | copy-start | bytes 786436
  129.4 12.3 %copy-start.8 = (f32[2,128,512]{2,1,0:T(8,128)}, f32[2,128,512]{2,1,0:T(8,128)S(1)}, u32[]{:S(2)}) copy-start(f32[2,128,512]{2,1,0:T(8,128)S(1)} %get-tuple-element.678) | copy-start | bytes 1572868
  131.0 4.8 copy-start.45
  131.0 4.8 copy-start.47
  136.9 3.3 copy-start.13
  143.0 3.1 copy-start.21
  144.3 362.7 %all-reduce.4.cloned.1.call-start = ((), (), s32[]{:S(2)}) async-start(), calls=%async_computation.4 | async-start | bytes 25165824 | tf_op jit(solution)/shard_map/psum | solution.py:316
  154.4 3.0 copy-start.5
  162.4 3.0 copy-start.5
  170.2 28.7 %copy-start.24 = (bf16[2,128,512]{2,1,0:T(8,128)(2,1)S(1)}, bf16[2,128,512]{2,1,0:T(8,128)(2,1)}, u32[]{:S(2)}) copy-start(bf16[2,128,512]{2,1,0:T(8,128)(2,1)} %copy-done.23) | copy-start | bytes 786436
  170.2 28.7 %copy-start.26 = (bf16[2,128,8,64]{1,3,2,0:T(8,128)(2,1)S(1)}, bf16[2,128,8,64]{1,3,2,0:T(8,128)(2,1)}, u32[]{:S(2)}) copy-start(bf16[2,128,8,64]{1,3,2,0:T(8,128)(2,1)} %copy-done.25) | copy-start | bytes 786436
  170.2 30.0 %copy-start.11 = (bf16[2,128,2048]{2,1,0:T(8,128)(2,1)S(1)}, bf16[2,128,2048]{2,1,0:T(8,128)(2,1)}, u32[]{:S(2)}) copy-start(bf16[2,128,2048]{2,1,0:T(8,128)(2,1)} %copy-done.10) | copy-start | bytes 3145732
  200.2 3.8 copy-start.9
  200.2 3.8 copy-start.32
  206.8 35.7 %copy-start.7 = (f32[2,128,8,64]{1,3,2,0:T(8,128)S(1)}, f32[2,128,8,64]{1,3,2,0:T(8,128)}, u32[]{:S(2)}) copy-start(f32[2,128,8,64]{1,3,2,0:T(8,128)} %custom-call.4) | copy-start | bytes 1572868
  275.6 3.1 copy-start.44
  507.0 3.9 copy-start.34
  507.0 4.9 copy-start.16
  511.9 3.7 copy-start.15
  515.6 3.1 copy-start.1
  (27 other events, 46.7 us)
Sparse Core Ops, SparseCore 0:
  12.7 50.2 all-gather.4
  65.1 47.7 all-gather.6
  115.1 47.7 all-gather.8
  164.9 72.2 all-gather.10
  274.5 232.4 all-reduce.3
where the time goes:
time: 528 us; the launch traced here: 525 us
  waiting for transfers between devices  309 us (59%)
  matrix products  73.8 us (14%)
  blocking collectives  67.3 us (13%)
  local copies, waits for them, and re-layouts  49.4 us (9%)
  between operations  14.4 us (3%)
  other arithmetic  10.9 us (2%)
    psum x1, waiting for transfers between devices, local(): lax.psum((pair_table_grad, qkv_weight_grad, q_bias_grad, v_bias_grad, out...  186 us
    all_gather x1, waiting for transfers between devices, local(): lax.all_gather(key_rows, 'seq', axis=1, tiled=True)  46.1 us
    all_gather x1, waiting for transfers between devices, local(): lax.all_gather(value_rows, 'seq', axis=1, tiled=True)  45.9 us
    psum x1, blocking collectives, local(): lax.psum((pair_table_grad, qkv_weight_grad, q_bias_grad, v_bias_grad, out...  42.7 us
    all_gather x1, waiting for transfers between devices, local(): lax.all_gather(grad_rows, 'seq', axis=1, tiled=True)  30.3 us
    all_gather x1, blocking collectives, local(): lax.all_gather(total_grad, 'seq', axis=1, tiled=True)  24.6 us
    unnamed x95, local copies, waits for them, and re-layouts  19.8 us
    dot_general x2, matrix products, key_one_block(): jnp.einsum('rihd,rjhd->rhij', grad_block, value_wide, precision=highest,...  15.9 us
  transfers between devices with their start and end apart: 5, of which 4 were waited for; matrix products, arithmetic and copies ran while one was open for 15% of the time, Pallas kernels for 0%

commit v1 on v0

--- a/solution.py
+++ b/solution.py
@@ -1,6 +1,8 @@
 import jax
 import jax.numpy as jnp
 from jax import lax
+from jax.experimental import pallas as pl
+from jax.experimental.pallas import tpu as pltpu
 from jax.sharding import PartitionSpec as P
 
 HEADS = 8
@@ -352,6 +354,664 @@
     )
 
 
+MESH = pl.DeviceIdType.MESH
+f32, bf16 = jnp.float32, jnp.bfloat16
+LANES = 9
+
+
+def mm(a, b):
+    return jnp.dot(a, b, preferred_element_type=f32)
+
+
+def mm_nt(a, b):
+    return lax.dot_general(a, b, (((1,), (1,)), ((), ())), preferred_element_type=f32)
+
+
+def mm_tn(a, b):
+    return lax.dot_general(a, b, (((0,), (0,)), ((), ())), preferred_element_type=f32)
+
+
+class Numbers:
+    def __init__(self):
+        self.count = 0
+        self.first = {}
+
+    def take(self, name, size=1):
+        self.first[name] = self.count
+        self.count += size
+
+    def __getitem__(self, name):
+        return self.first[name]
+
+
+def semaphore_numbers():
+    numbers = Numbers()
+    for name, size in (
+        ("x", 2), ("cot", 2), ("lo", 2), ("ig", 2),
+        ("xn", 2), ("core_own", 2), ("core_far", 2), ("meta", 1),
+        ("o", 3), ("do", 3), ("dx_core", 2), ("dx_x", 1), ("vec", 6),
+        ("lane", LANES * 12), ("qkv", 3 * 12),
+    ):
+        numbers.take(name, size)
+    return numbers
+
+
+NUM = semaphore_numbers()
+LOCAL = 24 + LANES + 8
+
+
+def fused(
+    x_in, cot_in, groups, lengths, table_in, wqkv_in, qb_in, vb_in, wo_in, ob_in, g1_in, b1_in,
+    wup_in, ub_in, wdn_in, db_in, g2_in, b2_in,
+    lo_out, ig_out, gw_out, gqkv_out, vec_out,
+    xb, lowb, cotb, table, meta, meta_far, wq, wo, wup, wdn, qb, vb, ob, g1, b1, ub, db, g2, b2,
+    q, k, v, vaug, vback, att, inv, obuf, abuf, gelu_grad, act, pre_grad, res, lob, igb,
+    dob, dor, probs, dq, dkt, dvt, dqkv, dxb, dxr0, dxr1,
+    vecb, vecr, vecz,
+    own, r0, r1, r2, r3, full, qown, qr1, qr3, qfull,
+    ssem, rsem, lsem,
+):
+    b_index, s_index = lax.axis_index("batch"), lax.axis_index("seq")
+    x, z = s_index % 2, s_index // 2
+    y, c = b_index // 2, b_index % 2
+    me = 2 * x + c
+
+    def dev(x, y, z, c):
+        return (2 * y + c, 2 * z + x)
+
+    core_dev = dev(x, y, z, 1 - c)
+    x_dev = dev(1 - x, y, z, c)
+    y_dev = dev(x, 1 - y, z, c)
+    diag_dev = dev(1 - x, y, z, 1 - c)
+    z_devs = [dev(x, y, (z + d) % 4, c) for d in (1, 2, 3)]
+    crossing = c != z // 2
+
+    pending = []
+
+    def send(src, dst, s_number, r_number, device, when=None):
+        copy = pltpu.make_async_remote_copy(
+            src_ref=src, dst_ref=dst, send_sem=ssem.at[s_number], recv_sem=rsem.at[r_number],
+            device_id=device, device_id_type=MESH,
+        )
+        if when is None:
+            copy.start()
+        else:
+            pl.when(when)(copy.start)
+        pending.append((copy, when))
+
+    def arrived(dst, number):
+        pltpu.make_async_remote_copy(
+            src_ref=dst, dst_ref=dst, send_sem=ssem.at[number], recv_sem=rsem.at[number],
+            device_id=core_dev, device_id_type=MESH,
+        ).wait_recv()
+
+    local_copies = []
+
+    def fetch(src, dst):
+        copy = pltpu.make_async_copy(src, dst, lsem.at[len(local_copies)])
+        copy.start()
+        local_copies.append(copy)
+        return copy
+
+    wait_qkv = [fetch(table_in, table), fetch(qb_in, qb), fetch(vb_in, vb)]
+    for t in range(3):
+        columns = pl.ds(pl.multiple_of(512 * t + 128 * me, 128), 128)
+        wait_qkv.append(fetch(wqkv_in.at[:, columns], wq.at[:, pl.ds(128 * t, 128)]))
+    wait_ffn = [
+        fetch(a, b)
+        for a, b in ((wo_in, wo), (ob_in, ob), (g1_in, g1), (b1_in, b1), (wup_in, wup), (ub_in, ub),
+                     (wdn_in, wdn), (db_in, db), (g2_in, g2), (b2_in, b2))
+    ]
+
+    barrier = pltpu.get_barrier_semaphore()
+    near = [core_dev, x_dev, y_dev, diag_dev] + z_devs
+    for device in near:
+        pl.semaphore_signal(barrier, inc=1, device_id=device, device_id_type=MESH)
+
+    @pl.when(crossing)
+    def _():
+        for i in range(2):
+            pl.semaphore_signal(
+                barrier, inc=1, device_id=dev(x, y, 2 * c + i, z // 2), device_id_type=MESH
+            )
+        pl.semaphore_wait(barrier, len(near) + 2)
+
+    @pl.when(jnp.logical_not(crossing))
+    def _():
+        pl.semaphore_wait(barrier, len(near))
+
+    own_slot = 4 * x + 2 * c
+    far_slot = 4 * (1 - x) + 2 * c
+
+    def to_peer(src, dst, i, name, here):
+        is_self = 2 * c + i == z
+        send(src, dst, NUM[name] + i, NUM[name] + z % 2, dev(x, y, 2 * c + i, z // 2),
+             when=jnp.logical_not(is_self))
+
+    first = jnp.where(crossing, 1 - c, z % 2)
+    for i in (first, 1 - first):
+        to_peer(x_in.at[i], xb.at[4 * x + z], i, "x", None)
+    for i in (0, 1):
+        to_peer(cot_in.at[i], cotb.at[z % 2], i, "cot", None)
+
+    def own_block(src, dst, number):
+        return pltpu.make_async_copy(src, dst, lsem.at[number])
+
+    self_x = own_block(x_in.at[z % 2], xb.at[4 * x + z], LOCAL - 1)
+    self_cot = own_block(cot_in.at[z % 2], cotb.at[z % 2], LOCAL - 2)
+
+    @pl.when(jnp.logical_not(crossing))
+    def _():
+        self_x.start()
+        self_cot.start()
+        self_x.wait()
+
+    for w in wait_qkv:
+        w.wait()
+    slot = z % 2
+    group, length = groups[slot], lengths[slot]
+    meta[0:1, :] = table[pl.ds(group, 1), :]
+    meta[1:2, :] = jnp.full((1, 512), length.astype(f32))
+    meta[2:3, :] = jnp.full((1, 512), group.astype(f32))
+    meta[3:8, :] = jnp.zeros((5, 512), f32)
+    send(meta, meta_far, NUM["meta"], NUM["meta"], core_dev)
+
+    for i in (first, 1 - first):
+        @pl.when(2 * c + i != z)
+        def _():
+            arrived(xb.at[own_slot + i], NUM["x"] + i)
+        send(xb.at[own_slot + i], xb.at[own_slot + i], NUM["xn"] + i, NUM["xn"] + i, x_dev)
+        send(xb.at[own_slot + i], xb.at[own_slot + i], NUM["core_own"] + i, NUM["core_own"] + i, core_dev)
+
+    arrived(meta_far, NUM["meta"])
+    facts = jnp.where(crossing, meta_far[...], meta[...])
+    pair_row, length_row, group_row = facts[0:1, :], facts[1:2, :], facts[2:3, :]
+    row_length = length_row[:, 0:128]
+
+    lane = lax.broadcasted_iota(jnp.int32, (1, 128), 1)
+    head_lanes = [lane < 64, lane >= 64]
+
+    def project(base, natural):
+        low = (xb[pl.ds(base, 2)].reshape(256, 512).astype(f32) + pair_row).astype(bf16)
+        lowb[pl.ds(base, 2)] = low.reshape(2, 128, 512)
+        rows = pl.ds(pl.multiple_of(base * 128, 256), 256)
+        y_all = mm(low, wq[...])
+        row = lax.broadcasted_iota(jnp.int32, (256, 1), 0)
+        place = natural + row + jnp.where(row >= 128, 128, 0)
+        usable = place.astype(f32) < row_length
+        q_bias = qb[:, pl.ds(pl.multiple_of(128 * me, 128), 128)]
+        v_bias = vb[:, pl.ds(pl.multiple_of(128 * me, 128), 128)]
+        q[rows, :] = (y_all[:, 0:128] + q_bias).astype(bf16) * jnp.asarray(0.125, bf16)
+        k[rows, :] = jnp.where(usable, y_all[:, 128:256], 0.0).astype(bf16)
+        value = jnp.where(usable, y_all[:, 256:384] + v_bias, 0.0)
+        one = jnp.where(usable, 1.0, 0.0)
+        for h in range(2):
+            vaug[h, rows, 0:128] = jnp.where(head_lanes[h], value, 0.0).astype(bf16)
+            vaug[h, rows, 128:256] = jnp.where(head_lanes[h], one, 0.0).astype(bf16)
+            edge = 64 * (1 - h)
+            extra = jnp.where((lane == edge) | (lane == edge + 1), one, 0.0)
+            vback[h, rows, :] = jnp.where(head_lanes[h], value, extra).astype(bf16)
+
+    project(own_slot, 128 * (4 * c + x))
+    for i in (first, 1 - first):
+        arrived(xb.at[far_slot + i], NUM["xn"] + i)
+        send(xb.at[far_slot + i], xb.at[far_slot + i], NUM["core_far"] + i, NUM["core_far"] + i, core_dev)
+    project(far_slot, 128 * (4 * c + 1 - x))
+    for name, base, natural in (
+        ("core_own", 4 * x + 2 * (1 - c), 128 * (4 * (1 - c) + x)),
+        ("core_far", 4 * (1 - x) + 2 * (1 - c), 128 * (4 * (1 - c) + 1 - x)),
+    ):
+        for i in range(2):
+            arrived(xb.at[base + i], NUM[name] + i)
+        project(base, natural)
+
+    order = [(1 - x, c), (1 - x, 1 - c), (x, 1 - c), (x, c)]
+    for step, (ox, oc) in enumerate(order):
+        owner = 2 * ox + oc
+        rows = pl.ds(pl.multiple_of(256 * owner, 256), 256)
+        q_rows = q[rows, :]
+        total = jnp.zeros((256, 256), f32)
+        for h in range(2):
+            scores = mm_nt(jnp.where(head_lanes[h], q_rows, 0), k[...])
+            prob = jnp.exp(scores).astype(bf16)
+            probs[h, rows, :] = prob
+            total = total + mm(prob, vaug[h])
+        inverse = 1.0 / total[:, 128:256]
+        attended = total[:, 0:128] * inverse
+        att[rows, :] = attended
+        inv[rows, :] = inverse
+        columns = pl.ds(pl.multiple_of(128 * me, 128), 128)
+        if step < 3:
+            obuf[step] = attended.astype(bf16)
+            send(obuf.at[step], abuf.at[:, columns], NUM["o"] + step, NUM["o"] + step, dev(ox, y, z, oc))
+        else:
+            abuf[:, columns] = attended.astype(bf16)
+
+    for w in wait_ffn:
+        w.wait()
+    for step, (ox, oc) in enumerate(order[:3]):
+        columns = pl.ds(pl.multiple_of(128 * (2 * ox + oc), 128), 128)
+        arrived(abuf.at[:, columns], NUM["o"] + step)
+
+    def norm(hidden):
+        centred = hidden - jnp.mean(hidden, axis=-1, keepdims=True)
+        scale = lax.rsqrt(jnp.mean(centred * centred, axis=-1, keepdims=True) + eps_norm)
+        return centred * scale, scale
+
+    def norm_back(grad, normalized, scale, gain):
+        e = grad * gain
+        return scale * (
+            e - jnp.mean(e, axis=-1, keepdims=True)
+            - normalized * jnp.mean(e * normalized, axis=-1, keepdims=True)
+        )
+
+    def column_sum(values):
+        return jnp.sum(values, axis=0, keepdims=True)
+
+    start_x = xb[pl.ds(own_slot, 2)].reshape(256, 512).astype(f32) + pair_row
+    attn_low = abuf[...]
+    n1, s1 = norm(start_x + (mm(attn_low, wo[...]) + ob[...]))
+    normed = n1 * g1[...] + b1[...]
+    normed_low = normed.astype(bf16)
+    ffn = jnp.zeros((256, 512), f32)
+    for j in range(4):
+        cols = pl.ds(512 * j, 512)
+        pre = mm(normed_low, wup[:, cols]) + ub[:, cols]
+        cdf = 0.5 * (1.0 + lax.erf(pre * 0.7071067811865476))
+        gelu_grad[:, cols] = cdf + pre * (jnp.exp(-0.5 * pre * pre) * 0.3989422804014327)
+        act_low = (pre * cdf).astype(bf16)
+        act[:, cols] = act_low
+        ffn = ffn + mm(act_low, wdn[cols, :])
+    n2, s2 = norm((ffn + db[...]) + normed + start_x)
+    layer_out = n2 * g2[...] + b2[...]
+    lob[...] = layer_out.astype(bf16).reshape(2, 128, 512)
+
+    def give_back(block, out, name, number):
+        for i in (0, 1):
+            to_peer(block.at[i], out.at[z % 2], i, name, None)
+        self_copy = own_block(block.at[z % 2], out.at[z % 2], number)
+        pl.when(jnp.logical_not(crossing))(self_copy.start)
+        return self_copy
+
+    self_lo = give_back(lob, lo_out, "lo", LOCAL - 3)
+
+    for i in (0, 1):
+        @pl.when(2 * c + i != z)
+        def _():
+            arrived(cotb.at[i], NUM["cot"] + i)
+    pl.when(jnp.logical_not(crossing))(self_cot.wait)
+    g = cotb[...].reshape(256, 512).astype(f32)
+    vecb[14:15, :] = column_sum(g * n2)
+    vecb[15:16, :] = column_sum(g)
+    second_grad = norm_back(g, n2, s2, g2[...])
+    ffn_grad = second_grad.astype(bf16)
+    vecb[13:14, :] = column_sum(ffn_grad.astype(f32))
+
+    def axes(lane_number):
+        pair = [(x, x_dev, 1 - x), (y, y_dev, 1 - y)]
+        return pair[::-1] if lane_number % 2 == 0 else pair
+
+    def number(lane_number, step):
+        return NUM["lane"] + 12 * lane_number + step
+
+    def place(lane_number, level, other=False):
+        (a, _, _), (bb, _, _) = axes(lane_number)
+        mine = [c, a, bb, z]
+        base = 0
+        for at, size in zip(range(level + 1), (16, 8, 4, 1)):
+            digit = mine[at]
+            if other and at == level:
+                digit = 1 - digit
+            base = base + digit * size
+        return base
+
+    def fold(lane_number, level, size, received):
+        base = place(lane_number, level)
+
+        def body(t, carry):
+            at = base + t * 4
+            own[lane_number, pl.ds(at, 4)] = (
+                own[lane_number, pl.ds(at, 4)].astype(f32) + received[lane_number, pl.ds(t * 4, 4)].astype(f32)
+            ).astype(bf16)
+            return carry
+
+        lax.fori_loop(0, size // 4, body, 0)
+
+    def lane_start(n):
+        send(own.at[n, pl.ds(place(n, 0, True), 16)], r0.at[n], number(n, 0), number(n, 0), core_dev)
+
+    def lane_step(n, step):
+        (a, a_dev, _), (bb, b_dev, _) = axes(n)
+        if step == 0:
+            arrived(r0.at[n], number(n, 0))
+            fold(n, 0, 16, r0)
+            send(own.at[n, pl.ds(place(n, 1, True), 8)], r1.at[n], number(n, 1), number(n, 1), a_dev)
+        elif step == 1:
+            arrived(r1.at[n], number(n, 1))
+            fold(n, 1, 8, r1)
+            send(own.at[n, pl.ds(place(n, 2, True), 4)], r2.at[n], number(n, 2), number(n, 2), b_dev)
+        elif step == 2:
+            arrived(r2.at[n], number(n, 2))
+            fold(n, 2, 4, r2)
+            for d in (1, 2, 3):
+                send(own.at[n, place(n, 2) + (z + d) % 4], r3.at[n, 3 - d],
+                     number(n, 2 + d), number(n, 6 - d), z_devs[d - 1])
+        elif step == 3:
+            for d in (1, 2, 3):
+                arrived(r3.at[n, d - 1], number(n, 2 + d))
+            mine = place(n, 3)
+            value = own[n, mine].astype(f32)
+            for d in range(3):
+                value = value + r3[n, d].astype(f32)
+            full[n, mine] = value.astype(bf16)
+            for d in (1, 2, 3):
+                send(full.at[n, mine], full.at[n, mine], number(n, 5 + d), number(n, 9 - d), z_devs[d - 1])
+        elif step == 4:
+            base = place(n, 2)
+            for d in (1, 2, 3):
+                arrived(full.at[n, base + (z + d) % 4], number(n, 5 + d))
+            send(full.at[n, pl.ds(base, 4)], full.at[n, pl.ds(base, 4)], number(n, 9), number(n, 9), b_dev)
+        elif step == 5:
+            base = place(n, 1)
+            arrived(full.at[n, pl.ds(place(n, 2, True), 4)], number(n, 9))
+            send(full.at[n, pl.ds(base, 8)], full.at[n, pl.ds(base, 8)], number(n, 10), number(n, 10), a_dev)
+        elif step == 6:
+            base = place(n, 0)
+            arrived(full.at[n, pl.ds(place(n, 1, True), 8)], number(n, 10))
+            send(full.at[n, pl.ds(base, 16)], full.at[n, pl.ds(base, 16)], number(n, 11), number(n, 11), core_dev)
+        else:
+            arrived(full.at[n, pl.ds(place(n, 0, True), 16)], number(n, 11))
+            fetch(full.at[n], gw_out.at[n])
+
+    def lane_fill(n, value):
+        own[n] = value.astype(bf16).reshape(32, 16, 512)
+        lane_start(n)
+
+    waves = [(0, 1), (2, 3), (4, 5), (6, 7), (8,)]
+    progress = {n: 0 for n in range(LANES)}
+
+    def advance(wave):
+        for n in waves[wave]:
+            if progress[n] < 8:
+                lane_step(n, progress[n])
+                progress[n] += 1
+
+    for n in range(4):
+        lane_fill(n, mm_tn(act[:, pl.ds(512 * n, 512)], ffn_grad))
+    advance(0)
+    advance(1)
+
+    normed_grad = second_grad
+    for j in range(4):
+        cols = pl.ds(512 * j, 512)
+        grad = (mm_nt(ffn_grad, wdn[cols, :]) * gelu_grad[:, cols]).astype(bf16)
+        pre_grad[:, cols] = grad
+        vecb[16 + j : 17 + j, :] = column_sum(grad.astype(f32))
+        normed_grad = normed_grad + mm_nt(grad, wup[:, cols])
+    vecb[11:12, :] = column_sum(normed_grad * n1)
+    vecb[12:13, :] = column_sum(normed_grad)
+    first_grad = norm_back(normed_grad, n1, s1, g1[...])
+    attn_grad = first_grad.astype(bf16)
+    dob[...] = mm_nt(attn_grad, wo[...]).astype(bf16)
+    for step, (ox, oc) in enumerate(order[:3]):
+        owner = 2 * ox + oc
+        send(dob.at[:, pl.ds(pl.multiple_of(128 * owner, 128), 128)], dor.at[me],
+             NUM["do"] + step, NUM["do"] + step, dev(ox, y, z, oc))
+    dor[me] = dob[:, pl.ds(pl.multiple_of(128 * me, 128), 128)]
+    vecb[10:11, :] = column_sum(attn_grad.astype(f32))
+    res[...] = first_grad + second_grad
+    for n in range(4):
+        lane_fill(4 + n, mm_tn(normed_low, pre_grad[:, pl.ds(512 * n, 512)]))
+    advance(2)
+    lane_fill(8, mm_tn(attn_low, attn_grad))
+    advance(0)
+    advance(3)
+    advance(4)
+
+    dkt[...] = jnp.zeros((128, 1024), f32)
+    dvt[...] = jnp.zeros((128, 1024), f32)
+    plan = [[1], [0, 2], [1, 3], [0, 2, 4]]
+    for turn, (ox, oc) in enumerate(order[::-1]):
+        owner = 2 * ox + oc
+        if turn > 0:
+            arrived(dor.at[owner], NUM["do"] + 3 - turn)
+        rows = pl.ds(pl.multiple_of(256 * owner, 256), 256)
+        d_out = dor[owner].astype(f32)
+        inverse = inv[rows, :]
+        numer_grad = d_out * inverse
+        product = numer_grad.astype(bf16).astype(f32) * att[rows, :]
+        q_rows = q[rows, :]
+        dq_rows = jnp.zeros((256, 128), f32)
+        for h in range(2):
+            total = -jnp.sum(jnp.where(head_lanes[h], product, 0.0), axis=1, keepdims=True)
+            high = total.astype(bf16).astype(f32)
+            edge = 64 * (1 - h)
+            rest = jnp.where(lane == edge, high, jnp.where(lane == edge + 1, total - high, 0.0))
+            grad_low = jnp.where(head_lanes[h], numer_grad, rest).astype(bf16)
+            prob = probs[h, rows, :]
+            score_grad = (prob.astype(f32) * mm_nt(grad_low, vback[h])).astype(bf16)
+            dq_rows = dq_rows + jnp.where(head_lanes[h], mm(score_grad, k[...]), 0.0)
+            mine = pl.ds(64 * h, 64)
+            q_t = jnp.transpose(q_rows)[64 * h : 64 * h + 64, :]
+            g_t = jnp.transpose(grad_low)[64 * h : 64 * h + 64, :]
+            dkt[mine, :] += mm(q_t, score_grad)
+            dvt[mine, :] += mm(g_t, prob)
+        dqkv[rows, 0:128] = (dq_rows * 0.125).astype(bf16)
+        for wave in plan[turn]:
+            advance(wave)
+
+    for rows_first in range(0, 1024, 256):
+        rows = pl.ds(rows_first, 256)
+        row = lax.broadcasted_iota(jnp.int32, (256, 1), 0)
+        owner = rows_first // 256
+        start = 128 * (4 * (owner % 2) + owner // 2)
+        usable = (start + row + jnp.where(row >= 128, 128, 0)).astype(f32) < row_length
+        dqkv[rows, 128:256] = jnp.transpose(dkt[:, rows]).astype(bf16)
+        dqkv[rows, 256:384] = jnp.where(usable, jnp.transpose(dvt[:, rows]), 0.0).astype(bf16)
+
+    def qnumber(t, step):
+        return NUM["qkv"] + 12 * t + step
+
+    low_all = lowb[...].reshape(1024, 512)
+    for t in range(3):
+        value = mm_tn(low_all, dqkv[:, pl.ds(128 * t, 128)])
+        qown[t] = value.astype(bf16).reshape(8, 64, 128)
+        send(qown.at[t, pl.ds(4 * (1 - y), 4)], qr1.at[t], qnumber(t, 0), qnumber(t, 0), y_dev)
+
+    def dx_block(ox, oc):
+        owner = 2 * ox + oc
+        rows = pl.ds(pl.multiple_of(256 * owner, 256), 256)
+        return mm_nt(dqkv[rows, :], wq[...])
+
+    column_total = jnp.zeros((1, 512), f32)
+    for t, ox in enumerate((1 - x, x)):
+        block = dx_block(ox, 1 - c)
+        column_total = column_total + column_sum(block)
+        dxb[t] = block.astype(bf16)
+        send(dxb.at[t], dxr0.at[t], NUM["dx_core"] + t, NUM["dx_core"] + t, core_dev)
+
+    advance(1)
+    advance(2)
+    block = dx_block(1 - x, c)
+    column_total = column_total + column_sum(block)
+    arrived(dxr0.at[0], NUM["dx_core"])
+    dxb[2] = (block + dxr0[0].astype(f32)).astype(bf16)
+    send(dxb.at[2], dxr1, NUM["dx_x"], NUM["dx_x"], x_dev)
+    block = dx_block(x, c)
+    column_total = column_total + column_sum(block)
+    arrived(dxr0.at[1], NUM["dx_core"] + 1)
+    block = block + dxr0[1].astype(f32) + res[...]
+    column_total = column_total + column_sum(res[...])
+
+    group_iota = lax.broadcasted_iota(jnp.int32, (8, 512), 0).astype(f32)
+    vecb[0:8, :] = jnp.where(group_iota == group_row, column_total, 0.0)
+    vecb[8:10, :] = jnp.zeros((2, 512), f32)
+    mine = pl.ds(pl.multiple_of(128 * me, 128), 128)
+    vecb[8:9, mine] = column_sum(dqkv[:, 0:128].astype(f32))
+    vecb[9:10, mine] = column_sum(dqkv[:, 256:384].astype(f32))
+    vecb[20:24, :] = jnp.zeros((4, 512), f32)
+    for level, device in enumerate((core_dev, x_dev, y_dev)):
+        src = vecb if level == 0 else vecr.at[2 + level]
+        send(src, vecr.at[level], NUM["vec"] + level, NUM["vec"] + level, device)
+        arrived(vecr.at[level], NUM["vec"] + level)
+        value = (vecb[...] if level == 0 else vecr[2 + level]) + vecr[level]
+        if level < 2:
+            vecr[3 + level] = value
+        else:
+            vecz[z] = value
+    for d in (1, 2, 3):
+        send(vecz.at[z], vecz.at[z], NUM["vec"] + 2 + d, NUM["vec"] + 6 - d, z_devs[d - 1])
+
+    for t in range(3):
+        arrived(qr1.at[t], qnumber(t, 0))
+        at = pl.ds(4 * y, 4)
+        qown[t, at] = (qown[t, at].astype(f32) + qr1[t].astype(f32)).astype(bf16)
+        for d in (1, 2, 3):
+            send(qown.at[t, 4 * y + (z + d) % 4], qr3.at[t, 3 - d], qnumber(t, d), qnumber(t, 4 - d), z_devs[d - 1])
+    advance(3)
+    arrived(dxr1, NUM["dx_x"])
+    igb[...] = (block + dxr1[...].astype(f32)).astype(bf16).reshape(2, 128, 512)
+    self_ig = give_back(igb, ig_out, "ig", LOCAL - 4)
+
+    for wave in (0, 1, 4, 2):
+        advance(wave)
+    for t in range(3):
+        for d in (1, 2, 3):
+            arrived(qr3.at[t, d - 1], qnumber(t, d))
+        value = qown[t, 4 * y + z].astype(f32)
+        for d in range(3):
+            value = value + qr3[t, d].astype(f32)
+        shard = qfull.at[t, me, 4 * y + z]
+        shard[...] = value.astype(bf16)
+        for d in (1, 2, 3):
+            send(shard, shard, qnumber(t, 3 + d), qnumber(t, 7 - d), z_devs[d - 1])
+    for wave in (3, 0, 1, 4):
+        advance(wave)
+    for t in range(3):
+        for d in (1, 2, 3):
+            arrived(qfull.at[t, me, 4 * y + (z + d) % 4], qnumber(t, 3 + d))
+        part = qfull.at[t, me, pl.ds(4 * y, 4)]
+        send(part, part, qnumber(t, 7), qnumber(t, 7), y_dev)
+    for wave in (2, 3, 0, 1, 4):
+        advance(wave)
+    for t in range(3):
+        arrived(qfull.at[t, me, pl.ds(4 * (1 - y), 4)], qnumber(t, 7))
+        part = qfull.at[t, me]
+        send(part, part, qnumber(t, 8), qnumber(t, 8), x_dev)
+        send(part, part, qnumber(t, 9), qnumber(t, 9), core_dev)
+    for wave in (2, 3, 4, 2, 3, 4, 4):
+        advance(wave)
+    for t in range(3):
+        theirs = 2 * (1 - x) + c
+        arrived(qfull.at[t, theirs], qnumber(t, 8))
+        part = qfull.at[t, theirs]
+        send(part, part, qnumber(t, 10), qnumber(t, 10), core_dev)
+    for wave in (4, 0, 1, 2, 3, 4):
+        for _ in range(8):
+            advance(wave)
+    for t in range(3):
+        arrived(qfull.at[t, 2 * x + 1 - c], qnumber(t, 9))
+        arrived(qfull.at[t, 2 * (1 - x) + 1 - c], qnumber(t, 10))
+        fetch(qfull.at[t], gqkv_out.at[t])
+
+    for d in (1, 2, 3):
+        arrived(vecz.at[(z + d) % 4], NUM["vec"] + 2 + d)
+    vecb_sum = vecz[0]
+    for t in range(1, 4):
+        vecb_sum = vecb_sum + vecz[t]
+    vecr[0] = vecb_sum
+    fetch(vecr.at[0], vec_out)
+
+    for name, out, self_copy in (("lo", lo_out, self_lo), ("ig", ig_out, self_ig)):
+        for i in (0, 1):
+            @pl.when(2 * c + i != z)
+            def _():
+                arrived(out.at[i], NUM[name] + i)
+        pl.when(jnp.logical_not(crossing))(self_copy.wait)
+    for copy in local_copies[16:]:
+        copy.wait()
+    for copy, when in pending:
+        if when is None:
+            copy.wait_send()
+        else:
+            pl.when(when)(copy.wait_send)
+
+
+def pair_plan(mesh):
+    return dict(mesh.shape) == {"batch": 4, "seq": 8}
+
+
+def fused_local(
+    block_input, cotangent, groups, lengths, pair_table, qkv_weight, q_bias, v_bias, out_weight,
+    out_bias, norm1_gain, norm1_bias, up_weight, up_bias, down_weight, down_bias, norm2_gain, norm2_bias,
+):
+    any_spec, smem = pl.BlockSpec(memory_space=pl.ANY), pl.BlockSpec(memory_space=pltpu.SMEM)
+
+    def row(vector):
+        return vector[None, :]
+
+    operands = (
+        block_input, cotangent, groups, lengths, pair_table, qkv_weight, row(q_bias), row(v_bias),
+        out_weight, row(out_bias), row(norm1_gain), row(norm1_bias), up_weight, row(up_bias),
+        down_weight, row(down_bias), row(norm2_gain), row(norm2_bias),
+    )
+    in_specs = [smem if i in (2, 3) else any_spec for i in range(len(operands))]
+    out_shape = [
+        jax.ShapeDtypeStruct((2, 128, 512), bf16),
+        jax.ShapeDtypeStruct((2, 128, 512), bf16),
+        jax.ShapeDtypeStruct((LANES, 32, 16, 512), bf16),
+        jax.ShapeDtypeStruct((3, 4, 8, 64, 128), bf16),
+        jax.ShapeDtypeStruct((24, 512), f32),
+    ]
+    scratch = [
+        pltpu.VMEM(shape, dtype)
+        for shape, dtype in (
+            ((8, 128, 512), bf16), ((8, 128, 512), bf16), ((2, 128, 512), bf16),
+            ((8, 512), f32), ((8, 512), f32), ((8, 512), f32),
+            ((512, 384), bf16), ((512, 512), bf16), ((512, 2048), bf16), ((2048, 512), bf16),
+            ((1, 512), f32), ((1, 512), f32), ((1, 512), f32), ((1, 512), f32), ((1, 512), f32),
+            ((1, 2048), f32), ((1, 512), f32), ((1, 512), f32), ((1, 512), f32),
+            ((1024, 128), bf16), ((1024, 128), bf16), ((1024, 128), bf16),
+            ((2, 1024, 256), bf16), ((2, 1024, 128), bf16),
+            ((1024, 128), f32), ((1024, 128), f32),
+            ((3, 256, 128), bf16), ((256, 512), bf16),
+            ((256, 2048), f32), ((256, 2048), bf16), ((256, 2048), bf16),
+            ((256, 512), f32), ((2, 128, 512), bf16), ((2, 128, 512), bf16),
+            ((256, 512), bf16), ((4, 256, 128), bf16), ((2, 1024, 1024), bf16),
+            ((8, 128), f32), ((128, 1024), f32), ((128, 1024), f32), ((1024, 384), bf16),
+            ((3, 256, 512), bf16), ((2, 256, 512), bf16), ((256, 512), bf16),
+            ((24, 512), f32), ((5, 24, 512), f32), ((4, 24, 512), f32),
+            ((LANES, 32, 16, 512), bf16), ((LANES, 16, 16, 512), bf16), ((LANES, 8, 16, 512), bf16),
+            ((LANES, 4, 16, 512), bf16), ((LANES, 3, 16, 512), bf16), ((LANES, 32, 16, 512), bf16),
+            ((3, 8, 64, 128), bf16), ((3, 4, 64, 128), bf16), ((3, 3, 64, 128), bf16), ((3, 4, 8, 64, 128), bf16),
+        )
+    ] + [
+        pltpu.SemaphoreType.DMA((NUM.count,)),
+        pltpu.SemaphoreType.DMA((NUM.count,)),
+        pltpu.SemaphoreType.DMA((LOCAL,)),
+    ]
+    layer_out, input_grad, lanes, qkv_parts, vectors = pl.pallas_call(
+        fused,
+        out_shape=out_shape,
+        in_specs=in_specs,
+        out_specs=[any_spec] * len(out_shape),
+        scratch_shapes=scratch,
+        compiler_params=pltpu.CompilerParams(
+            collective_id=0, has_side_effects=True, vmem_limit_bytes=60 * 2**20
+        ),
+    )(*operands)
+    lanes = lanes.reshape(LANES, 512, 512)
+    down_grad = lanes[0:4].reshape(2048, 512).astype(f32)
+    up_grad = jnp.transpose(lanes[4:8], (1, 0, 2)).reshape(512, 2048).astype(f32)
+    out_grad = lanes[8].astype(f32)
+    qkv_grad = jnp.transpose(qkv_parts.reshape(3, 4, 512, 128), (2, 0, 1, 3)).reshape(512, 1536).astype(f32)
+    return (
+        layer_out.astype(f32), input_grad.astype(f32), vectors[0:8], qkv_grad, vectors[8], vectors[9],
+        out_grad, vectors[10], vectors[11], vectors[12], up_grad, vectors[16:20].reshape(2048),
+        down_grad, vectors[13], vectors[14], vectors[15],
+    )
+
+
 def solution(mesh):
     in_specs = (
         P("batch", "seq", None),
@@ -391,4 +1051,4 @@
         P(),
         P(),
     )
-    return jax.shard_map(local, mesh=mesh, in_specs=in_specs, out_specs=out_specs, check_vma=False)
+    return jax.shard_map(fused_local if pair_plan(mesh) else local, mesh=mesh, in_specs=in_specs, out_specs=out_specs, check_vma=False)

time: 528 us -> 145 us (0.27)
  waiting for transfers between devices: 309 us -> 0 us
  Pallas kernels: 0 us -> 121 us
  matrix products: 73.8 us -> 0 us
  blocking collectives: 67.3 us -> 0 us
  local copies, waits for them, and re-layouts: 49.4 us -> 13.4 us
  between operations: 14.4 us -> 0.71 us
    psum x1 -> x0, waiting for transfers between devices: 186 us -> none  [local(): lax.psum((pair_table_grad, qkv_weight_grad, q_bias_grad, v_bias_grad, out...]
    all_gather x4 -> x0, waiting for transfers between devices: 122 us -> none  [the longest x1 46.1 us: local(): lax.all_gather(key_rows, 'seq', axis=1, tiled=True)]
    pallas_call x0 -> x1, Pallas kernels: none -> 121 us  [fused_local(): pl.pallas_call(fused, out_shape=out_shape, in_specs=in_specs, out_specs=[...]
    dot_general x32 -> x0, matrix products: 73.8 us -> none  [the longest x2 15.9 us: key_one_block(): jnp.einsum('rihd,rjhd->rhij', grad_block, value_wide, precision=highest,...]
    psum x1 -> x0, blocking collectives: 42.7 us -> none  [local(): lax.psum((pair_table_grad, qkv_weight_grad, q_bias_grad, v_bias_grad, out...]
    all_gather x1 -> x0, blocking collectives: 24.6 us -> none  [local(): lax.all_gather(total_grad, 'seq', axis=1, tiled=True)]
    unnamed x95 -> x4, local copies, waits for them, and re-layouts: 19.8 us -> 0.61 us
    all_gather x3 -> x0, local copies, waits for them, and re-layouts: 13.2 us -> none  [the longest x1 5.34 us: local(): lax.all_gather(grad_rows, 'seq', axis=1, tiled=True)]
  transfers between devices with their start and end apart: 5 -> 0, of which waited for: 4 -> 0; matrix products, arithmetic and copies ran while one was open for 15% -> 0% of each run, Pallas kernels for 0% -> 0%
where the time goes in v1:
time: 145 us
  Pallas kernels  121 us (83%)
  local copies, waits for them, and re-layouts  13.4 us (9%)
  other arithmetic  9.88 us (7%)
    pallas_call x1, Pallas kernels, fused_local(): pl.pallas_call(fused, out_shape=out_shape, in_specs=in_specs, out_specs=[...  121 us
    convert_element_type x2, local copies, waits for them, and re-layouts, fused_local(): jnp.transpose(qkv_parts.reshape(3, 4, 512, 128), (2, 0, 1, 3))  4.46 us

profile of v1, /device:TPU:1, one launch (start us, length us, event | category | flops | bytes accessed | tf_op | source)
XLA Modules:
  0.0 144.9 jit_solution(5479154419947807700)
XLA Ops:
  0.7 120.9 %shard_map.297 = (bf16[2,128,512]{2,1,0:T(8,128)(2,1)}, bf16[2,128,512]{2,1,0:T(8,128)(2,1)}, bf16[9,32,16,512]{3,2,1,0:T(8,128)(2,1)}, bf16[3,4,8,64,128]{4,3,2,1,0:T(8,128)(2,1)}, f32[24,512]{1,0:T(8,128)}) custom-call(bf16[2,128,512]{2,1,0:T(8,128)(2,1)} %x_in.1, bf16[2,128,512]{2,1,0:T(8,128)(2,1)} %cot_in.1, s32[2]{0:T(128)} %groups.1, s32[2]{0:T(128)} %lengths.1, ...), custom_call_target="tpu_custom_call" | custom-call | tf_op jit(solution)/shard_map/pallas_call | solution.py:993
  121.6 1.8 %convert_element_type.42 = f32[2,128,512]{2,1,0:T(8,128)} convert(bf16[2,128,512]{2,1,0:T(8,128)(2,1)} %get-tuple-element.21) | non-fusion elementwise | flops 131072 | bytes 786432 | tf_op jit(solution)/shard_map/convert_element_type | solution.py:1009
  123.4 1.8 %convert_element_type.43 = f32[2,128,512]{2,1,0:T(8,128)} convert(bf16[2,128,512]{2,1,0:T(8,128)(2,1)} %get-tuple-element.22) | non-fusion elementwise | flops 131072 | bytes 786432 | tf_op jit(solution)/shard_map/convert_element_type | solution.py:1009
  125.2 1.3 slice.42
  126.5 1.7 %convert_bitcast_fusion.1 = f32[512,3,4,128]{3,0,2,1:T(8,128)S(1)} fusion(bf16[3,4,8,64,128]{4,3,2,1,0:T(8,128)(2,1)} %get-tuple-element.24), kind=kLoop, calls=%fused_computation.1 | loop fusion | flops 786432 | bytes 4718592 | tf_op jit(solution)/shard_map/convert_element_type | solution.py:1007
  128.2 2.0 %copy.34 = f32[512,3,4,128]{3,2,1,0:T(4,128)S(1)} copy(f32[512,3,4,128]{3,0,2,1:T(8,128)S(1)} %convert_bitcast_fusion.1) | data formatting | bytes 6291456 | tf_op jit(solution)/shard_map/convert_element_type | solution.py:1007
  130.2 0.0 copy-start
  130.2 2.4 %reshape.58 = f32[512,1536]{1,0:T(8,128)} reshape(f32[512,3,4,128]{3,2,1,0:T(4,128)S(1)} %copy.34) | data formatting | bytes 6291456 | tf_op jit(solution)/shard_map/convert_element_type | solution.py:1007
  132.7 0.0 copy-done
  132.7 0.6 fusion.1
  133.3 1.1 slice.45
  134.4 1.1 bitcast_convert_fusion.1
  135.5 2.7 %fusion = (bf16[4,32,16,512]{3,2,1,0:T(8,128)(2,1)S(1)}, bf16[4,32,16,512]{3,2,1,0:T(8,128)(2,1)S(1)}) fusion(bf16[9,32,16,512]{3,2,1,0:T(8,128)(2,1)} %get-tuple-element.25), kind=kLoop, calls=%fused_computation.5 | loop fusion | bytes 8388608 | tf_op jit(solution)/shard_map/slice | solution.py:1004
  138.2 0.7 convert_bitcast_fusion
  138.9 2.7 %copy.36 = f32[4,64,8,512]{3,2,0,1:T(8,128)} copy(f32[4,64,8,512]{3,2,1,0:T(8,128)S(1)} %convert_bitcast_fusion) | data formatting | bytes 8388608 | tf_op jit(solution)/shard_map/convert_element_type | solution.py:1005
  141.6 0.6 copy.37
  142.2 2.7 %bitcast_convert_fusion = f32[2048,512]{1,0:T(8,128)} fusion(bf16[4,32,16,512]{3,2,1,0:T(8,128)(2,1)S(1)} %get-tuple-element.26), kind=kLoop, calls=%fused_computation.2 | loop fusion | flops 1048576 | bytes 6291456 | tf_op jit(solution)/shard_map/convert_element_type | solution.py:1004
  (1 shorter events, 0.0 us)
Async XLA Ops:
  130.2 2.4 %copy-start = (f32[24,512]{1,0:T(8,128)S(1)}, f32[24,512]{1,0:T(8,128)}, u32[]{:S(2)}) copy-start(f32[24,512]{1,0:T(8,128)} %get-tuple-element.23) | copy-start | bytes 147460

commit v2 on v0

--- a/solution.py
+++ b/solution.py
@@ -1,6 +1,10 @@
+import functools
+
 import jax
 import jax.numpy as jnp
 from jax import lax
+from jax.experimental import pallas as pl
+from jax.experimental.pallas import tpu as pltpu
 from jax.sharding import PartitionSpec as P
 
 HEADS = 8
@@ -352,6 +356,749 @@
     )
 
 
+MESH = pl.DeviceIdType.MESH
+f32, bf16 = jnp.float32, jnp.bfloat16
+LANES = 9
+
+
+def mm(a, b):
+    return jnp.dot(a, b, preferred_element_type=f32)
+
+
+def mm_nt(a, b):
+    return lax.dot_general(a, b, (((1,), (1,)), ((), ())), preferred_element_type=f32)
+
+
+def mm_tn(a, b):
+    return lax.dot_general(a, b, (((0,), (0,)), ((), ())), preferred_element_type=f32)
+
+
+class Numbers:
+    def __init__(self):
+        self.count = 0
+        self.first = {}
+
+    def take(self, name, size=1):
+        self.first[name] = self.count
+        self.count += size
+
+    def __getitem__(self, name):
+        return self.first[name]
+
+
+def semaphore_numbers():
+    numbers = Numbers()
+    for name, size in (
+        ("x", 4), ("cot", 2), ("lo", 2), ("ig", 2), ("cot_x", 2),
+        ("xn", 4), ("core_own", 4), ("core_far", 4), ("meta", 1),
+        ("o_core", 2), ("o_x", 2), ("o_diag", 2), ("do", 1), ("dx_core", 2), ("dx_x", 1), ("vec", 6),
+        ("lane", LANES * 12), ("qkv", 3 * 12),
+    ):
+        numbers.take(name, size)
+    return numbers
+
+
+NUM = semaphore_numbers()
+LOCAL = 16 + 2
+
+SCATTER = ('zy', 'yz', 'yz', 'zy', 'yz', 'yz', 'yz', 'yz', 'yz')
+GATHER = ('zxy', 'zxy', 'zyx', 'zyx', 'zyx', 'zxy', 'zyx', 'zxy', 'zyx')
+QGATHER = ('zyx', 'yxz', 'xzy')
+FILL, LANE, FFN, NORM, ATTN, SPLIT, WEIGHT, PART, INPUT, RETURN, SMALL = range(11)
+ORDER = (
+    (FILL, 3, 0), (FILL, 1, 0), (FILL, 0, 0), (FILL, 2, 0), (FFN, 0, 0), (LANE, 3, 0), (LANE, 1, 0),
+    (FFN, 1, 0), (LANE, 0, 0), (LANE, 2, 0), (FFN, 2, 0), (FFN, 3, 0), (FILL, 7, 0), (FILL, 5, 0),
+    (FILL, 6, 0), (NORM, 0, 0), (LANE, 7, 0), (LANE, 1, 1), (FILL, 8, 0), (LANE, 6, 0), (LANE, 5, 0),
+    (FILL, 4, 0), (ATTN, 0, 0), (LANE, 4, 0), (LANE, 8, 0), (LANE, 3, 1), (LANE, 2, 1), (ATTN, 1, 0),
+    (LANE, 7, 1), (ATTN, 2, 0), (LANE, 0, 1), (LANE, 6, 1), (ATTN, 3, 0), (LANE, 1, 2), (LANE, 5, 1),
+    (SPLIT, 0, 0), (WEIGHT, 2, 0), (WEIGHT, 0, 0), (WEIGHT, 1, 0), (LANE, 2, 2), (LANE, 4, 1), (INPUT, 0, 0),
+    (INPUT, 1, 0), (LANE, 8, 1), (LANE, 7, 2), (LANE, 3, 2), (LANE, 0, 2), (LANE, 6, 2), (INPUT, 2, 0),
+    (INPUT, 3, 0), (SMALL, 0, 0), (PART, 2, 0), (LANE, 1, 3), (SMALL, 1, 0), (PART, 0, 0), (LANE, 5, 2),
+    (PART, 1, 0), (LANE, 2, 3), (LANE, 4, 2), (LANE, 8, 2), (LANE, 2, 4), (RETURN, 0, 0), (LANE, 7, 3),
+    (LANE, 1, 4), (LANE, 3, 3), (SMALL, 2, 0), (LANE, 0, 3), (LANE, 6, 3), (LANE, 2, 5), (PART, 2, 1),
+    (LANE, 1, 5), (LANE, 2, 6), (LANE, 7, 4), (PART, 0, 1), (LANE, 1, 6), (LANE, 3, 4), (LANE, 0, 4),
+    (PART, 2, 2), (LANE, 5, 3), (SMALL, 3, 0), (PART, 1, 1), (LANE, 6, 4), (LANE, 4, 3), (LANE, 3, 5),
+    (LANE, 8, 3), (LANE, 7, 5), (LANE, 3, 6), (LANE, 5, 4), (LANE, 7, 6), (LANE, 0, 5), (PART, 1, 2),
+    (LANE, 6, 5), (LANE, 0, 6), (LANE, 4, 4), (LANE, 6, 6), (LANE, 8, 4), (PART, 1, 3), (PART, 0, 2),
+    (LANE, 5, 5), (LANE, 4, 5), (PART, 2, 3), (LANE, 5, 6), (PART, 0, 3), (SMALL, 4, 0), (LANE, 4, 6),
+    (LANE, 8, 5), (LANE, 8, 6), (PART, 2, 4), (PART, 0, 4), (PART, 2, 5), (PART, 1, 4), (PART, 0, 5),
+    (PART, 1, 5),
+)
+
+
+def fused(
+    x_in, cot_in, groups, lengths, table_in, wqkv_in, qb_in, vb_in, wo_in, ob_in, g1_in, b1_in,
+    wup_in, ub_in, wdn_in, db_in, g2_in, b2_in,
+    lo_out, ig_out, full, qfull, vec_out,
+    xb, lowb, cotb, table, meta, meta_far, wq, wo, wup, wdn, qb, vb, ob, g1, b1, ub, db, g2, b2,
+    q, k, vaug, vback, att, inv, obuf, abuf, gelu_grad, act, pre_grad, res, lob, igb, n1, n2, s2b, attn_grad,
+    normed_low, ffn_grad, second, normed_grad, dob, dor, probs, dkt, dvt, dqkv, dxb, dxr0, dxr1, dxo,
+    vecb, vecr, vecz,
+    own, r0, r1, r3, qown, qr1, qr3,
+    ssem, rsem, lsem,
+):
+    b_index, s_index = lax.axis_index("batch"), lax.axis_index("seq")
+    x, z = s_index % 2, s_index // 2
+    y, c = b_index // 2, b_index % 2
+    me = 2 * x + c
+
+    def dev(x, y, z, c):
+        return (2 * y + c, 2 * z + x)
+
+    core_dev = dev(x, y, z, 1 - c)
+    x_dev = dev(1 - x, y, z, c)
+    y_dev = dev(x, 1 - y, z, c)
+    diag_dev = dev(1 - x, y, z, 1 - c)
+    z_devs = [dev(x, y, (z + d) % 4, c) for d in (1, 2, 3)]
+    crossing = c != z // 2
+
+    pending = []
+
+    def send(src, dst, s_number, r_number, device, when=None):
+        copy = pltpu.make_async_remote_copy(
+            src_ref=src, dst_ref=dst, send_sem=ssem.at[s_number], recv_sem=rsem.at[r_number],
+            device_id=device, device_id_type=MESH,
+        )
+        if when is None:
+            copy.start()
+        else:
+            pl.when(when)(copy.start)
+        pending.append((copy, when))
+
+    def arrived(dst, number):
+        pltpu.make_async_remote_copy(
+            src_ref=dst, dst_ref=dst, send_sem=ssem.at[number], recv_sem=rsem.at[number],
+            device_id=core_dev, device_id_type=MESH,
+        ).wait_recv()
+
+    local_copies = []
+
+    def fetch(src, dst):
+        copy = pltpu.make_async_copy(src, dst, lsem.at[len(local_copies)])
+        copy.start()
+        local_copies.append(copy)
+        return copy
+
+    def land(copies):
+        for copy in copies:
+            copy.wait()
+            local_copies[local_copies.index(copy)] = None
+
+    wait_qkv = [fetch(table_in, table), fetch(qb_in, qb), fetch(vb_in, vb)]
+    for t in range(3):
+        columns = pl.ds(pl.multiple_of(512 * t + 128 * me, 128), 128)
+        wait_qkv.append(fetch(wqkv_in.at[:, columns], wq.at[:, pl.ds(128 * t, 128)]))
+    wait_ffn = [
+        fetch(a, b)
+        for a, b in ((wo_in, wo), (ob_in, ob), (g1_in, g1), (b1_in, b1), (wup_in, wup), (ub_in, ub),
+                     (wdn_in, wdn), (db_in, db), (g2_in, g2), (b2_in, b2))
+    ]
+
+    barrier = pltpu.get_barrier_semaphore()
+    near = [core_dev, x_dev, y_dev, diag_dev] + z_devs
+    for device in near:
+        pl.semaphore_signal(barrier, inc=1, device_id=device, device_id_type=MESH)
+
+    @pl.when(crossing)
+    def _():
+        for i in range(2):
+            pl.semaphore_signal(
+                barrier, inc=1, device_id=dev(x, y, 2 * c + i, z // 2), device_id_type=MESH
+            )
+        pl.semaphore_wait(barrier, len(near) + 2)
+
+    @pl.when(jnp.logical_not(crossing))
+    def _():
+        pl.semaphore_wait(barrier, len(near))
+
+    def half(ref, h):
+        return ref.at[pl.ds(64 * h, 64)]
+
+    def peer(i):
+        return dev(x, y, 2 * c + i, z // 2)
+
+    first = jnp.where(crossing, 1 - c, z % 2)
+    in_turn = [(i, h) for i in (first, 1 - first) for h in (0, 1)]
+    for i, h in in_turn:
+        send(half(x_in.at[i], h), half(xb.at[x, z], h), NUM["x"] + 2 * i + h, NUM["x"] + 2 * (z % 2) + h,
+             peer(i), when=2 * c + i != z)
+    self_x = pltpu.make_async_copy(x_in.at[z % 2], xb.at[x, z], lsem.at[LOCAL - 1])
+    self_cot = pltpu.make_async_copy(cot_in.at[z % 2], cotb.at[x, z % 2], lsem.at[LOCAL - 2])
+
+    @pl.when(jnp.logical_not(crossing))
+    def _():
+        self_x.start()
+        self_cot.start()
+        self_x.wait()
+
+
+    land(wait_qkv)
+    slot = z % 2
+    group, length = groups[slot], lengths[slot]
+    meta[0:1, :] = table[pl.ds(group, 1), :]
+    meta[1:2, :] = jnp.full((1, 512), length.astype(f32))
+    meta[2:3, :] = jnp.full((1, 512), group.astype(f32))
+    meta[3:8, :] = jnp.zeros((5, 512), f32)
+    send(meta, meta_far, NUM["meta"], NUM["meta"], core_dev)
+
+    for i, h in in_turn:
+        block = half(xb.at[x, 2 * c + i], h)
+
+        @pl.when(2 * c + i != z)
+        def _():
+            arrived(block, NUM["x"] + 2 * i + h)
+
+        number = NUM["xn"] + 2 * i + h
+        send(block, block, number, number, x_dev)
+        number = NUM["core_own"] + 2 * i + h
+        send(block, block, number, number, core_dev)
+
+    arrived(meta_far, NUM["meta"])
+    facts = jnp.where(crossing, meta_far[...], meta[...])
+    pair_row, length_row, group_row = facts[0:1, :], facts[1:2, :], facts[2:3, :]
+    row_length = length_row[:, 0:128]
+
+    lane = lax.broadcasted_iota(jnp.int32, (1, 128), 1)
+    head_lanes = [lane < 64, lane >= 64]
+    row = lax.broadcasted_iota(jnp.int32, (256, 1), 0)
+
+    def rows_of(xx, cc):
+        return pl.ds(pl.multiple_of(512 * xx + 256 * cc, 256), 256)
+
+    def usable_rows(xx, cc):
+        place = 128 * (4 * cc + xx) + row + jnp.where(row >= 128, 128, 0)
+        return place.astype(f32) < row_length
+
+    def project(xx, cc):
+        low = (xb[xx, pl.ds(2 * cc, 2)].reshape(256, 512).astype(f32) + pair_row).astype(bf16)
+        rows = rows_of(xx, cc)
+        lowb[rows, :] = low
+        y_all = mm(low, wq[...])
+        usable = usable_rows(xx, cc)
+        q_bias = qb[:, pl.ds(pl.multiple_of(128 * me, 128), 128)]
+        v_bias = vb[:, pl.ds(pl.multiple_of(128 * me, 128), 128)]
+        q[rows, :] = (y_all[:, 0:128] + q_bias).astype(bf16) * jnp.asarray(0.125, bf16)
+        k[rows, :] = jnp.where(usable, y_all[:, 128:256], 0.0).astype(bf16)
+        value = jnp.where(usable, y_all[:, 256:384] + v_bias, 0.0)
+        one = jnp.where(usable, 1.0, 0.0)
+        for h in range(2):
+            vaug[h, rows, 0:128] = jnp.where(head_lanes[h], value, 0.0).astype(bf16)
+            vaug[h, rows, 128:256] = jnp.where(head_lanes[h], one, 0.0).astype(bf16)
+            edge = 64 * (1 - h)
+            extra = jnp.where((lane == edge) | (lane == edge + 1), one, 0.0)
+            vback[h, rows, :] = jnp.where(head_lanes[h], value, extra).astype(bf16)
+
+    project(x, c)
+    for i, h in in_turn:
+        arrived(half(xb.at[x, 2 * (1 - c) + i], h), NUM["core_own"] + 2 * i + h)
+    project(x, 1 - c)
+    for i, h in in_turn:
+        block = half(xb.at[1 - x, 2 * c + i], h)
+        arrived(block, NUM["xn"] + 2 * i + h)
+        number = NUM["core_far"] + 2 * i + h
+        send(block, block, number, number, core_dev)
+    for i in (0, 1):
+        send(cot_in.at[i], cotb.at[x, z % 2], NUM["cot"] + i, NUM["cot"] + z % 2, peer(i), when=2 * c + i != z)
+    project(1 - x, c)
+    for i, h in in_turn:
+        arrived(half(xb.at[1 - x, 2 * (1 - c) + i], h), NUM["core_far"] + 2 * i + h)
+    project(1 - x, 1 - c)
+
+    mine = pl.ds(pl.multiple_of(128 * me, 128), 128)
+    for turn, (xx, cc) in enumerate(((0, 1 - c), (1, 1 - c), (0, c), (1, c))):
+        rows = rows_of(xx, cc)
+        q_rows = q[rows, :]
+        total = jnp.zeros((256, 256), f32)
+        for h in range(2):
+            scores = mm_nt(jnp.where(head_lanes[h], q_rows, 0), k[...])
+            prob = jnp.exp(scores).astype(bf16)
+            probs[h, rows, :] = prob
+            total = total + mm(prob, vaug[h])
+        inverse = 1.0 / total[:, 128:256]
+        attended = total[:, 0:128] * inverse
+        att[rows, :] = attended
+        inv[rows, :] = inverse
+        obuf[turn] = attended.astype(bf16)
+        there = abuf.at[pl.ds(256 * xx, 256), mine]
+        if turn < 2:
+            send(obuf.at[turn], there, NUM["o_diag"] + xx, NUM["o_diag"] + xx, diag_dev)
+            send(obuf.at[turn], there, NUM["o_core"] + xx, NUM["o_core"] + xx, core_dev)
+        else:
+            send(obuf.at[turn], there, NUM["o_x"] + xx, NUM["o_x"] + xx, x_dev)
+            abuf[256 * xx : 256 * xx + 256, mine] = attended.astype(bf16)
+
+    for i in (0, 1):
+        @pl.when(2 * c + i != z)
+        def _():
+            arrived(cotb.at[x, i], NUM["cot"] + i)
+    pl.when(jnp.logical_not(crossing))(self_cot.wait)
+    for i in (0, 1):
+        send(cotb.at[x, i], cotb.at[x, i], NUM["cot_x"] + i, NUM["cot_x"] + i, x_dev)
+
+    def norm(hidden):
+        centred = hidden - jnp.mean(hidden, axis=-1, keepdims=True)
+        scale = lax.rsqrt(jnp.mean(centred * centred, axis=-1, keepdims=True) + eps_norm)
+        return centred * scale, scale
+
+    def norm_back(grad, normalized, scale, gain):
+        e = grad * gain
+        return scale * (
+            e - jnp.mean(e, axis=-1, keepdims=True)
+            - normalized * jnp.mean(e * normalized, axis=-1, keepdims=True)
+        )
+
+    def column_sum(values):
+        return jnp.sum(values, axis=0, keepdims=True)
+
+    once = jnp.where(x == 0, 1.0, 0.0)
+    land(wait_ffn)
+    s1_parts = []
+    for xx in (0, 1):
+        there = pl.ds(256 * xx, 256)
+
+        def columns_of(hx, hc):
+            return pl.ds(pl.multiple_of(128 * (2 * hx + hc), 128), 128)
+
+        arrived(abuf.at[there, columns_of(x, 1 - c)], NUM["o_core"] + xx)
+        arrived(abuf.at[there, columns_of(1 - x, 1 - c)], NUM["o_diag"] + xx)
+        arrived(abuf.at[there, columns_of(1 - x, c)], NUM["o_x"] + xx)
+        start_x = xb[xx, pl.ds(2 * c, 2)].reshape(256, 512).astype(f32) + pair_row
+        normalized, s1 = norm(start_x + (mm(abuf[there, :], wo[...]) + ob[...]))
+        s1_parts.append(s1)
+        n1[there, :] = normalized
+        normed = normalized * g1[...] + b1[...]
+        low = normed.astype(bf16)
+        normed_low[there, :] = low
+        ffn = jnp.zeros((256, 512), f32)
+        for j in range(4):
+            cols = pl.ds(512 * j, 512)
+            pre = mm(low, wup[:, cols]) + ub[:, cols]
+            cdf = 0.5 * (1.0 + lax.erf(pre * 0.7071067811865476))
+            gelu_grad[there, cols] = cdf + pre * (jnp.exp(-0.5 * pre * pre) * 0.3989422804014327)
+            act_low = (pre * cdf).astype(bf16)
+            act[there, cols] = act_low
+            ffn = ffn + mm(act_low, wdn[cols, :])
+        normalized, s2 = norm((ffn + db[...]) + normed + start_x)
+        n2[there, :] = normalized
+        s2b[there, :] = jnp.broadcast_to(s2, (256, 128))
+    own_half = pl.ds(pl.multiple_of(256 * x, 256), 256)
+    lob[...] = (n2[own_half, :] * g2[...] + b2[...]).astype(bf16).reshape(2, 128, 512)
+
+    def give_back(block, out, name):
+        for i in (0, 1):
+            send(block.at[i], out.at[z % 2], NUM[name] + i, NUM[name] + z % 2, peer(i), when=2 * c + i != z)
+
+        @pl.when(jnp.logical_not(crossing))
+        def _():
+            out[z % 2] = block[z % 2]
+
+    give_back(lob, lo_out, "lo")
+    for i in (0, 1):
+        arrived(cotb.at[1 - x, i], NUM["cot_x"] + i)
+    for xx in (0, 1):
+        there = pl.ds(256 * xx, 256)
+        g = cotb[xx].reshape(256, 512).astype(f32)
+        normalized = n2[there, :]
+        gain_part, bias_part = column_sum(g * normalized), column_sum(g)
+        grad = norm_back(g, normalized, s2b[there, 0:1], g2[...])
+        second[there, :] = grad
+        low = grad.astype(bf16)
+        ffn_grad[there, :] = low
+        down_part = column_sum(low.astype(f32))
+        for at, part in ((14, gain_part), (15, bias_part), (13, down_part)):
+            vecb[at : at + 1, :] = part * once if xx == 0 else vecb[at : at + 1, :] + part * once
+
+    def number(n, step):
+        return NUM["lane"] + 12 * n + step
+
+    def fold(target, received):
+        target[...] = (target[...].astype(f32) + received[...].astype(f32)).astype(bf16)
+
+    def scatter(n, axis, last):
+        if axis == "y":
+            part = own.at[n, c, 1 - y, z] if last else own.at[n, c, 1 - y]
+            send(part, r1.at[n, 0] if last else r1.at[n], number(n, 1), number(n, 1), y_dev)
+        else:
+            for d in (1, 2, 3):
+                part = own.at[n, c, y, (z + d) % 4] if last else own.at[n, c, :, (z + d) % 4]
+                send(part, r3.at[n, 3 - d, 0] if last else r3.at[n, 3 - d],
+                     number(n, 1 + d), number(n, 5 - d), z_devs[d - 1])
+
+    def collect(n, axis, last):
+        if axis == "y":
+            arrived(r1.at[n, 0] if last else r1.at[n], number(n, 1))
+            parts = [r1.at[n, 0] if last else r1.at[n]]
+        else:
+            for d in (1, 2, 3):
+                arrived(r3.at[n, d - 1, 0] if last else r3.at[n, d - 1], number(n, 1 + d))
+            parts = [r3.at[n, d, 0] if last else r3.at[n, d] for d in range(3)]
+        if last:
+            target = own.at[n, c, y, z]
+        else:
+            target = own.at[n, c, y] if axis == "y" else own.at[n, c, :, z]
+        value = target[...].astype(f32)
+        for part in parts:
+            value = value + part[...].astype(f32)
+        if last:
+            target = full.at[n, x, c, y, z]
+        target[...] = value.astype(bf16)
+
+    def region(buffer, n, done, **other):
+        place = dict(x=x, y=y, z=z) | other
+        at = {axis: slice(None) if axis in done else place[axis] for axis in "xyz"}
+        return buffer.at[n, at["x"], c, at["y"], at["z"]]
+
+    def spread(buffer, n, number_of, order, stage):
+        part = region(buffer, n, order[:stage])
+        if stage == 3:
+            send(part, part, number_of(10), number_of(10), core_dev)
+        elif order[stage] == "z":
+            for d in (1, 2, 3):
+                send(part, part, number_of(4 + d), number_of(8 - d), z_devs[d - 1])
+        else:
+            at, device = {"x": (9, x_dev), "y": (8, y_dev)}[order[stage]]
+            send(part, part, number_of(at), number_of(at), device)
+
+    def gather(buffer, n, number_of, order, stage):
+        if stage == 3:
+            arrived(buffer.at[n, :, 1 - c], number_of(10))
+        elif order[stage] == "z":
+            for d in (1, 2, 3):
+                arrived(region(buffer, n, order[:stage], z=(z + d) % 4), number_of(4 + d))
+        elif order[stage] == "x":
+            arrived(region(buffer, n, order[:stage], x=1 - x), number_of(9))
+        else:
+            arrived(region(buffer, n, order[:stage], y=1 - y), number_of(8))
+
+    def lane_step(n, step):
+        scatter_order, order = SCATTER[n], GATHER[n]
+        number_of = functools.partial(number, n)
+        if step == 0:
+            arrived(r0.at[n], number(n, 0))
+            fold(own.at[n, c], r0.at[n])
+            scatter(n, scatter_order[0], False)
+        elif step == 1:
+            collect(n, scatter_order[0], False)
+            scatter(n, scatter_order[1], True)
+        elif step == 2:
+            collect(n, scatter_order[1], True)
+            spread(full, n, number_of, order, 0)
+        else:
+            gather(full, n, number_of, order, step - 3)
+            if step < 6:
+                spread(full, n, number_of, order, step - 2)
+
+    own_columns = pl.ds(pl.multiple_of(256 * x, 256), 256)
+
+    def lane_fill(n):
+        if n < 4:
+            value = mm_tn(act[:, pl.ds(pl.multiple_of(512 * n + 256 * x, 256), 256)], ffn_grad[...])
+        elif n < 8:
+            value = mm_tn(normed_low[:, own_columns], pre_grad[:, pl.ds(512 * (n - 4), 512)])
+        else:
+            value = mm_tn(abuf[:, own_columns], attn_grad[...])
+        own[n] = value.astype(bf16).reshape(2, 2, 4, 16, 512)
+        send(own.at[n, 1 - c], r0.at[n], number(n, 0), number(n, 0), core_dev)
+
+    def ffn_back(j):
+        cols = pl.ds(512 * j, 512)
+        for xx in (0, 1):
+            there = pl.ds(256 * xx, 256)
+            grad = (mm_nt(ffn_grad[there, :], wdn[cols, :]) * gelu_grad[there, cols]).astype(bf16)
+            pre_grad[there, cols] = grad
+            part = column_sum(grad.astype(f32)) * once
+            vecb[16 + j : 17 + j, :] = part if xx == 0 else vecb[16 + j : 17 + j, :] + part
+            term = mm_nt(grad, wup[:, cols])
+            normed_grad[there, :] = (second if j == 0 else normed_grad)[there, :] + term
+
+    def first_back():
+        for xx in (0, 1):
+            there = pl.ds(256 * xx, 256)
+            grad, normalized = normed_grad[there, :], n1[there, :]
+            first_grad = norm_back(grad, normalized, s1_parts[xx], g1[...])
+            low = first_grad.astype(bf16)
+            attn_grad[there, :] = low
+            for at, part in ((11, column_sum(grad * normalized)), (12, column_sum(grad)),
+                             (10, column_sum(low.astype(f32)))):
+                vecb[at : at + 1, :] = part * once if xx == 0 else vecb[at : at + 1, :] + part * once
+            second[there, :] = second[there, :] + first_grad
+        res[...] = second[own_half, :]
+        low = attn_grad[...]
+
+        def heads(cc):
+            return pl.ds(pl.multiple_of(128 * (2 * x + cc), 128), 128)
+
+        dob[...] = mm_nt(low, wo[heads(1 - c), :]).astype(bf16)
+        send(dob, dor.at[c], NUM["do"], NUM["do"], core_dev)
+        dor[c] = mm_nt(low, wo[heads(c), :]).astype(bf16)
+
+    turns = ((0, c), (1, c), (0, 1 - c), (1, 1 - c))
+
+    def attention_back(turn):
+        xx, cc = turns[turn]
+        if turn == 2:
+            arrived(dor.at[cc], NUM["do"])
+        rows = rows_of(xx, cc)
+        d_out = dor[cc, 256 * xx : 256 * xx + 256, :].astype(f32)
+        numer_grad = d_out * inv[rows, :]
+        product = numer_grad.astype(bf16).astype(f32) * att[rows, :]
+        q_rows = q[rows, :]
+        dq_rows = jnp.zeros((256, 128), f32)
+        for h in range(2):
+            total = -jnp.sum(jnp.where(head_lanes[h], product, 0.0), axis=1, keepdims=True)
+            high = total.astype(bf16).astype(f32)
+            edge = 64 * (1 - h)
+            rest = jnp.where(lane == edge, high, jnp.where(lane == edge + 1, total - high, 0.0))
+            grad_low = jnp.where(head_lanes[h], numer_grad, rest).astype(bf16)
+            prob = probs[h, rows, :]
+            score_grad = (prob.astype(f32) * mm_nt(grad_low, vback[h])).astype(bf16)
+            dq_rows = dq_rows + jnp.where(head_lanes[h], mm(score_grad, k[...]), 0.0)
+            part = slice(64 * h, 64 * h + 64)
+            dk_part = mm(jnp.transpose(q_rows)[part, :], score_grad)
+            dv_part = mm(jnp.transpose(grad_low)[part, :], prob)
+            dkt[part, :] = dk_part if turn == 0 else dkt[part, :] + dk_part
+            dvt[part, :] = dv_part if turn == 0 else dvt[part, :] + dv_part
+        dqkv[rows, 0:128] = (dq_rows * 0.125).astype(bf16)
+
+    def projection_grads():
+        for xx in (0, 1):
+            for cc in (0, 1):
+                rows = pl.ds(512 * xx + 256 * cc, 256)
+                dqkv[rows, 128:256] = jnp.transpose(dkt[:, rows]).astype(bf16)
+                dqkv[rows, 256:384] = jnp.where(usable_rows(xx, cc), jnp.transpose(dvt[:, rows]), 0.0).astype(bf16)
+
+    def qnumber(t, step):
+        return NUM["qkv"] + 12 * t + step
+
+    def projection_weights(t):
+        value = mm_tn(lowb[...], dqkv[:, 128 * t : 128 * t + 128])
+        qown[t] = value.astype(bf16).reshape(2, 4, 64, 128)
+        send(qown.at[t, 1 - y], qr1.at[t], qnumber(t, 0), qnumber(t, 0), y_dev)
+
+    def projection_step(t, step):
+        number_of, order = functools.partial(qnumber, t), QGATHER[t]
+        if step == 0:
+            arrived(qr1.at[t], qnumber(t, 0))
+            fold(qown.at[t, y], qr1.at[t])
+            for d in (1, 2, 3):
+                send(qown.at[t, y, (z + d) % 4], qr3.at[t, 3 - d], qnumber(t, d), qnumber(t, 4 - d), z_devs[d - 1])
+        elif step == 1:
+            for d in (1, 2, 3):
+                arrived(qr3.at[t, d - 1], qnumber(t, d))
+            value = qown[t, y, z].astype(f32)
+            for d in range(3):
+                value = value + qr3[t, d].astype(f32)
+            qfull[t, x, c, y, z] = value.astype(bf16)
+            spread(qfull, t, number_of, order, 0)
+        else:
+            gather(qfull, t, number_of, order, step - 2)
+            if step < 5:
+                spread(qfull, t, number_of, order, step - 1)
+
+    def input_back(step):
+        xx, cc = ((1 - x, 1 - c), (x, 1 - c), (1 - x, c), (x, c))[step]
+        block = mm_nt(dqkv[rows_of(xx, cc), :], wq[...])
+        vecb[20:21, :] = column_sum(block) if step == 0 else vecb[20:21, :] + column_sum(block)
+        if step < 2:
+            dxb[step] = block.astype(bf16)
+            send(dxb.at[step], dxr0.at[step], NUM["dx_core"] + step, NUM["dx_core"] + step, core_dev)
+        elif step == 2:
+            arrived(dxr0.at[0], NUM["dx_core"])
+            dxb[2] = (block + dxr0[0].astype(f32)).astype(bf16)
+            send(dxb.at[2], dxr1, NUM["dx_x"], NUM["dx_x"], x_dev)
+        else:
+            arrived(dxr0.at[1], NUM["dx_core"] + 1)
+            dxo[...] = block + dxr0[1].astype(f32) + res[...]
+
+    def input_out():
+        arrived(dxr1, NUM["dx_x"])
+        igb[...] = (dxo[...] + dxr1[...].astype(f32)).astype(bf16).reshape(2, 128, 512)
+        give_back(igb, ig_out, "ig")
+
+    def vectors(step):
+        if step == 0:
+            group_iota = lax.broadcasted_iota(jnp.int32, (8, 512), 0).astype(f32)
+            column_total = vecb[20:21, :] + column_sum(res[...])
+            vecb[0:8, :] = jnp.where(group_iota == group_row, column_total, 0.0)
+            vecb[8:10, :] = jnp.zeros((2, 512), f32)
+            vecb[8:9, mine] = column_sum(dqkv[:, 0:128].astype(f32))
+            vecb[9:10, mine] = column_sum(dqkv[:, 256:384].astype(f32))
+            vecb[20:24, :] = jnp.zeros((4, 512), f32)
+            send(vecb, vecr.at[0], NUM["vec"], NUM["vec"], core_dev)
+        elif step < 4:
+            level = step - 1
+            arrived(vecr.at[level], NUM["vec"] + level)
+            value = (vecb[...] if level == 0 else vecr[2 + level]) + vecr[level]
+            if level < 2:
+                vecr[3 + level] = value
+                send(vecr.at[3 + level], vecr.at[level + 1], NUM["vec"] + level + 1, NUM["vec"] + level + 1,
+                     (x_dev, y_dev)[level])
+            else:
+                vecz[z] = value
+                for d in (1, 2, 3):
+                    send(vecz.at[z], vecz.at[z], NUM["vec"] + 2 + d, NUM["vec"] + 6 - d, z_devs[d - 1])
+        else:
+            for d in (1, 2, 3):
+                arrived(vecz.at[(z + d) % 4], NUM["vec"] + 2 + d)
+            value = vecz[0]
+            for t in range(1, 4):
+                value = value + vecz[t]
+            vec_out[...] = value
+
+    tasks = {(NORM, 0, 0): first_back, (SPLIT, 0, 0): projection_grads, (RETURN, 0, 0): input_out}
+    for kind, task, counts in (
+        (FILL, lane_fill, (LANES,)), (FFN, ffn_back, (4,)), (ATTN, attention_back, (4,)), (WEIGHT, projection_weights, (3,)),
+        (INPUT, input_back, (4,)), (SMALL, vectors, (5,)), (LANE, lane_step, (LANES, 7)), (PART, projection_step, (3, 6)),
+    ):
+        for at in range(counts[0]):
+            for step in range(counts[-1]) if len(counts) == 2 else (0,):
+                tasks[kind, at, step] = functools.partial(task, *(at, step)[: len(counts)])
+    for entry in ORDER:
+        tasks.pop(entry)()
+    assert not tasks
+
+    for name, out in (("lo", lo_out), ("ig", ig_out)):
+        for i in (0, 1):
+            @pl.when(2 * c + i != z)
+            def _():
+                arrived(out.at[i], NUM[name] + i)
+    land([copy for copy in local_copies if copy is not None])
+    for copy, when in pending:
+        if when is None:
+            copy.wait_send()
+        else:
+            pl.when(when)(copy.wait_send)
+
+
+VECTOR_ROWS = (8, 9, 10, 11, 12, 13, 14, 15)
+
+
+def finish(lo, ig, full, qfull, vec, *refs):
+    lo_out, ig_out, down_out, up_out, out_out, qkv_out, pair_out = refs[:7]
+    vector_outs, up_bias_out = refs[7:15], refs[15]
+    lo_wide, ig_wide, full_wide, qkv_wide, rows, up_bias, sems = *refs[16:20], refs[20:28], refs[28], refs[29]
+    writes = []
+
+    def write(src, dst):
+        made = pltpu.make_async_copy(src, dst, sems.at[len(writes)])
+        made.start()
+        writes.append(made)
+
+    for n in range(LANES):
+        for half in range(2):
+            at = pl.ds(256 * half, 256)
+            full_wide[n, at, :] = full[n, half].reshape(256, 512).astype(f32)
+            if n < 4:
+                write(full_wide.at[n, at], down_out.at[pl.ds(512 * n + 256 * half, 256)])
+            elif n < 8:
+                write(full_wide.at[n, at], up_out.at[at, pl.ds(512 * (n - 4), 512)])
+            else:
+                write(full_wide.at[n, at], out_out.at[at])
+    for t in range(3):
+        for h in range(4):
+            columns = pl.ds(512 * t + 128 * h, 128)
+            qkv_wide[:, columns] = qfull[t, h // 2, h % 2].reshape(512, 128).astype(f32)
+        columns = pl.ds(512 * t, 512)
+        write(qkv_wide.at[:, columns], qkv_out.at[:, columns])
+    for block, wide, out in ((lo, lo_wide, lo_out), (ig, ig_wide, ig_out)):
+        wide[...] = block[...].astype(f32)
+        write(wide, out)
+    write(vec.at[pl.ds(0, 8)], pair_out)
+    for at, row, out in zip(VECTOR_ROWS, rows, vector_outs):
+        row[...] = vec[at : at + 1, :]
+        write(row, out)
+    for j in range(4):
+        up_bias[:, 512 * j : 512 * j + 512] = vec[16 + j : 17 + j, :]
+    write(up_bias, up_bias_out)
+    for made in writes:
+        made.wait()
+
+
+def pair_plan(mesh):
+    return dict(mesh.shape) == {"batch": 4, "seq": 8}
+
+
+def fused_local(
+    block_input, cotangent, groups, lengths, pair_table, qkv_weight, q_bias, v_bias, out_weight,
+    out_bias, norm1_gain, norm1_bias, up_weight, up_bias, down_weight, down_bias, norm2_gain, norm2_bias,
+):
+    any_spec, smem = pl.BlockSpec(memory_space=pl.ANY), pl.BlockSpec(memory_space=pltpu.SMEM)
+
+    def row(vector):
+        return vector[None, :]
+
+    operands = (
+        block_input, cotangent, groups, lengths, pair_table, qkv_weight, row(q_bias), row(v_bias),
+        out_weight, row(out_bias), row(norm1_gain), row(norm1_bias), up_weight, row(up_bias),
+        down_weight, row(down_bias), row(norm2_gain), row(norm2_bias),
+    )
+    in_specs = [smem if i in (2, 3) else any_spec for i in range(len(operands))]
+    vmem = pl.BlockSpec(memory_space=pltpu.VMEM)
+    out_shape = [
+        pltpu.VMEM(shape, dtype)
+        for shape, dtype in (
+            ((2, 128, 512), bf16), ((2, 128, 512), bf16), ((LANES, 2, 2, 2, 4, 16, 512), bf16),
+            ((3, 2, 2, 2, 4, 64, 128), bf16), ((24, 512), f32),
+        )
+    ]
+    scratch = [
+        pltpu.VMEM(shape, dtype)
+        for shape, dtype in (
+            ((2, 4, 128, 512), bf16), ((1024, 512), bf16), ((2, 2, 128, 512), bf16),
+            ((8, 512), f32), ((8, 512), f32), ((8, 512), f32),
+            ((512, 384), bf16), ((512, 512), bf16), ((512, 2048), bf16), ((2048, 512), bf16),
+            ((1, 512), f32), ((1, 512), f32), ((1, 512), f32), ((1, 512), f32), ((1, 512), f32),
+            ((1, 2048), f32), ((1, 512), f32), ((1, 512), f32), ((1, 512), f32),
+            ((1024, 128), bf16), ((1024, 128), bf16),
+            ((2, 1024, 256), bf16), ((2, 1024, 128), bf16),
+            ((1024, 128), f32), ((1024, 128), f32),
+            ((4, 256, 128), bf16), ((512, 512), bf16),
+            ((512, 2048), f32), ((512, 2048), bf16), ((512, 2048), bf16),
+            ((256, 512), f32), ((2, 128, 512), bf16), ((2, 128, 512), bf16),
+            ((512, 512), f32), ((512, 512), f32), ((512, 128), f32), ((512, 512), bf16),
+            ((512, 512), bf16), ((512, 512), bf16), ((512, 512), f32), ((512, 512), f32),
+            ((512, 128), bf16), ((2, 512, 128), bf16), ((2, 1024, 1024), bf16),
+            ((128, 1024), f32), ((128, 1024), f32), ((1024, 384), bf16),
+            ((3, 256, 512), bf16), ((2, 256, 512), bf16), ((256, 512), bf16), ((256, 512), f32),
+            ((24, 512), f32), ((5, 24, 512), f32), ((4, 24, 512), f32),
+            ((LANES, 2, 2, 4, 16, 512), bf16), ((LANES, 2, 4, 16, 512), bf16), ((LANES, 4, 16, 512), bf16),
+            ((LANES, 3, 2, 16, 512), bf16),
+            ((3, 2, 4, 64, 128), bf16), ((3, 4, 64, 128), bf16), ((3, 3, 64, 128), bf16),
+        )
+    ] + [
+        pltpu.SemaphoreType.DMA((NUM.count,)),
+        pltpu.SemaphoreType.DMA((NUM.count,)),
+        pltpu.SemaphoreType.DMA((LOCAL,)),
+    ]
+    results = pl.pallas_call(
+        fused,
+        out_shape=out_shape,
+        in_specs=in_specs,
+        out_specs=[vmem] * len(out_shape),
+        scratch_shapes=scratch,
+        compiler_params=pltpu.CompilerParams(
+            collective_id=0, has_side_effects=True, vmem_limit_bytes=54 * 2**20
+        ),
+    )(*operands)
+    shapes = [(2, 128, 512)] * 2 + [(2048, 512), (512, 2048), (512, 512), (512, 1536), (8, 512)]
+    shapes += [(1, 512)] * 8 + [(1, 2048)]
+    scratch_sizes = [(2, 128, 512)] * 2 + [(LANES, 512, 512), (512, 1536)] + [(1, 512)] * 8 + [(1, 2048)]
+    results = pl.pallas_call(
+        finish,
+        out_shape=[jax.ShapeDtypeStruct(shape, f32) for shape in shapes],
+        in_specs=[vmem] * 5,
+        out_specs=[any_spec] * len(shapes),
+        scratch_shapes=[pltpu.VMEM(shape, f32) for shape in scratch_sizes] + [pltpu.SemaphoreType.DMA((40,))],
+        compiler_params=pltpu.CompilerParams(vmem_limit_bytes=40 * 2**20),
+    )(*results)
+    layer_out, input_grad, down_grad, up_grad, out_grad, qkv_grad, pair_grad = results[:7]
+    q_grad, v_grad, ob_grad, g1_grad, b1_grad, db_grad, g2_grad, b2_grad = [r.reshape(512) for r in results[7:15]]
+    return (
+        layer_out, input_grad, pair_grad, qkv_grad, q_grad, v_grad,
+        out_grad, ob_grad, g1_grad, b1_grad, up_grad, results[15].reshape(2048), down_grad, db_grad, g2_grad, b2_grad,
+    )
+
+
 def solution(mesh):
     in_specs = (
         P("batch", "seq", None),
@@ -391,4 +1138,4 @@
         P(),
         P(),
     )
-    return jax.shard_map(local, mesh=mesh, in_specs=in_specs, out_specs=out_specs, check_vma=False)
+    return jax.shard_map(fused_local if pair_plan(mesh) else local, mesh=mesh, in_specs=in_specs, out_specs=out_specs, check_vma=False)

time: 528 us -> 102 us (0.19)
  waiting for transfers between devices: 309 us -> 0 us
  Pallas kernels: 0 us -> 101 us
  matrix products: 73.8 us -> 0 us
  blocking collectives: 67.3 us -> 0 us
  local copies, waits for them, and re-layouts: 49.4 us -> 0 us
  between operations: 14.4 us -> 0.84 us
  other arithmetic: 10.9 us -> 0 us
    psum x1 -> x0, waiting for transfers between devices: 186 us -> none  [local(): lax.psum((pair_table_grad, qkv_weight_grad, q_bias_grad, v_bias_grad, out...]
    all_gather x4 -> x0, waiting for transfers between devices: 122 us -> none  [the longest x1 46.1 us: local(): lax.all_gather(key_rows, 'seq', axis=1, tiled=True)]
    pallas_call x0 -> x2, Pallas kernels: none -> 101 us  [the longest x1 96 us: fused_local(): pl.pallas_call(fused, out_shape=out_shape, in_specs=in_specs, out_specs=[...]
    dot_general x32 -> x0, matrix products: 73.8 us -> none  [the longest x2 15.9 us: key_one_block(): jnp.einsum('rihd,rjhd->rhij', grad_block, value_wide, precision=highest,...]
    psum x1 -> x0, blocking collectives: 42.7 us -> none  [local(): lax.psum((pair_table_grad, qkv_weight_grad, q_bias_grad, v_bias_grad, out...]
    all_gather x1 -> x0, blocking collectives: 24.6 us -> none  [local(): lax.all_gather(total_grad, 'seq', axis=1, tiled=True)]
    unnamed x95 -> x0, local copies, waits for them, and re-layouts: 19.8 us -> none
    all_gather x3 -> x0, local copies, waits for them, and re-layouts: 13.2 us -> none  [the longest x1 5.34 us: local(): lax.all_gather(grad_rows, 'seq', axis=1, tiled=True)]
  transfers between devices with their start and end apart: 5 -> 0, of which waited for: 4 -> 0; matrix products, arithmetic and copies ran while one was open for 15% -> 0% of each run, Pallas kernels for 0% -> 0%
where the time goes in v2:
time: 102 us
  Pallas kernels  101 us (99%)
    pallas_call x1, Pallas kernels, fused_local(): pl.pallas_call(fused, out_shape=out_shape, in_specs=in_specs, out_specs=[...  96 us
    pallas_call x1, Pallas kernels, fused_local(): pl.pallas_call(finish, out_shape=[jax.ShapeDtypeStruct(shape, f32) for sh...  5.27 us

profile of v2, /device:TPU:1, one launch (start us, length us, event | category | flops | bytes accessed | tf_op | source)
XLA Modules:
  0.0 102.1 jit_solution(12755988461595942750)
XLA Ops:
  0.7 96.0 %shard_map.297 = (bf16[2,128,512]{2,1,0:T(8,128)(2,1)S(1)}, bf16[2,128,512]{2,1,0:T(8,128)(2,1)S(1)}, bf16[9,2,2,2,4,16,512]{6,5,4,3,2,1,0:T(8,128)(2,1)S(1)}, b...) custom-call(bf16[2,128,512]{2,1,0:T(8,128)(2,1)} %x_in.1, bf16[2,128,512]{2,1,0:T(8,128)(2,1)} %cot_in.1, ...), custom_call_target="tpu_custom_call" | custom-call | tf_op jit(solution)/shard_map/pallas_call | solution.py:1073
  96.7 5.3 %shard_map.298 = (f32[2,128,512]{2,1,0:T(8,128)}, f32[2,128,512]{2,1,0:T(8,128)}, f32[2048,512]{1,0:T(8,128)}, f32[512,2048]{1,0:T(8,128)}, f32[512,512]{1,0:T(8...) custom-call(bf16[2,128,512]{2,1,0:T(8,128)(2,1)S(1)} %get-tuple-elem, ...), custom_call_target="tpu_custom_call" | custom-call | tf_op jit(solution)/shard_map/pallas_call | solution.py:1086

commit v3 on v2

--- a/solution.py
+++ b/solution.py
@@ -391,7 +391,7 @@
     for name, size in (
         ("x", 4), ("cot", 2), ("lo", 2), ("ig", 2), ("cot_x", 2),
         ("xn", 4), ("core_own", 4), ("core_far", 4), ("meta", 1),
-        ("o_core", 2), ("o_x", 2), ("o_diag", 2), ("do", 1), ("dx_core", 2), ("dx_x", 1), ("vec", 6),
+        ("do", 1), ("dx_core", 2), ("dx_x", 1), ("vec", 6),
         ("lane", LANES * 12), ("qkv", 3 * 12),
     ):
         numbers.take(name, size)
@@ -399,30 +399,33 @@
 
 
 NUM = semaphore_numbers()
-LOCAL = 16 + 2
-
-SCATTER = ('zy', 'yz', 'yz', 'zy', 'yz', 'yz', 'yz', 'yz', 'yz')
-GATHER = ('zxy', 'zxy', 'zyx', 'zyx', 'zyx', 'zxy', 'zyx', 'zxy', 'zyx')
-QGATHER = ('zyx', 'yxz', 'xzy')
-FILL, LANE, FFN, NORM, ATTN, SPLIT, WEIGHT, PART, INPUT, RETURN, SMALL = range(11)
+LOCAL = 17 + 2
+
+SCATTER = ('yz', 'yz', 'yz', 'yz', 'yw', 'yw', 'yw', 'yw', 'yw')
+GATHER = ('wxy', 'wxy', 'zxy', 'wyx', 'wxy', 'wxy', 'zxy', 'wyx', 'zyx')
+QSCATTER = ('yw', 'yw', 'yw')
+QGATHER = ('yzx', 'yxz', 'zxy')
+FILL, LANE, FFN, NORM, ATTN, SPLIT, WEIGHT, PART, INPUT, RETURN, SMALL, PROBS = range(12)
 ORDER = (
-    (FILL, 3, 0), (FILL, 1, 0), (FILL, 0, 0), (FILL, 2, 0), (FFN, 0, 0), (LANE, 3, 0), (LANE, 1, 0),
-    (FFN, 1, 0), (LANE, 0, 0), (LANE, 2, 0), (FFN, 2, 0), (FFN, 3, 0), (FILL, 7, 0), (FILL, 5, 0),
-    (FILL, 6, 0), (NORM, 0, 0), (LANE, 7, 0), (LANE, 1, 1), (FILL, 8, 0), (LANE, 6, 0), (LANE, 5, 0),
-    (FILL, 4, 0), (ATTN, 0, 0), (LANE, 4, 0), (LANE, 8, 0), (LANE, 3, 1), (LANE, 2, 1), (ATTN, 1, 0),
-    (LANE, 7, 1), (ATTN, 2, 0), (LANE, 0, 1), (LANE, 6, 1), (ATTN, 3, 0), (LANE, 1, 2), (LANE, 5, 1),
-    (SPLIT, 0, 0), (WEIGHT, 2, 0), (WEIGHT, 0, 0), (WEIGHT, 1, 0), (LANE, 2, 2), (LANE, 4, 1), (INPUT, 0, 0),
-    (INPUT, 1, 0), (LANE, 8, 1), (LANE, 7, 2), (LANE, 3, 2), (LANE, 0, 2), (LANE, 6, 2), (INPUT, 2, 0),
-    (INPUT, 3, 0), (SMALL, 0, 0), (PART, 2, 0), (LANE, 1, 3), (SMALL, 1, 0), (PART, 0, 0), (LANE, 5, 2),
-    (PART, 1, 0), (LANE, 2, 3), (LANE, 4, 2), (LANE, 8, 2), (LANE, 2, 4), (RETURN, 0, 0), (LANE, 7, 3),
-    (LANE, 1, 4), (LANE, 3, 3), (SMALL, 2, 0), (LANE, 0, 3), (LANE, 6, 3), (LANE, 2, 5), (PART, 2, 1),
-    (LANE, 1, 5), (LANE, 2, 6), (LANE, 7, 4), (PART, 0, 1), (LANE, 1, 6), (LANE, 3, 4), (LANE, 0, 4),
-    (PART, 2, 2), (LANE, 5, 3), (SMALL, 3, 0), (PART, 1, 1), (LANE, 6, 4), (LANE, 4, 3), (LANE, 3, 5),
-    (LANE, 8, 3), (LANE, 7, 5), (LANE, 3, 6), (LANE, 5, 4), (LANE, 7, 6), (LANE, 0, 5), (PART, 1, 2),
-    (LANE, 6, 5), (LANE, 0, 6), (LANE, 4, 4), (LANE, 6, 6), (LANE, 8, 4), (PART, 1, 3), (PART, 0, 2),
-    (LANE, 5, 5), (LANE, 4, 5), (PART, 2, 3), (LANE, 5, 6), (PART, 0, 3), (SMALL, 4, 0), (LANE, 4, 6),
-    (LANE, 8, 5), (LANE, 8, 6), (PART, 2, 4), (PART, 0, 4), (PART, 2, 5), (PART, 1, 4), (PART, 0, 5),
-    (PART, 1, 5),
+    (FILL, 1, 0), (FFN, 0, 0), (FILL, 2, 0), (FILL, 3, 0), (FILL, 0, 0), (LANE, 1, 0), (FFN, 1, 0),
+    (FFN, 2, 0), (LANE, 2, 0), (FFN, 3, 0), (LANE, 3, 0), (LANE, 0, 0), (FILL, 6, 0), (FILL, 4, 0),
+    (FILL, 7, 0), (NORM, 0, 0), (LANE, 1, 1), (LANE, 4, 0), (ATTN, 0, 0), (LANE, 2, 1), (ATTN, 1, 0),
+    (LANE, 3, 1), (LANE, 7, 0), (LANE, 6, 0), (FILL, 8, 0), (FILL, 5, 0), (PROBS, 1, 0), (LANE, 1, 2),
+    (LANE, 0, 1), (LANE, 8, 0), (LANE, 5, 0), (PROBS, 0, 0), (LANE, 4, 1), (LANE, 2, 2), (ATTN, 2, 0),
+    (LANE, 7, 1), (ATTN, 3, 0), (LANE, 1, 3), (LANE, 3, 2), (SPLIT, 0, 0), (WEIGHT, 2, 0), (LANE, 8, 1),
+    (LANE, 0, 2), (WEIGHT, 1, 0), (WEIGHT, 0, 0), (LANE, 4, 2), (LANE, 6, 1), (INPUT, 0, 0), (INPUT, 1, 0),
+    (LANE, 5, 1), (LANE, 2, 3), (LANE, 7, 2), (LANE, 1, 4), (INPUT, 2, 0), (INPUT, 3, 0), (LANE, 3, 3),
+    (SMALL, 0, 0), (PART, 2, 0), (LANE, 8, 2), (LANE, 0, 3), (SMALL, 1, 0), (PART, 1, 0), (LANE, 4, 3),
+    (LANE, 6, 2), (LANE, 2, 4), (LANE, 5, 2), (PART, 0, 0), (LANE, 7, 3), (LANE, 3, 4), (LANE, 1, 5),
+    (PART, 2, 1), (LANE, 8, 3), (LANE, 0, 4), (PART, 1, 1), (LANE, 4, 4), (LANE, 6, 3), (LANE, 2, 5),
+    (LANE, 5, 3), (PART, 0, 1), (LANE, 7, 4), (LANE, 2, 6), (LANE, 3, 5), (PART, 2, 2), (RETURN, 0, 0),
+    (SMALL, 2, 0), (LANE, 8, 4), (PART, 1, 2), (LANE, 1, 6), (LANE, 4, 5), (LANE, 0, 5), (LANE, 1, 7),
+    (LANE, 6, 4), (SMALL, 3, 0), (LANE, 5, 4), (PART, 0, 2), (LANE, 3, 6), (LANE, 7, 5), (LANE, 8, 5),
+    (PART, 1, 3), (LANE, 4, 6), (LANE, 3, 7), (PART, 2, 3), (LANE, 6, 5), (LANE, 0, 6), (PART, 0, 3),
+    (LANE, 0, 7), (LANE, 7, 6), (LANE, 8, 6), (PART, 1, 4), (LANE, 8, 7), (PART, 2, 4), (LANE, 4, 7),
+    (SMALL, 4, 0), (LANE, 5, 5), (LANE, 4, 8), (LANE, 7, 7), (LANE, 6, 6), (PART, 0, 4), (LANE, 7, 8),
+    (LANE, 5, 6), (LANE, 6, 7), (PART, 2, 5), (PART, 2, 6), (PART, 0, 5), (PART, 1, 5), (LANE, 5, 7),
+    (PART, 0, 6), (PART, 1, 6), (LANE, 5, 8), (SMALL, 5, 0),
 )
 
 
@@ -430,10 +433,10 @@
     x_in, cot_in, groups, lengths, table_in, wqkv_in, qb_in, vb_in, wo_in, ob_in, g1_in, b1_in,
     wup_in, ub_in, wdn_in, db_in, g2_in, b2_in,
     lo_out, ig_out, full, qfull, vec_out,
-    xb, lowb, cotb, table, meta, meta_far, wq, wo, wup, wdn, qb, vb, ob, g1, b1, ub, db, g2, b2,
-    q, k, vaug, vback, att, inv, obuf, abuf, gelu_grad, act, pre_grad, res, lob, igb, n1, n2, s2b, attn_grad,
+    xb, lowb, cotb, table, meta, meta_far, wqkv, wq, wo, wup, wdn, qb, vb, ob, g1, b1, ub, db, g2, b2,
+    qt, q, k, vaug, vback, att, inv, sums, abuf, gelu_grad, act, pre_grad, res, lob, igb, n1, n2, s2b, attn_grad,
     normed_low, ffn_grad, second, normed_grad, dob, dor, probs, dkt, dvt, dqkv, dxb, dxr0, dxr1, dxo,
-    vecb, vecr, vecz,
+    vecb, vecr,
     own, r0, r1, r3, qown, qr1, qr3,
     ssem, rsem, lsem,
 ):
@@ -448,8 +451,9 @@
     core_dev = dev(x, y, z, 1 - c)
     x_dev = dev(1 - x, y, z, c)
     y_dev = dev(x, 1 - y, z, c)
-    diag_dev = dev(1 - x, y, z, 1 - c)
     z_devs = [dev(x, y, (z + d) % 4, c) for d in (1, 2, 3)]
+    z_near = z + 1 - 2 * (z % 2)
+    near_dev, mirror_dev = dev(x, y, z_near, c), dev(x, y, 3 - z, c)
     crossing = c != z // 2
 
     pending = []
@@ -488,6 +492,7 @@
     for t in range(3):
         columns = pl.ds(pl.multiple_of(512 * t + 128 * me, 128), 128)
         wait_qkv.append(fetch(wqkv_in.at[:, columns], wq.at[:, pl.ds(128 * t, 128)]))
+    wait_qkv.append(fetch(wqkv_in, wqkv))
     wait_ffn = [
         fetch(a, b)
         for a, b in ((wo_in, wo), (ob_in, ob), (g1_in, g1), (b1_in, b1), (wup_in, wup), (ub_in, ub),
@@ -495,7 +500,7 @@
     ]
 
     barrier = pltpu.get_barrier_semaphore()
-    near = [core_dev, x_dev, y_dev, diag_dev] + z_devs
+    near = [core_dev, x_dev, y_dev] + z_devs
     for device in near:
         pl.semaphore_signal(barrier, inc=1, device_id=device, device_id_type=MESH)
 
@@ -522,6 +527,9 @@
     for i, h in in_turn:
         send(half(x_in.at[i], h), half(xb.at[x, z], h), NUM["x"] + 2 * i + h, NUM["x"] + 2 * (z % 2) + h,
              peer(i), when=2 * c + i != z)
+    def send_cot():
+        for i in (first, 1 - first):
+            send(cot_in.at[i], cotb.at[x, z % 2], NUM["cot"] + i, NUM["cot"] + z % 2, peer(i), when=2 * c + i != z)
     self_x = pltpu.make_async_copy(x_in.at[z % 2], xb.at[x, z], lsem.at[LOCAL - 1])
     self_cot = pltpu.make_async_copy(cot_in.at[z % 2], cotb.at[x, z % 2], lsem.at[LOCAL - 2])
 
@@ -553,10 +561,11 @@
         number = NUM["core_own"] + 2 * i + h
         send(block, block, number, number, core_dev)
 
+    send_cot()
     arrived(meta_far, NUM["meta"])
     facts = jnp.where(crossing, meta_far[...], meta[...])
     pair_row, length_row, group_row = facts[0:1, :], facts[1:2, :], facts[2:3, :]
-    row_length = length_row[:, 0:128]
+    row_length = length_row[:, 0:1]
 
     lane = lax.broadcasted_iota(jnp.int32, (1, 128), 1)
     head_lanes = [lane < 64, lane >= 64]
@@ -569,71 +578,106 @@
         place = 128 * (4 * cc + xx) + row + jnp.where(row >= 128, 128, 0)
         return place.astype(f32) < row_length
 
-    def project(xx, cc):
+    mine = pl.ds(pl.multiple_of(128 * me, 128), 128)
+    all_lanes = lax.broadcasted_iota(jnp.int32, (1, 256), 1)
+    first_head = all_lanes % 128 < 64
+
+    def project(xx, cc, ours):
         low = (xb[xx, pl.ds(2 * cc, 2)].reshape(256, 512).astype(f32) + pair_row).astype(bf16)
         rows = rows_of(xx, cc)
         lowb[rows, :] = low
-        y_all = mm(low, wq[...])
         usable = usable_rows(xx, cc)
-        q_bias = qb[:, pl.ds(pl.multiple_of(128 * me, 128), 128)]
-        v_bias = vb[:, pl.ds(pl.multiple_of(128 * me, 128), 128)]
-        q[rows, :] = (y_all[:, 0:128] + q_bias).astype(bf16) * jnp.asarray(0.125, bf16)
-        k[rows, :] = jnp.where(usable, y_all[:, 128:256], 0.0).astype(bf16)
-        value = jnp.where(usable, y_all[:, 256:384] + v_bias, 0.0)
-        one = jnp.where(usable, 1.0, 0.0)
+        eighth = jnp.asarray(0.125, bf16)
+        if ours:
+            there = pl.ds(pl.multiple_of(256 * xx, 256), 256)
+            qt[there, :] = (mm(low, wqkv[:, 0:512]) + qb[...]).astype(bf16) * eighth
+            q[rows, :] = qt[there, mine]
+        else:
+            q[rows, :] = (mm(low, wq[:, 0:128]) + qb[:, mine]).astype(bf16) * eighth
+        k[rows, :] = jnp.where(usable, mm(low, wqkv[:, 512:1024]), 0.0).astype(bf16)
+        value = jnp.where(usable, mm(low, wqkv[:, 1024:1536]) + vb[...], 0.0).astype(bf16)
+        one = jnp.broadcast_to(jnp.where(usable, 1.0, 0.0), (256, 128))
+        for pair in range(4):
+            vaug[pair, rows, 0:128] = value[:, 128 * pair : 128 * pair + 128]
+            vaug[pair, rows, 128:256] = one.astype(bf16)
+        own_value = vaug[me, rows, 0:128].astype(f32)
         for h in range(2):
-            vaug[h, rows, 0:128] = jnp.where(head_lanes[h], value, 0.0).astype(bf16)
-            vaug[h, rows, 128:256] = jnp.where(head_lanes[h], one, 0.0).astype(bf16)
             edge = 64 * (1 - h)
             extra = jnp.where((lane == edge) | (lane == edge + 1), one, 0.0)
-            vback[h, rows, :] = jnp.where(head_lanes[h], value, extra).astype(bf16)
-
-    project(x, c)
+            vback[h, rows, :] = jnp.where(head_lanes[h], own_value, extra).astype(bf16)
+
+    def attend(q_rows, pair, h, keys, probs_rows):
+        columns = pl.ds(pl.multiple_of(128 * pair, 128), 128)
+        prob = jnp.exp(mm_nt(jnp.where(head_lanes[h], q_rows, 0), k[keys, columns])).astype(bf16)
+        if probs_rows is not None:
+            probs[h, probs_rows, keys] = prob
+        return mm(prob, vaug[pair, keys, :])
+
+    def attended_of(sums, rows):
+        both = jnp.where(first_head, sums[0], sums[1])
+        inverse = 1.0 / both[:, 128:256]
+        attended = both[:, 0:128] * inverse
+        if rows is not None:
+            att[rows, :] = attended
+            inv[rows, :] = inverse
+        return attended.astype(bf16)
+
+    every = pl.ds(0, 1024)
+    early = pl.ds(pl.multiple_of(512 * x, 512), 512)
+    late = pl.ds(pl.multiple_of(512 * (1 - x), 512), 512)
+    pairs = [(me + d) % 4 for d in range(4)]
+    own_rows, far_rows = rows_of(x, c), rows_of(1 - x, c)
+    own_half = pl.ds(pl.multiple_of(256 * x, 256), 256)
+    far_half = pl.ds(pl.multiple_of(256 * (1 - x), 256), 256)
+
+    def pair_columns(pair):
+        return pl.ds(pl.multiple_of(128 * pair, 128), 128)
+
+    def early_part(d, h):
+        sums[d, h] = attend(qt[own_half, pair_columns(pairs[d])], pairs[d], h, early, own_rows if d == 0 else None)
+
+    project(x, c, True)
     for i, h in in_turn:
         arrived(half(xb.at[x, 2 * (1 - c) + i], h), NUM["core_own"] + 2 * i + h)
-    project(x, 1 - c)
-    for i, h in in_turn:
+    project(x, 1 - c, False)
+    for at, (i, h) in enumerate(in_turn):
+        early_part(at, 0)
+        early_part(at, 1)
         block = half(xb.at[1 - x, 2 * c + i], h)
         arrived(block, NUM["xn"] + 2 * i + h)
         number = NUM["core_far"] + 2 * i + h
         send(block, block, number, number, core_dev)
-    for i in (0, 1):
-        send(cot_in.at[i], cotb.at[x, z % 2], NUM["cot"] + i, NUM["cot"] + z % 2, peer(i), when=2 * c + i != z)
-    project(1 - x, c)
+    project(1 - x, c, True)
     for i, h in in_turn:
         arrived(half(xb.at[1 - x, 2 * (1 - c) + i], h), NUM["core_far"] + 2 * i + h)
-    project(1 - x, 1 - c)
-
-    mine = pl.ds(pl.multiple_of(128 * me, 128), 128)
-    for turn, (xx, cc) in enumerate(((0, 1 - c), (1, 1 - c), (0, c), (1, c))):
-        rows = rows_of(xx, cc)
-        q_rows = q[rows, :]
-        total = jnp.zeros((256, 256), f32)
-        for h in range(2):
-            scores = mm_nt(jnp.where(head_lanes[h], q_rows, 0), k[...])
-            prob = jnp.exp(scores).astype(bf16)
-            probs[h, rows, :] = prob
-            total = total + mm(prob, vaug[h])
-        inverse = 1.0 / total[:, 128:256]
-        attended = total[:, 0:128] * inverse
-        att[rows, :] = attended
-        inv[rows, :] = inverse
-        obuf[turn] = attended.astype(bf16)
-        there = abuf.at[pl.ds(256 * xx, 256), mine]
-        if turn < 2:
-            send(obuf.at[turn], there, NUM["o_diag"] + xx, NUM["o_diag"] + xx, diag_dev)
-            send(obuf.at[turn], there, NUM["o_core"] + xx, NUM["o_core"] + xx, core_dev)
-        else:
-            send(obuf.at[turn], there, NUM["o_x"] + xx, NUM["o_x"] + xx, x_dev)
-            abuf[256 * xx : 256 * xx + 256, mine] = attended.astype(bf16)
-
-    for i in (0, 1):
+    project(1 - x, 1 - c, False)
+    def forward_cot(i):
         @pl.when(2 * c + i != z)
         def _():
             arrived(cotb.at[x, i], NUM["cot"] + i)
-    pl.when(jnp.logical_not(crossing))(self_cot.wait)
-    for i in (0, 1):
+
+        @pl.when(2 * c + i == z)
+        def _():
+            self_cot.wait()
+
         send(cotb.at[x, i], cotb.at[x, i], NUM["cot_x"] + i, NUM["cot_x"] + i, x_dev)
+
+
+    for d in range(4):
+        sums_all = [sums[d, h] + attend(qt[own_half, pair_columns(pairs[d])], pairs[d], h, late,
+                                        own_rows if d == 0 else None) for h in range(2)]
+        abuf[own_half, pair_columns(pairs[d])] = attended_of(sums_all, own_rows if d == 0 else None)
+    forward_cot(first)
+    for d in range(4):
+        sums_all = [attend(qt[far_half, pair_columns(pairs[d])], pairs[d], h, every,
+                           far_rows if d == 0 else None) for h in range(2)]
+        abuf[far_half, pair_columns(pairs[d])] = attended_of(sums_all, far_rows if d == 0 else None)
+        if d == 1:
+            forward_cot(1 - first)
+
+    def other_probs(xx):
+        rows = rows_of(xx, 1 - c)
+        attended_of([attend(q[rows, :], me, h, every, rows) for h in range(2)], rows)
 
     def norm(hidden):
         centred = hidden - jnp.mean(hidden, axis=-1, keepdims=True)
@@ -656,12 +700,6 @@
     for xx in (0, 1):
         there = pl.ds(256 * xx, 256)
 
-        def columns_of(hx, hc):
-            return pl.ds(pl.multiple_of(128 * (2 * hx + hc), 128), 128)
-
-        arrived(abuf.at[there, columns_of(x, 1 - c)], NUM["o_core"] + xx)
-        arrived(abuf.at[there, columns_of(1 - x, 1 - c)], NUM["o_diag"] + xx)
-        arrived(abuf.at[there, columns_of(1 - x, c)], NUM["o_x"] + xx)
         start_x = xb[xx, pl.ds(2 * c, 2)].reshape(256, 512).astype(f32) + pair_row
         normalized, s1 = norm(start_x + (mm(abuf[there, :], wo[...]) + ob[...]))
         s1_parts.append(s1)
@@ -681,7 +719,6 @@
         normalized, s2 = norm((ffn + db[...]) + normed + start_x)
         n2[there, :] = normalized
         s2b[there, :] = jnp.broadcast_to(s2, (256, 128))
-    own_half = pl.ds(pl.multiple_of(256 * x, 256), 256)
     lob[...] = (n2[own_half, :] * g2[...] + b2[...]).astype(bf16).reshape(2, 128, 512)
 
     def give_back(block, out, name):
@@ -693,10 +730,10 @@
             out[z % 2] = block[z % 2]
 
     give_back(lob, lo_out, "lo")
-    for i in (0, 1):
-        arrived(cotb.at[1 - x, i], NUM["cot_x"] + i)
-    for xx in (0, 1):
-        there = pl.ds(256 * xx, 256)
+    for turn, (xx, there) in enumerate(((x, own_half), (1 - x, far_half))):
+        if turn == 1:
+            for i in (0, 1):
+                arrived(cotb.at[1 - x, i], NUM["cot_x"] + i)
         g = cotb[xx].reshape(256, 512).astype(f32)
         normalized = n2[there, :]
         gain_part, bias_part = column_sum(g * normalized), column_sum(g)
@@ -706,87 +743,143 @@
         ffn_grad[there, :] = low
         down_part = column_sum(low.astype(f32))
         for at, part in ((14, gain_part), (15, bias_part), (13, down_part)):
-            vecb[at : at + 1, :] = part * once if xx == 0 else vecb[at : at + 1, :] + part * once
+            vecb[at : at + 1, :] = part * once if turn == 0 else vecb[at : at + 1, :] + part * once
 
     def number(n, step):
         return NUM["lane"] + 12 * n + step
 
-    def fold(target, received):
-        target[...] = (target[...].astype(f32) + received[...].astype(f32)).astype(bf16)
-
-    def scatter(n, axis, last):
-        if axis == "y":
-            part = own.at[n, c, 1 - y, z] if last else own.at[n, c, 1 - y]
-            send(part, r1.at[n, 0] if last else r1.at[n], number(n, 1), number(n, 1), y_dev)
-        else:
-            for d in (1, 2, 3):
-                part = own.at[n, c, y, (z + d) % 4] if last else own.at[n, c, :, (z + d) % 4]
-                send(part, r3.at[n, 3 - d, 0] if last else r3.at[n, 3 - d],
-                     number(n, 1 + d), number(n, 5 - d), z_devs[d - 1])
-
-    def collect(n, axis, last):
-        if axis == "y":
-            arrived(r1.at[n, 0] if last else r1.at[n], number(n, 1))
-            parts = [r1.at[n, 0] if last else r1.at[n]]
-        else:
-            for d in (1, 2, 3):
-                arrived(r3.at[n, d - 1, 0] if last else r3.at[n, d - 1], number(n, 1 + d))
-            parts = [r3.at[n, d, 0] if last else r3.at[n, d] for d in range(3)]
-        if last:
-            target = own.at[n, c, y, z]
-        else:
-            target = own.at[n, c, y] if axis == "y" else own.at[n, c, :, z]
+    def add_up(target, parts, result=None):
         value = target[...].astype(f32)
         for part in parts:
             value = value + part[...].astype(f32)
-        if last:
-            target = full.at[n, x, c, y, z]
-        target[...] = value.astype(bf16)
-
-    def region(buffer, n, done, **other):
-        place = dict(x=x, y=y, z=z) | other
-        at = {axis: slice(None) if axis in done else place[axis] for axis in "xyz"}
-        return buffer.at[n, at["x"], c, at["y"], at["z"]]
-
-    def spread(buffer, n, number_of, order, stage):
-        part = region(buffer, n, order[:stage])
-        if stage == 3:
-            send(part, part, number_of(10), number_of(10), core_dev)
-        elif order[stage] == "z":
-            for d in (1, 2, 3):
-                send(part, part, number_of(4 + d), number_of(8 - d), z_devs[d - 1])
-        else:
-            at, device = {"x": (9, x_dev), "y": (8, y_dev)}[order[stage]]
-            send(part, part, number_of(at), number_of(at), device)
-
-    def gather(buffer, n, number_of, order, stage):
-        if stage == 3:
-            arrived(buffer.at[n, :, 1 - c], number_of(10))
-        elif order[stage] == "z":
-            for d in (1, 2, 3):
-                arrived(region(buffer, n, order[:stage], z=(z + d) % 4), number_of(4 + d))
-        elif order[stage] == "x":
-            arrived(region(buffer, n, order[:stage], x=1 - x), number_of(9))
-        else:
-            arrived(region(buffer, n, order[:stage], y=1 - y), number_of(8))
+        (target if result is None else result)[...] = value.astype(bf16)
+
+    def travel(mine, r1, r3, whole, number_of, scatter, order):
+        stages = []
+
+        def scatter_stages(axis, last):
+            def part(zz):
+                return mine.at[y, zz] if last else mine.at[:, zz]
+
+            def slot(d):
+                return r3.at[d, 0] if last else r3.at[d]
+
+            result = whole.at[x, c, y, z] if last else None
+            if axis == "y":
+                box = r1.at[0] if last else r1
+
+                def start():
+                    send(mine.at[1 - y, z] if last else mine.at[1 - y], box, number_of(1), number_of(1), y_dev)
+
+                def finish():
+                    arrived(box, number_of(1))
+                    add_up(mine.at[y, z] if last else mine.at[y], [box], result)
+
+                stages.append((start, finish))
+            elif axis == "z":
+                def start():
+                    for d in (1, 2, 3):
+                        send(part((z + d) % 4), slot(3 - d), number_of(1 + d), number_of(5 - d), z_devs[d - 1])
+
+                def finish():
+                    for d in (1, 2, 3):
+                        arrived(slot(d - 1), number_of(1 + d))
+                    add_up(part(z), [slot(d) for d in range(3)], result)
+
+                stages.append((start, finish))
+            else:
+                def start():
+                    send(part(3 - z_near), slot(0), number_of(2), number_of(2), near_dev)
+
+                def finish():
+                    arrived(slot(0), number_of(2))
+                    add_up(part(3 - z), [slot(0)])
+
+                def start_two():
+                    send(part(3 - z), slot(1), number_of(3), number_of(3), mirror_dev)
+                    send(part(z_near), slot(2), number_of(4), number_of(4), near_dev)
+
+                def finish_two():
+                    arrived(slot(1), number_of(3))
+                    arrived(slot(2), number_of(4))
+                    add_up(part(z), [slot(1), slot(2)], result)
+
+                stages.append((start, finish))
+                stages.append((start_two, finish_two))
+
+        def region(done, **other):
+            place = dict(x=x, y=y, z=z) | other
+            at = {axis: slice(None) if axis in done else place[axis] for axis in "xyz"}
+            return whole.at[at["x"], c, at["y"], at["z"]]
+
+        def gather_stages(axis, done):
+            part = region(done)
+            if axis == "z":
+                def start():
+                    for d in (1, 2, 3):
+                        send(part, part, number_of(4 + d), number_of(8 - d), z_devs[d - 1])
+
+                def finish():
+                    for d in (1, 2, 3):
+                        arrived(region(done, z=(z + d) % 4), number_of(4 + d))
+
+                stages.append((start, finish))
+            elif axis == "w":
+                def start():
+                    send(part, part, number_of(6), number_of(6), mirror_dev)
+                    send(part, part, number_of(5), number_of(5), near_dev)
+
+                def finish():
+                    arrived(region(done, z=z_near), number_of(5))
+                    arrived(region(done, z=3 - z), number_of(6))
+
+                def start_two():
+                    passed = region(done, z=3 - z)
+                    send(passed, passed, number_of(7), number_of(7), near_dev)
+
+                def finish_two():
+                    arrived(region(done, z=3 - z_near), number_of(7))
+
+                stages.append((start, finish))
+                stages.append((start_two, finish_two))
+            else:
+                at, device, there = {"x": (9, x_dev, dict(x=1 - x)), "y": (8, y_dev, dict(y=1 - y))}[axis]
+
+                def start():
+                    send(part, part, number_of(at), number_of(at), device)
+
+                def finish():
+                    arrived(region(done, **there), number_of(at))
+
+                stages.append((start, finish))
+
+        scatter_stages(scatter[0], False)
+        scatter_stages(scatter[1], True)
+        for at, axis in enumerate(order):
+            gather_stages(axis, order[:at].replace("w", "z"))
+
+        def start():
+            send(whole.at[:, c], whole.at[:, c], number_of(10), number_of(10), core_dev)
+
+        def finish():
+            arrived(whole.at[:, 1 - c], number_of(10))
+
+        stages.append((start, finish))
+        return stages
+
+    lane_stages = [
+        travel(own.at[n, c], r1.at[n], r3.at[n], full.at[n], functools.partial(number, n), SCATTER[n], GATHER[n])
+        for n in range(LANES)
+    ]
 
     def lane_step(n, step):
-        scatter_order, order = SCATTER[n], GATHER[n]
-        number_of = functools.partial(number, n)
         if step == 0:
             arrived(r0.at[n], number(n, 0))
-            fold(own.at[n, c], r0.at[n])
-            scatter(n, scatter_order[0], False)
-        elif step == 1:
-            collect(n, scatter_order[0], False)
-            scatter(n, scatter_order[1], True)
-        elif step == 2:
-            collect(n, scatter_order[1], True)
-            spread(full, n, number_of, order, 0)
+            add_up(own.at[n, c], [r0.at[n]])
         else:
-            gather(full, n, number_of, order, step - 3)
-            if step < 6:
-                spread(full, n, number_of, order, step - 2)
+            lane_stages[n][step - 1][1]()
+        if step < len(lane_stages[n]):
+            lane_stages[n][step][0]()
 
     own_columns = pl.ds(pl.multiple_of(256 * x, 256), 256)
 
@@ -852,7 +945,7 @@
             grad_low = jnp.where(head_lanes[h], numer_grad, rest).astype(bf16)
             prob = probs[h, rows, :]
             score_grad = (prob.astype(f32) * mm_nt(grad_low, vback[h])).astype(bf16)
-            dq_rows = dq_rows + jnp.where(head_lanes[h], mm(score_grad, k[...]), 0.0)
+            dq_rows = dq_rows + jnp.where(head_lanes[h], mm(score_grad, k[:, mine]), 0.0)
             part = slice(64 * h, 64 * h + 64)
             dk_part = mm(jnp.transpose(q_rows)[part, :], score_grad)
             dv_part = mm(jnp.transpose(grad_low)[part, :], prob)
@@ -870,30 +963,20 @@
     def qnumber(t, step):
         return NUM["qkv"] + 12 * t + step
 
+    part_stages = [
+        travel(qown.at[t], qr1.at[t], qr3.at[t], qfull.at[t], functools.partial(qnumber, t), QSCATTER[t], QGATHER[t])
+        for t in range(3)
+    ]
+
     def projection_weights(t):
         value = mm_tn(lowb[...], dqkv[:, 128 * t : 128 * t + 128])
         qown[t] = value.astype(bf16).reshape(2, 4, 64, 128)
-        send(qown.at[t, 1 - y], qr1.at[t], qnumber(t, 0), qnumber(t, 0), y_dev)
+        part_stages[t][0][0]()
 
     def projection_step(t, step):
-        number_of, order = functools.partial(qnumber, t), QGATHER[t]
-        if step == 0:
-            arrived(qr1.at[t], qnumber(t, 0))
-            fold(qown.at[t, y], qr1.at[t])
-            for d in (1, 2, 3):
-                send(qown.at[t, y, (z + d) % 4], qr3.at[t, 3 - d], qnumber(t, d), qnumber(t, 4 - d), z_devs[d - 1])
-        elif step == 1:
-            for d in (1, 2, 3):
-                arrived(qr3.at[t, d - 1], qnumber(t, d))
-            value = qown[t, y, z].astype(f32)
-            for d in range(3):
-                value = value + qr3[t, d].astype(f32)
-            qfull[t, x, c, y, z] = value.astype(bf16)
-            spread(qfull, t, number_of, order, 0)
-        else:
-            gather(qfull, t, number_of, order, step - 2)
-            if step < 5:
-                spread(qfull, t, number_of, order, step - 1)
+        part_stages[t][step][1]()
+        if step + 1 < len(part_stages[t]):
+            part_stages[t][step + 1][0]()
 
     def input_back(step):
         xx, cc = ((1 - x, 1 - c), (x, 1 - c), (1 - x, c), (x, c))[step]
@@ -925,35 +1008,31 @@
             vecb[9:10, mine] = column_sum(dqkv[:, 256:384].astype(f32))
             vecb[20:24, :] = jnp.zeros((4, 512), f32)
             send(vecb, vecr.at[0], NUM["vec"], NUM["vec"], core_dev)
-        elif step < 4:
+        else:
             level = step - 1
             arrived(vecr.at[level], NUM["vec"] + level)
-            value = (vecb[...] if level == 0 else vecr[2 + level]) + vecr[level]
-            if level < 2:
-                vecr[3 + level] = value
-                send(vecr.at[3 + level], vecr.at[level + 1], NUM["vec"] + level + 1, NUM["vec"] + level + 1,
-                     (x_dev, y_dev)[level])
+            value = (vecb if level == 0 else vecr.at[4 + level])[...] + vecr[level]
+            if level < 4:
+                vecr[5 + level] = value
+                send(vecr.at[5 + level], vecr.at[level + 1], NUM["vec"] + level + 1, NUM["vec"] + level + 1,
+                     (x_dev, y_dev, near_dev, mirror_dev)[level])
             else:
-                vecz[z] = value
-                for d in (1, 2, 3):
-                    send(vecz.at[z], vecz.at[z], NUM["vec"] + 2 + d, NUM["vec"] + 6 - d, z_devs[d - 1])
-        else:
-            for d in (1, 2, 3):
-                arrived(vecz.at[(z + d) % 4], NUM["vec"] + 2 + d)
-            value = vecz[0]
-            for t in range(1, 4):
-                value = value + vecz[t]
-            vec_out[...] = value
+                vec_out[...] = value
 
     tasks = {(NORM, 0, 0): first_back, (SPLIT, 0, 0): projection_grads, (RETURN, 0, 0): input_out}
-    for kind, task, counts in (
-        (FILL, lane_fill, (LANES,)), (FFN, ffn_back, (4,)), (ATTN, attention_back, (4,)), (WEIGHT, projection_weights, (3,)),
-        (INPUT, input_back, (4,)), (SMALL, vectors, (5,)), (LANE, lane_step, (LANES, 7)), (PART, projection_step, (3, 6)),
+    for kind, task, count in (
+        (FILL, lane_fill, LANES), (FFN, ffn_back, 4), (ATTN, attention_back, 4), (PROBS, other_probs, 2), (WEIGHT, projection_weights, 3),
+        (INPUT, input_back, 4), (SMALL, vectors, 6),
     ):
-        for at in range(counts[0]):
-            for step in range(counts[-1]) if len(counts) == 2 else (0,):
-                tasks[kind, at, step] = functools.partial(task, *(at, step)[: len(counts)])
-    for entry in ORDER:
+        for at in range(count):
+            tasks[kind, at, 0] = functools.partial(task, at)
+    for n in range(LANES):
+        for step in range(len(lane_stages[n]) + 1):
+            tasks[LANE, n, step] = functools.partial(lane_step, n, step)
+    for t in range(3):
+        for step in range(len(part_stages[t])):
+            tasks[PART, t, step] = functools.partial(projection_step, t, step)
+    for at, entry in enumerate(ORDER):
         tasks.pop(entry)()
     assert not tasks
 
@@ -1046,13 +1125,13 @@
         for shape, dtype in (
             ((2, 4, 128, 512), bf16), ((1024, 512), bf16), ((2, 2, 128, 512), bf16),
             ((8, 512), f32), ((8, 512), f32), ((8, 512), f32),
-            ((512, 384), bf16), ((512, 512), bf16), ((512, 2048), bf16), ((2048, 512), bf16),
+            ((512, 1536), bf16), ((512, 384), bf16), ((512, 512), bf16), ((512, 2048), bf16), ((2048, 512), bf16),
             ((1, 512), f32), ((1, 512), f32), ((1, 512), f32), ((1, 512), f32), ((1, 512), f32),
             ((1, 2048), f32), ((1, 512), f32), ((1, 512), f32), ((1, 512), f32),
-            ((1024, 128), bf16), ((1024, 128), bf16),
-            ((2, 1024, 256), bf16), ((2, 1024, 128), bf16),
+            ((512, 512), bf16), ((1024, 128), bf16), ((1024, 512), bf16),
+            ((4, 1024, 256), bf16), ((2, 1024, 128), bf16),
             ((1024, 128), f32), ((1024, 128), f32),
-            ((4, 256, 128), bf16), ((512, 512), bf16),
+            ((4, 2, 256, 256), f32), ((512, 512), bf16),
             ((512, 2048), f32), ((512, 2048), bf16), ((512, 2048), bf16),
             ((256, 512), f32), ((2, 128, 512), bf16), ((2, 128, 512), bf16),
             ((512, 512), f32), ((512, 512), f32), ((512, 128), f32), ((512, 512), bf16),
@@ -1060,10 +1139,10 @@
             ((512, 128), bf16), ((2, 512, 128), bf16), ((2, 1024, 1024), bf16),
             ((128, 1024), f32), ((128, 1024), f32), ((1024, 384), bf16),
             ((3, 256, 512), bf16), ((2, 256, 512), bf16), ((256, 512), bf16), ((256, 512), f32),
-            ((24, 512), f32), ((5, 24, 512), f32), ((4, 24, 512), f32),
+            ((24, 512), f32), ((9, 24, 512), f32),
             ((LANES, 2, 2, 4, 16, 512), bf16), ((LANES, 2, 4, 16, 512), bf16), ((LANES, 4, 16, 512), bf16),
             ((LANES, 3, 2, 16, 512), bf16),
-            ((3, 2, 4, 64, 128), bf16), ((3, 4, 64, 128), bf16), ((3, 3, 64, 128), bf16),
+            ((3, 2, 4, 64, 128), bf16), ((3, 4, 64, 128), bf16), ((3, 3, 2, 64, 128), bf16),
         )
     ] + [
         pltpu.SemaphoreType.DMA((NUM.count,)),

time: 102 us -> 92.3 us (0.905)
  Pallas kernels: 101 us -> 91.2 us
    pallas_call x1, Pallas kernels: 96 us -> 86 us  [fused_local(): pl.pallas_call(fused, out_shape=out_shape, in_specs=in_specs, out_specs=[...]
where the time goes in v3:
time: 92.3 us; the launch traced here: 92.1 us
  Pallas kernels  91.2 us (99%)
    pallas_call x1, Pallas kernels, fused_local(): pl.pallas_call(fused, out_shape=out_shape, in_specs=in_specs, out_specs=[...  86 us
    pallas_call x1, Pallas kernels, fused_local(): pl.pallas_call(finish, out_shape=[jax.ShapeDtypeStruct(shape, f32) for sh...  5.27 us

profile of v3, /device:TPU:1, one launch (start us, length us, event | category | flops | bytes accessed | tf_op | source)
XLA Modules:
  0.0 92.1 jit_solution(11908218881485684604)
XLA Ops:
  0.7 86.0 %shard_map.297 = (bf16[2,128,512]{2,1,0:T(8,128)(2,1)S(1)}, bf16[2,128,512]{2,1,0:T(8,128)(2,1)S(1)}, bf16[9,2,2,2,4,16,512]{6,5,4,3,2,1,0:T(8,128)(2,1)S(1)}, b...) custom-call(bf16[2,128,512]{2,1,0:T(8,128)(2,1)} %x_in.1, bf16[2,128,512]{2,1,0:T(8,128)(2,1)} %cot_in.1, ...), custom_call_target="tpu_custom_call" | custom-call | tf_op jit(solution)/shard_map/pallas_call | solution.py:1152
  86.6 5.3 %shard_map.298 = (f32[2,128,512]{2,1,0:T(8,128)}, f32[2,128,512]{2,1,0:T(8,128)}, f32[2048,512]{1,0:T(8,128)}, f32[512,2048]{1,0:T(8,128)}, f32[512,512]{1,0:T(8...) custom-call(bf16[2,128,512]{2,1,0:T(8,128)(2,1)S(1)} %get-tuple-elem, ...), custom_call_target="tpu_custom_call" | custom-call | tf_op jit(solution)/shard_map/pallas_call | solution.py:1165

commit v4 on v3

--- a/solution.py
+++ b/solution.py
@@ -359,6 +359,7 @@
 MESH = pl.DeviceIdType.MESH
 f32, bf16 = jnp.float32, jnp.bfloat16
 LANES = 9
+PIECES, PIECE = 4, 32
 
 
 def mm(a, b):
@@ -389,8 +390,8 @@
 def semaphore_numbers():
     numbers = Numbers()
     for name, size in (
-        ("x", 4), ("cot", 2), ("lo", 2), ("ig", 2), ("cot_x", 2),
-        ("xn", 4), ("core_own", 4), ("core_far", 4), ("meta", 1),
+        ("x", 2 * PIECES), ("cot", 2), ("lo", 2), ("ig", 2), ("cot_x", 2),
+        ("xn", 2 * PIECES), ("core_own", 2 * PIECES), ("core_far", 2 * PIECES), ("meta", 1),
         ("do", 1), ("dx_core", 2), ("dx_x", 1), ("vec", 6),
         ("lane", LANES * 12), ("qkv", 3 * 12),
     ):
@@ -399,33 +400,33 @@
 
 
 NUM = semaphore_numbers()
-LOCAL = 17 + 2
+LOCAL = 19
 
 SCATTER = ('yz', 'yz', 'yz', 'yz', 'yw', 'yw', 'yw', 'yw', 'yw')
-GATHER = ('wxy', 'wxy', 'zxy', 'wyx', 'wxy', 'wxy', 'zxy', 'wyx', 'zyx')
+GATHER = ('wxy', 'wxy', 'wyx', 'wyx', 'wyx', 'zyx', 'zxy', 'zxy', 'zyx')
 QSCATTER = ('yw', 'yw', 'yw')
-QGATHER = ('yzx', 'yxz', 'zxy')
-FILL, LANE, FFN, NORM, ATTN, SPLIT, WEIGHT, PART, INPUT, RETURN, SMALL, PROBS = range(12)
+QGATHER = ('zxy', 'zyx', 'wxy')
+FILL, LANE, FFN, NORM, ATTN, SPLIT, WEIGHT, PART, INPUT, RETURN, SMALL, PROBS, SUMS = range(13)
 ORDER = (
-    (FILL, 1, 0), (FFN, 0, 0), (FILL, 2, 0), (FILL, 3, 0), (FILL, 0, 0), (LANE, 1, 0), (FFN, 1, 0),
-    (FFN, 2, 0), (LANE, 2, 0), (FFN, 3, 0), (LANE, 3, 0), (LANE, 0, 0), (FILL, 6, 0), (FILL, 4, 0),
-    (FILL, 7, 0), (NORM, 0, 0), (LANE, 1, 1), (LANE, 4, 0), (ATTN, 0, 0), (LANE, 2, 1), (ATTN, 1, 0),
-    (LANE, 3, 1), (LANE, 7, 0), (LANE, 6, 0), (FILL, 8, 0), (FILL, 5, 0), (PROBS, 1, 0), (LANE, 1, 2),
-    (LANE, 0, 1), (LANE, 8, 0), (LANE, 5, 0), (PROBS, 0, 0), (LANE, 4, 1), (LANE, 2, 2), (ATTN, 2, 0),
-    (LANE, 7, 1), (ATTN, 3, 0), (LANE, 1, 3), (LANE, 3, 2), (SPLIT, 0, 0), (WEIGHT, 2, 0), (LANE, 8, 1),
-    (LANE, 0, 2), (WEIGHT, 1, 0), (WEIGHT, 0, 0), (LANE, 4, 2), (LANE, 6, 1), (INPUT, 0, 0), (INPUT, 1, 0),
-    (LANE, 5, 1), (LANE, 2, 3), (LANE, 7, 2), (LANE, 1, 4), (INPUT, 2, 0), (INPUT, 3, 0), (LANE, 3, 3),
-    (SMALL, 0, 0), (PART, 2, 0), (LANE, 8, 2), (LANE, 0, 3), (SMALL, 1, 0), (PART, 1, 0), (LANE, 4, 3),
-    (LANE, 6, 2), (LANE, 2, 4), (LANE, 5, 2), (PART, 0, 0), (LANE, 7, 3), (LANE, 3, 4), (LANE, 1, 5),
-    (PART, 2, 1), (LANE, 8, 3), (LANE, 0, 4), (PART, 1, 1), (LANE, 4, 4), (LANE, 6, 3), (LANE, 2, 5),
-    (LANE, 5, 3), (PART, 0, 1), (LANE, 7, 4), (LANE, 2, 6), (LANE, 3, 5), (PART, 2, 2), (RETURN, 0, 0),
-    (SMALL, 2, 0), (LANE, 8, 4), (PART, 1, 2), (LANE, 1, 6), (LANE, 4, 5), (LANE, 0, 5), (LANE, 1, 7),
-    (LANE, 6, 4), (SMALL, 3, 0), (LANE, 5, 4), (PART, 0, 2), (LANE, 3, 6), (LANE, 7, 5), (LANE, 8, 5),
-    (PART, 1, 3), (LANE, 4, 6), (LANE, 3, 7), (PART, 2, 3), (LANE, 6, 5), (LANE, 0, 6), (PART, 0, 3),
-    (LANE, 0, 7), (LANE, 7, 6), (LANE, 8, 6), (PART, 1, 4), (LANE, 8, 7), (PART, 2, 4), (LANE, 4, 7),
-    (SMALL, 4, 0), (LANE, 5, 5), (LANE, 4, 8), (LANE, 7, 7), (LANE, 6, 6), (PART, 0, 4), (LANE, 7, 8),
-    (LANE, 5, 6), (LANE, 6, 7), (PART, 2, 5), (PART, 2, 6), (PART, 0, 5), (PART, 1, 5), (LANE, 5, 7),
-    (PART, 0, 6), (PART, 1, 6), (LANE, 5, 8), (SMALL, 5, 0),
+    (RETURN, 1, 0), (FILL, 0, 0), (FFN, 0, 0), (FILL, 3, 0), (FILL, 2, 0), (LANE, 0, 0), (FILL, 1, 0),
+    (FFN, 1, 0), (LANE, 3, 0), (LANE, 2, 0), (FFN, 2, 0), (LANE, 1, 0), (FFN, 3, 0), (FILL, 5, 0),
+    (FILL, 7, 0), (PROBS, 1, 0), (LANE, 0, 1), (NORM, 0, 0), (FILL, 6, 0), (LANE, 5, 0), (LANE, 3, 1),
+    (ATTN, 0, 0), (FILL, 4, 0), (LANE, 2, 1), (ATTN, 1, 0), (LANE, 6, 0), (LANE, 4, 0), (LANE, 1, 1),
+    (PROBS, 0, 0), (ATTN, 2, 0), (LANE, 5, 1), (LANE, 7, 0), (LANE, 0, 2), (LANE, 3, 2), (ATTN, 3, 0),
+    (SPLIT, 0, 0), (INPUT, 0, 0), (LANE, 2, 2), (FILL, 8, 0), (WEIGHT, 0, 0), (LANE, 6, 1), (LANE, 5, 2),
+    (INPUT, 1, 0), (SUMS, 0, 0), (INPUT, 2, 0), (LANE, 8, 0), (LANE, 1, 2), (SUMS, 1, 0), (LANE, 0, 3),
+    (LANE, 4, 1), (WEIGHT, 2, 0), (LANE, 3, 3), (WEIGHT, 1, 0), (INPUT, 3, 0), (LANE, 6, 2), (LANE, 2, 3),
+    (PART, 0, 0), (LANE, 5, 3), (LANE, 0, 4), (SMALL, 0, 0), (LANE, 1, 3), (LANE, 3, 4), (LANE, 7, 1),
+    (SMALL, 1, 0), (PART, 2, 0), (LANE, 8, 1), (PART, 0, 1), (LANE, 4, 2), (LANE, 2, 4), (LANE, 1, 4),
+    (LANE, 6, 3), (LANE, 5, 4), (PART, 2, 1), (LANE, 3, 5), (LANE, 0, 5), (LANE, 8, 2), (SMALL, 2, 0),
+    (PART, 0, 2), (PART, 1, 0), (LANE, 6, 4), (LANE, 4, 3), (PART, 2, 2), (LANE, 7, 2), (LANE, 5, 5),
+    (LANE, 1, 5), (LANE, 8, 3), (PART, 1, 1), (PART, 0, 3), (LANE, 6, 5), (PART, 2, 3), (LANE, 4, 4),
+    (LANE, 2, 5), (LANE, 7, 3), (LANE, 8, 4), (PART, 1, 2), (LANE, 0, 6), (LANE, 4, 5), (PART, 2, 4),
+    (PART, 0, 4), (SMALL, 3, 0), (LANE, 7, 4), (RETURN, 0, 0), (LANE, 8, 5), (LANE, 3, 6), (LANE, 4, 6),
+    (SMALL, 4, 0), (PART, 1, 3), (LANE, 6, 6), (LANE, 7, 5), (LANE, 2, 6), (LANE, 5, 6), (PART, 0, 5),
+    (PART, 1, 4), (PART, 0, 6), (PART, 2, 5), (LANE, 8, 6), (LANE, 7, 6), (LANE, 4, 7), (LANE, 7, 7),
+    (LANE, 6, 7), (LANE, 4, 8), (LANE, 1, 6), (LANE, 8, 7), (PART, 2, 6), (SMALL, 5, 0), (LANE, 3, 7),
+    (LANE, 0, 7), (PART, 1, 5), (LANE, 1, 7), (LANE, 2, 7), (LANE, 5, 7), (PART, 2, 7), (PART, 1, 6),
 )
 
 
@@ -433,8 +434,8 @@
     x_in, cot_in, groups, lengths, table_in, wqkv_in, qb_in, vb_in, wo_in, ob_in, g1_in, b1_in,
     wup_in, ub_in, wdn_in, db_in, g2_in, b2_in,
     lo_out, ig_out, full, qfull, vec_out,
-    xb, lowb, cotb, table, meta, meta_far, wqkv, wq, wo, wup, wdn, qb, vb, ob, g1, b1, ub, db, g2, b2,
-    qt, q, k, vaug, vback, att, inv, sums, abuf, gelu_grad, act, pre_grad, res, lob, igb, n1, n2, s2b, attn_grad,
+    x_here, cot_here, xb, lowb, cotb, table, meta, meta_far, wqkv, wq, wo, wup, wdn, qb, vb, ob, g1, b1, ub, db, g2, b2,
+    qt, q, k, vaug, vback, att, inv, sums, abuf, before, act, pre_grad, res, lob, igb, n1, n2, s1b, s2b, attn_grad,
     normed_low, ffn_grad, second, normed_grad, dob, dor, probs, dkt, dvt, dqkv, dxb, dxr0, dxr1, dxo,
     vecb, vecr,
     own, r0, r1, r3, qown, qr1, qr3,
@@ -486,9 +487,55 @@
     def land(copies):
         for copy in copies:
             copy.wait()
-            local_copies[local_copies.index(copy)] = None
-
-    wait_qkv = [fetch(table_in, table), fetch(qb_in, qb), fetch(vb_in, vb)]
+            local_copies[[entry is copy for entry in local_copies].index(True)] = None
+
+    wait_table = fetch(table_in, table)
+    wait_tokens = [fetch(x_in, x_here), fetch(cot_in, cot_here)]
+
+    barrier = pltpu.get_barrier_semaphore()
+    near = [core_dev, x_dev, y_dev] + z_devs
+    for device in near:
+        pl.semaphore_signal(barrier, inc=1, device_id=device, device_id_type=MESH)
+
+    def greet(devices):
+        for device in devices:
+            pl.semaphore_signal(barrier, inc=1, device_id=device, device_id_type=MESH)
+        pl.semaphore_wait(barrier, len(near) + len(devices))
+
+    @pl.when(crossing)
+    def _():
+        greet([dev(xx, y, 2 * c + i, z // 2) for i in range(2) for xx in (x, 1 - x)])
+
+    @pl.when(jnp.logical_not(crossing))
+    def _():
+        greet([dev(1 - x, y, z_near, c)])
+
+    def half(ref, h):
+        return ref.at[pl.ds(PIECE * h, PIECE)]
+
+    def peer(i):
+        return dev(x, y, 2 * c + i, z // 2)
+
+    land(wait_tokens)
+    first = jnp.where(crossing, 1 - c, z % 2)
+    in_turn = [(i, h) for i in (first, 1 - first) for h in range(PIECES)]
+    for i, h in in_turn:
+        send(half(x_here.at[i], h), half(xb.at[x, z], h), NUM["x"] + PIECES * i + h, NUM["x"] + PIECES * (z % 2) + h,
+             peer(i), when=2 * c + i != z)
+    def send_cot():
+        for i in (first, 1 - first):
+            send(cot_here.at[i], cotb.at[x, z % 2], NUM["cot"] + i, NUM["cot"] + z % 2, peer(i), when=2 * c + i != z)
+        for i in (first, 1 - first):
+            send(cot_here.at[i], cotb.at[x, z % 2], NUM["cot_x"] + i, NUM["cot_x"] + z % 2,
+                 dev(1 - x, y, 2 * c + i, z // 2))
+
+    send_cot()
+    @pl.when(jnp.logical_not(crossing))
+    def _():
+        xb[x, z] = x_here[z % 2]
+        cotb[x, z % 2] = cot_here[z % 2]
+
+    wait_qkv = [fetch(qb_in, qb), fetch(vb_in, vb)]
     for t in range(3):
         columns = pl.ds(pl.multiple_of(512 * t + 128 * me, 128), 128)
         wait_qkv.append(fetch(wqkv_in.at[:, columns], wq.at[:, pl.ds(128 * t, 128)]))
@@ -499,48 +546,7 @@
                      (wdn_in, wdn), (db_in, db), (g2_in, g2), (b2_in, b2))
     ]
 
-    barrier = pltpu.get_barrier_semaphore()
-    near = [core_dev, x_dev, y_dev] + z_devs
-    for device in near:
-        pl.semaphore_signal(barrier, inc=1, device_id=device, device_id_type=MESH)
-
-    @pl.when(crossing)
-    def _():
-        for i in range(2):
-            pl.semaphore_signal(
-                barrier, inc=1, device_id=dev(x, y, 2 * c + i, z // 2), device_id_type=MESH
-            )
-        pl.semaphore_wait(barrier, len(near) + 2)
-
-    @pl.when(jnp.logical_not(crossing))
-    def _():
-        pl.semaphore_wait(barrier, len(near))
-
-    def half(ref, h):
-        return ref.at[pl.ds(64 * h, 64)]
-
-    def peer(i):
-        return dev(x, y, 2 * c + i, z // 2)
-
-    first = jnp.where(crossing, 1 - c, z % 2)
-    in_turn = [(i, h) for i in (first, 1 - first) for h in (0, 1)]
-    for i, h in in_turn:
-        send(half(x_in.at[i], h), half(xb.at[x, z], h), NUM["x"] + 2 * i + h, NUM["x"] + 2 * (z % 2) + h,
-             peer(i), when=2 * c + i != z)
-    def send_cot():
-        for i in (first, 1 - first):
-            send(cot_in.at[i], cotb.at[x, z % 2], NUM["cot"] + i, NUM["cot"] + z % 2, peer(i), when=2 * c + i != z)
-    self_x = pltpu.make_async_copy(x_in.at[z % 2], xb.at[x, z], lsem.at[LOCAL - 1])
-    self_cot = pltpu.make_async_copy(cot_in.at[z % 2], cotb.at[x, z % 2], lsem.at[LOCAL - 2])
-
-    @pl.when(jnp.logical_not(crossing))
-    def _():
-        self_x.start()
-        self_cot.start()
-        self_x.wait()
-
-
-    land(wait_qkv)
+    land([wait_table])
     slot = z % 2
     group, length = groups[slot], lengths[slot]
     meta[0:1, :] = table[pl.ds(group, 1), :]
@@ -554,14 +560,14 @@
 
         @pl.when(2 * c + i != z)
         def _():
-            arrived(block, NUM["x"] + 2 * i + h)
-
-        number = NUM["xn"] + 2 * i + h
+            arrived(block, NUM["x"] + PIECES * i + h)
+
+        number = NUM["xn"] + PIECES * i + h
         send(block, block, number, number, x_dev)
-        number = NUM["core_own"] + 2 * i + h
+        number = NUM["core_own"] + PIECES * i + h
         send(block, block, number, number, core_dev)
 
-    send_cot()
+    land(wait_qkv)
     arrived(meta_far, NUM["meta"])
     facts = jnp.where(crossing, meta_far[...], meta[...])
     pair_row, length_row, group_row = facts[0:1, :], facts[1:2, :], facts[2:3, :]
@@ -609,12 +615,12 @@
     def attend(q_rows, pair, h, keys, probs_rows):
         columns = pl.ds(pl.multiple_of(128 * pair, 128), 128)
         prob = jnp.exp(mm_nt(jnp.where(head_lanes[h], q_rows, 0), k[keys, columns])).astype(bf16)
-        if probs_rows is not None:
-            probs[h, probs_rows, keys] = prob
+        for at, rows in enumerate(probs_rows):
+            probs[h, rows, keys] = prob[256 * at : 256 * at + 256]
         return mm(prob, vaug[pair, keys, :])
 
-    def attended_of(sums, rows):
-        both = jnp.where(first_head, sums[0], sums[1])
+    def attended_of(parts, rows):
+        both = jnp.where(first_head, parts[0], parts[1])
         inverse = 1.0 / both[:, 128:256]
         attended = both[:, 0:128] * inverse
         if rows is not None:
@@ -624,7 +630,6 @@
 
     every = pl.ds(0, 1024)
     early = pl.ds(pl.multiple_of(512 * x, 512), 512)
-    late = pl.ds(pl.multiple_of(512 * (1 - x), 512), 512)
     pairs = [(me + d) % 4 for d in range(4)]
     own_rows, far_rows = rows_of(x, c), rows_of(1 - x, c)
     own_half = pl.ds(pl.multiple_of(256 * x, 256), 256)
@@ -633,51 +638,50 @@
     def pair_columns(pair):
         return pl.ds(pl.multiple_of(128 * pair, 128), 128)
 
-    def early_part(d, h):
-        sums[d, h] = attend(qt[own_half, pair_columns(pairs[d])], pairs[d], h, early, own_rows if d == 0 else None)
+    def own_early(d, h):
+        keep = [own_rows] if d == 0 else []
+        sums[d, h, own_half, :] = attend(qt[own_half, pair_columns(pairs[d])], pairs[d], h, early, keep)
+
+    def far_early(d, h):
+        keep = [far_rows] if d == 0 else []
+        sums[d, h, far_half, :] = attend(qt[far_half, pair_columns(pairs[d])], pairs[d], h, early, keep)
+
+    def all_late(d, h, keys):
+        keep = [rows_of(0, c), rows_of(1, c)] if d == 0 else []
+        return sums[d, h] + attend(qt[:, pair_columns(pairs[d])], pairs[d], h, keys, keep)
 
     project(x, c, True)
     for i, h in in_turn:
-        arrived(half(xb.at[x, 2 * (1 - c) + i], h), NUM["core_own"] + 2 * i + h)
+        arrived(half(xb.at[x, 2 * (1 - c) + i], h), NUM["core_own"] + PIECES * i + h)
     project(x, 1 - c, False)
     for at, (i, h) in enumerate(in_turn):
-        early_part(at, 0)
-        early_part(at, 1)
+        if at % (PIECES // 2) == 0:
+            own_early(at // (PIECES // 2), 0)
+            own_early(at // (PIECES // 2), 1)
         block = half(xb.at[1 - x, 2 * c + i], h)
-        arrived(block, NUM["xn"] + 2 * i + h)
-        number = NUM["core_far"] + 2 * i + h
+        arrived(block, NUM["xn"] + PIECES * i + h)
+        number = NUM["core_far"] + PIECES * i + h
         send(block, block, number, number, core_dev)
     project(1 - x, c, True)
+    for d in range(4):
+        for h in range(2):
+            far_early(d, h)
+            sums[d, h] = all_late(d, h, far_rows)
     for i, h in in_turn:
-        arrived(half(xb.at[1 - x, 2 * (1 - c) + i], h), NUM["core_far"] + 2 * i + h)
+        arrived(half(xb.at[1 - x, 2 * (1 - c) + i], h), NUM["core_far"] + PIECES * i + h)
     project(1 - x, 1 - c, False)
-    def forward_cot(i):
-        @pl.when(2 * c + i != z)
-        def _():
-            arrived(cotb.at[x, i], NUM["cot"] + i)
-
-        @pl.when(2 * c + i == z)
-        def _():
-            self_cot.wait()
-
-        send(cotb.at[x, i], cotb.at[x, i], NUM["cot_x"] + i, NUM["cot_x"] + i, x_dev)
-
 
     for d in range(4):
-        sums_all = [sums[d, h] + attend(qt[own_half, pair_columns(pairs[d])], pairs[d], h, late,
-                                        own_rows if d == 0 else None) for h in range(2)]
-        abuf[own_half, pair_columns(pairs[d])] = attended_of(sums_all, own_rows if d == 0 else None)
-    forward_cot(first)
-    for d in range(4):
-        sums_all = [attend(qt[far_half, pair_columns(pairs[d])], pairs[d], h, every,
-                           far_rows if d == 0 else None) for h in range(2)]
-        abuf[far_half, pair_columns(pairs[d])] = attended_of(sums_all, far_rows if d == 0 else None)
-        if d == 1:
-            forward_cot(1 - first)
+        parts = [all_late(d, h, rows_of(1 - x, 1 - c)) for h in range(2)]
+        for xx in (0, 1):
+            there = pl.ds(256 * xx, 256)
+            abuf[there, pair_columns(pairs[d])] = attended_of(
+                [part[256 * xx : 256 * xx + 256] for part in parts], rows_of(xx, c) if d == 0 else None
+            )
 
     def other_probs(xx):
         rows = rows_of(xx, 1 - c)
-        attended_of([attend(q[rows, :], me, h, every, rows) for h in range(2)], rows)
+        attended_of([attend(q[rows, :], me, h, every, [rows]) for h in range(2)], rows)
 
     def norm(hidden):
         centred = hidden - jnp.mean(hidden, axis=-1, keepdims=True)
@@ -696,31 +700,28 @@
 
     once = jnp.where(x == 0, 1.0, 0.0)
     land(wait_ffn)
-    s1_parts = []
     for xx in (0, 1):
         there = pl.ds(256 * xx, 256)
-
         start_x = xb[xx, pl.ds(2 * c, 2)].reshape(256, 512).astype(f32) + pair_row
         normalized, s1 = norm(start_x + (mm(abuf[there, :], wo[...]) + ob[...]))
-        s1_parts.append(s1)
+        s1b[there, :] = jnp.broadcast_to(s1, (256, 128))
         n1[there, :] = normalized
         normed = normalized * g1[...] + b1[...]
-        low = normed.astype(bf16)
-        normed_low[there, :] = low
-        ffn = jnp.zeros((256, 512), f32)
-        for j in range(4):
-            cols = pl.ds(512 * j, 512)
-            pre = mm(low, wup[:, cols]) + ub[:, cols]
-            cdf = 0.5 * (1.0 + lax.erf(pre * 0.7071067811865476))
-            gelu_grad[there, cols] = cdf + pre * (jnp.exp(-0.5 * pre * pre) * 0.3989422804014327)
-            act_low = (pre * cdf).astype(bf16)
-            act[there, cols] = act_low
-            ffn = ffn + mm(act_low, wdn[cols, :])
-        normalized, s2 = norm((ffn + db[...]) + normed + start_x)
+        normed_low[there, :] = normed.astype(bf16)
+        normed_grad[there, :] = normed + start_x
+    for j in range(4):
+        cols = pl.ds(512 * j, 512)
+        pre = mm(normed_low[...], wup[:, cols]) + ub[:, cols]
+        before[:, cols] = pre
+        act_low = (pre * (0.5 * (1.0 + lax.erf(pre * 0.7071067811865476)))).astype(bf16)
+        act[:, cols] = act_low
+        term = mm(act_low, wdn[cols, :])
+        second[...] = term if j == 0 else second[...] + term
+    for xx in (0, 1):
+        there = pl.ds(256 * xx, 256)
+        normalized, s2 = norm((second[there, :] + db[...]) + normed_grad[there, :])
         n2[there, :] = normalized
         s2b[there, :] = jnp.broadcast_to(s2, (256, 128))
-    lob[...] = (n2[own_half, :] * g2[...] + b2[...]).astype(bf16).reshape(2, 128, 512)
-
     def give_back(block, out, name):
         for i in (0, 1):
             send(block.at[i], out.at[z % 2], NUM[name] + i, NUM[name] + z % 2, peer(i), when=2 * c + i != z)
@@ -729,21 +730,24 @@
         def _():
             out[z % 2] = block[z % 2]
 
-    give_back(lob, lo_out, "lo")
+    def layer_back():
+        lob[...] = (n2[own_half, :] * g2[...] + b2[...]).astype(bf16).reshape(2, 128, 512)
+        give_back(lob, lo_out, "lo")
+
+    for i in (0, 1):
+        @pl.when(2 * c + i != z)
+        def _():
+            arrived(cotb.at[x, i], NUM["cot"] + i)
     for turn, (xx, there) in enumerate(((x, own_half), (1 - x, far_half))):
         if turn == 1:
             for i in (0, 1):
                 arrived(cotb.at[1 - x, i], NUM["cot_x"] + i)
         g = cotb[xx].reshape(256, 512).astype(f32)
         normalized = n2[there, :]
-        gain_part, bias_part = column_sum(g * normalized), column_sum(g)
         grad = norm_back(g, normalized, s2b[there, 0:1], g2[...])
         second[there, :] = grad
         low = grad.astype(bf16)
         ffn_grad[there, :] = low
-        down_part = column_sum(low.astype(f32))
-        for at, part in ((14, gain_part), (15, bias_part), (13, down_part)):
-            vecb[at : at + 1, :] = part * once if turn == 0 else vecb[at : at + 1, :] + part * once
 
     def number(n, step):
         return NUM["lane"] + 12 * n + step
@@ -895,25 +899,21 @@
 
     def ffn_back(j):
         cols = pl.ds(512 * j, 512)
-        for xx in (0, 1):
-            there = pl.ds(256 * xx, 256)
-            grad = (mm_nt(ffn_grad[there, :], wdn[cols, :]) * gelu_grad[there, cols]).astype(bf16)
-            pre_grad[there, cols] = grad
-            part = column_sum(grad.astype(f32)) * once
-            vecb[16 + j : 17 + j, :] = part if xx == 0 else vecb[16 + j : 17 + j, :] + part
-            term = mm_nt(grad, wup[:, cols])
-            normed_grad[there, :] = (second if j == 0 else normed_grad)[there, :] + term
+        pre = before[:, cols]
+        cdf = 0.5 * (1.0 + lax.erf(pre * 0.7071067811865476))
+        slope = cdf + pre * (jnp.exp(-0.5 * pre * pre) * 0.3989422804014327)
+        grad = (mm_nt(ffn_grad[...], wdn[cols, :]) * slope).astype(bf16)
+        pre_grad[:, cols] = grad
+        vecb[16 + j : 17 + j, :] = column_sum(grad.astype(f32)) * once
+        normed_grad[...] = (second if j == 0 else normed_grad)[...] + mm_nt(grad, wup[:, cols])
 
     def first_back():
         for xx in (0, 1):
             there = pl.ds(256 * xx, 256)
             grad, normalized = normed_grad[there, :], n1[there, :]
-            first_grad = norm_back(grad, normalized, s1_parts[xx], g1[...])
+            first_grad = norm_back(grad, normalized, s1b[there, 0:1], g1[...])
             low = first_grad.astype(bf16)
             attn_grad[there, :] = low
-            for at, part in ((11, column_sum(grad * normalized)), (12, column_sum(grad)),
-                             (10, column_sum(low.astype(f32)))):
-                vecb[at : at + 1, :] = part * once if xx == 0 else vecb[at : at + 1, :] + part * once
             second[there, :] = second[there, :] + first_grad
         res[...] = second[own_half, :]
         low = attn_grad[...]
@@ -924,6 +924,15 @@
         dob[...] = mm_nt(low, wo[heads(1 - c), :]).astype(bf16)
         send(dob, dor.at[c], NUM["do"], NUM["do"], core_dev)
         dor[c] = mm_nt(low, wo[heads(c), :]).astype(bf16)
+
+    def norm_sums(which):
+        if which == 0:
+            grad, normalized, low, at = cotb[...].reshape(512, 512).astype(f32), n2[...], ffn_grad[...], 13
+        else:
+            grad, normalized, low, at = normed_grad[...], n1[...], attn_grad[...], 10
+        vecb[at : at + 1, :] = column_sum(low.astype(f32)) * once
+        vecb[at + 1 : at + 2, :] = column_sum(grad * normalized) * once
+        vecb[at + 2 : at + 3, :] = column_sum(grad) * once
 
     turns = ((0, c), (1, c), (0, 1 - c), (1, 1 - c))
 
@@ -1019,10 +1028,10 @@
             else:
                 vec_out[...] = value
 
-    tasks = {(NORM, 0, 0): first_back, (SPLIT, 0, 0): projection_grads, (RETURN, 0, 0): input_out}
+    tasks = {(NORM, 0, 0): first_back, (SPLIT, 0, 0): projection_grads, (RETURN, 0, 0): input_out, (RETURN, 1, 0): layer_back}
     for kind, task, count in (
         (FILL, lane_fill, LANES), (FFN, ffn_back, 4), (ATTN, attention_back, 4), (PROBS, other_probs, 2), (WEIGHT, projection_weights, 3),
-        (INPUT, input_back, 4), (SMALL, vectors, 6),
+        (INPUT, input_back, 4), (SMALL, vectors, 6), (SUMS, norm_sums, 2),
     ):
         for at in range(count):
             tasks[kind, at, 0] = functools.partial(task, at)
@@ -1123,6 +1132,7 @@
     scratch = [
         pltpu.VMEM(shape, dtype)
         for shape, dtype in (
+            ((2, 128, 512), bf16), ((2, 128, 512), bf16),
             ((2, 4, 128, 512), bf16), ((1024, 512), bf16), ((2, 2, 128, 512), bf16),
             ((8, 512), f32), ((8, 512), f32), ((8, 512), f32),
             ((512, 1536), bf16), ((512, 384), bf16), ((512, 512), bf16), ((512, 2048), bf16), ((2048, 512), bf16),
@@ -1131,10 +1141,11 @@
             ((512, 512), bf16), ((1024, 128), bf16), ((1024, 512), bf16),
             ((4, 1024, 256), bf16), ((2, 1024, 128), bf16),
             ((1024, 128), f32), ((1024, 128), f32),
-            ((4, 2, 256, 256), f32), ((512, 512), bf16),
+            ((4, 2, 512, 256), f32), ((512, 512), bf16),
             ((512, 2048), f32), ((512, 2048), bf16), ((512, 2048), bf16),
             ((256, 512), f32), ((2, 128, 512), bf16), ((2, 128, 512), bf16),
-            ((512, 512), f32), ((512, 512), f32), ((512, 128), f32), ((512, 512), bf16),
+            ((512, 512), f32), ((512, 512), f32), ((512, 128), f32), ((512, 128), f32),
+            ((512, 512), bf16),
             ((512, 512), bf16), ((512, 512), bf16), ((512, 512), f32), ((512, 512), f32),
             ((512, 128), bf16), ((2, 512, 128), bf16), ((2, 1024, 1024), bf16),
             ((128, 1024), f32), ((128, 1024), f32), ((1024, 384), bf16),

time: 92.3 us -> 89.5 us (0.970)
  Pallas kernels: 91.2 us -> 88.5 us
    pallas_call x1, Pallas kernels: 86 us -> 83.2 us  [fused_local(): pl.pallas_call(fused, out_shape=out_shape, in_specs=in_specs, out_specs=[...]
where the time goes in v4:
time: 89.5 us; the launch traced here: 89.4 us
  Pallas kernels  88.5 us (99%)
    pallas_call x1, Pallas kernels, fused_local(): pl.pallas_call(fused, out_shape=out_shape, in_specs=in_specs, out_specs=[...  83.2 us
    pallas_call x1, Pallas kernels, fused_local(): pl.pallas_call(finish, out_shape=[jax.ShapeDtypeStruct(shape, f32) for sh...  5.27 us

profile of v4, /device:TPU:1, one launch (start us, length us, event | category | flops | bytes accessed | tf_op | source)
XLA Modules:
  0.0 89.4 jit_solution(2146888656265131733)
XLA Ops:
  0.7 83.2 %shard_map.297 = (bf16[2,128,512]{2,1,0:T(8,128)(2,1)S(1)}, bf16[2,128,512]{2,1,0:T(8,128)(2,1)S(1)}, bf16[9,2,2,2,4,16,512]{6,5,4,3,2,1,0:T(8,128)(2,1)S(1)}, b...) custom-call(bf16[2,128,512]{2,1,0:T(8,128)(2,1)} %x_in.1, bf16[2,128,512]{2,1,0:T(8,128)(2,1)} %cot_in.1, ...), custom_call_target="tpu_custom_call" | custom-call | tf_op jit(solution)/shard_map/pallas_call | solution.py:1163
  83.9 5.3 %shard_map.298 = (f32[2,128,512]{2,1,0:T(8,128)}, f32[2,128,512]{2,1,0:T(8,128)}, f32[2048,512]{1,0:T(8,128)}, f32[512,2048]{1,0:T(8,128)}, f32[512,512]{1,0:T(8...) custom-call(bf16[2,128,512]{2,1,0:T(8,128)(2,1)S(1)} %get-tuple-elem, ...), custom_call_target="tpu_custom_call" | custom-call | tf_op jit(solution)/shard_map/pallas_call | solution.py:1176

commit v5 on v4

--- a/solution.py
+++ b/solution.py
@@ -403,30 +403,30 @@
 LOCAL = 19
 
 SCATTER = ('yz', 'yz', 'yz', 'yz', 'yw', 'yw', 'yw', 'yw', 'yw')
-GATHER = ('wxy', 'wxy', 'wyx', 'wyx', 'wyx', 'zyx', 'zxy', 'zxy', 'zyx')
+GATHER = ('wyx', 'wxy', 'zxy', 'wyx', 'wxy', 'zyx', 'zyx', 'zxy', 'zyx')
 QSCATTER = ('yw', 'yw', 'yw')
-QGATHER = ('zxy', 'zyx', 'wxy')
+QGATHER = ('wxy', 'zxy', 'zyx')
 FILL, LANE, FFN, NORM, ATTN, SPLIT, WEIGHT, PART, INPUT, RETURN, SMALL, PROBS, SUMS = range(13)
 ORDER = (
-    (RETURN, 1, 0), (FILL, 0, 0), (FFN, 0, 0), (FILL, 3, 0), (FILL, 2, 0), (LANE, 0, 0), (FILL, 1, 0),
-    (FFN, 1, 0), (LANE, 3, 0), (LANE, 2, 0), (FFN, 2, 0), (LANE, 1, 0), (FFN, 3, 0), (FILL, 5, 0),
-    (FILL, 7, 0), (PROBS, 1, 0), (LANE, 0, 1), (NORM, 0, 0), (FILL, 6, 0), (LANE, 5, 0), (LANE, 3, 1),
-    (ATTN, 0, 0), (FILL, 4, 0), (LANE, 2, 1), (ATTN, 1, 0), (LANE, 6, 0), (LANE, 4, 0), (LANE, 1, 1),
-    (PROBS, 0, 0), (ATTN, 2, 0), (LANE, 5, 1), (LANE, 7, 0), (LANE, 0, 2), (LANE, 3, 2), (ATTN, 3, 0),
-    (SPLIT, 0, 0), (INPUT, 0, 0), (LANE, 2, 2), (FILL, 8, 0), (WEIGHT, 0, 0), (LANE, 6, 1), (LANE, 5, 2),
-    (INPUT, 1, 0), (SUMS, 0, 0), (INPUT, 2, 0), (LANE, 8, 0), (LANE, 1, 2), (SUMS, 1, 0), (LANE, 0, 3),
-    (LANE, 4, 1), (WEIGHT, 2, 0), (LANE, 3, 3), (WEIGHT, 1, 0), (INPUT, 3, 0), (LANE, 6, 2), (LANE, 2, 3),
-    (PART, 0, 0), (LANE, 5, 3), (LANE, 0, 4), (SMALL, 0, 0), (LANE, 1, 3), (LANE, 3, 4), (LANE, 7, 1),
-    (SMALL, 1, 0), (PART, 2, 0), (LANE, 8, 1), (PART, 0, 1), (LANE, 4, 2), (LANE, 2, 4), (LANE, 1, 4),
-    (LANE, 6, 3), (LANE, 5, 4), (PART, 2, 1), (LANE, 3, 5), (LANE, 0, 5), (LANE, 8, 2), (SMALL, 2, 0),
-    (PART, 0, 2), (PART, 1, 0), (LANE, 6, 4), (LANE, 4, 3), (PART, 2, 2), (LANE, 7, 2), (LANE, 5, 5),
-    (LANE, 1, 5), (LANE, 8, 3), (PART, 1, 1), (PART, 0, 3), (LANE, 6, 5), (PART, 2, 3), (LANE, 4, 4),
-    (LANE, 2, 5), (LANE, 7, 3), (LANE, 8, 4), (PART, 1, 2), (LANE, 0, 6), (LANE, 4, 5), (PART, 2, 4),
-    (PART, 0, 4), (SMALL, 3, 0), (LANE, 7, 4), (RETURN, 0, 0), (LANE, 8, 5), (LANE, 3, 6), (LANE, 4, 6),
-    (SMALL, 4, 0), (PART, 1, 3), (LANE, 6, 6), (LANE, 7, 5), (LANE, 2, 6), (LANE, 5, 6), (PART, 0, 5),
-    (PART, 1, 4), (PART, 0, 6), (PART, 2, 5), (LANE, 8, 6), (LANE, 7, 6), (LANE, 4, 7), (LANE, 7, 7),
-    (LANE, 6, 7), (LANE, 4, 8), (LANE, 1, 6), (LANE, 8, 7), (PART, 2, 6), (SMALL, 5, 0), (LANE, 3, 7),
-    (LANE, 0, 7), (PART, 1, 5), (LANE, 1, 7), (LANE, 2, 7), (LANE, 5, 7), (PART, 2, 7), (PART, 1, 6),
+    (RETURN, 1, 0), (FILL, 2, 0), (FILL, 1, 0), (FFN, 0, 0), (FILL, 0, 0), (LANE, 2, 0), (LANE, 1, 0),
+    (FFN, 1, 0), (PROBS, 1, 0), (FILL, 4, 0), (FILL, 5, 0), (LANE, 0, 0), (FFN, 2, 0), (FFN, 3, 0),
+    (FILL, 3, 0), (LANE, 2, 1), (LANE, 4, 0), (NORM, 0, 0), (FILL, 8, 0), (LANE, 1, 1), (LANE, 5, 0),
+    (PROBS, 0, 0), (FILL, 6, 0), (FILL, 7, 0), (LANE, 8, 0), (LANE, 0, 1), (LANE, 3, 0), (ATTN, 0, 0),
+    (LANE, 7, 0), (LANE, 4, 1), (LANE, 2, 2), (ATTN, 1, 0), (LANE, 5, 1), (LANE, 6, 0), (LANE, 1, 2),
+    (ATTN, 2, 0), (LANE, 8, 1), (LANE, 0, 2), (LANE, 4, 2), (ATTN, 3, 0), (SPLIT, 0, 0), (LANE, 5, 2),
+    (INPUT, 0, 0), (LANE, 2, 3), (LANE, 3, 1), (WEIGHT, 0, 0), (INPUT, 1, 0), (LANE, 7, 1), (INPUT, 2, 0),
+    (WEIGHT, 1, 0), (WEIGHT, 2, 0), (INPUT, 3, 0), (LANE, 1, 3), (LANE, 0, 3), (LANE, 8, 2), (LANE, 4, 3),
+    (SUMS, 0, 0), (PART, 0, 0), (LANE, 5, 3), (LANE, 3, 2), (LANE, 0, 4), (LANE, 7, 2), (LANE, 2, 4),
+    (LANE, 1, 4), (SUMS, 1, 0), (LANE, 6, 1), (SMALL, 0, 0), (PART, 0, 1), (SMALL, 1, 0), (LANE, 4, 4),
+    (LANE, 8, 3), (PART, 1, 0), (LANE, 0, 5), (LANE, 5, 4), (PART, 2, 0), (LANE, 6, 2), (LANE, 7, 3),
+    (LANE, 1, 5), (LANE, 3, 3), (PART, 0, 2), (LANE, 4, 5), (PART, 2, 1), (LANE, 8, 4), (LANE, 5, 5),
+    (PART, 1, 1), (SMALL, 2, 0), (LANE, 6, 3), (LANE, 3, 4), (LANE, 7, 4), (LANE, 4, 6), (PART, 0, 3),
+    (LANE, 8, 5), (PART, 2, 2), (PART, 1, 2), (PART, 0, 4), (LANE, 6, 4), (LANE, 0, 6), (SMALL, 3, 0),
+    (LANE, 2, 5), (LANE, 1, 6), (LANE, 5, 6), (LANE, 7, 5), (LANE, 0, 7), (LANE, 3, 5), (RETURN, 0, 0),
+    (PART, 2, 3), (LANE, 4, 7), (LANE, 4, 8), (PART, 1, 3), (LANE, 8, 6), (LANE, 2, 6), (LANE, 8, 7),
+    (SMALL, 4, 0), (PART, 0, 5), (LANE, 6, 5), (PART, 1, 4), (LANE, 3, 6), (PART, 2, 4), (LANE, 7, 6),
+    (PART, 0, 6), (LANE, 6, 6), (LANE, 5, 7), (LANE, 7, 7), (LANE, 3, 7), (PART, 1, 5), (LANE, 6, 7),
+    (PART, 0, 7), (PART, 2, 5), (LANE, 1, 7), (PART, 1, 6), (SMALL, 5, 0), (PART, 2, 6),
 )
 
 

time: 89.5 us -> 88.7 us (level)
  no operation moved by 1% of the time
where the time goes in v5:
time: 88.7 us; the launch traced here: 88.6 us
  Pallas kernels  87.7 us (99%)
    pallas_call x1, Pallas kernels, fused_local(): pl.pallas_call(fused, out_shape=out_shape, in_specs=in_specs, out_specs=[...  82.5 us
    pallas_call x1, Pallas kernels, fused_local(): pl.pallas_call(finish, out_shape=[jax.ShapeDtypeStruct(shape, f32) for sh...  5.27 us

profile of v5, /device:TPU:1, one launch (start us, length us, event | category | flops | bytes accessed | tf_op | source)
XLA Modules:
  0.0 88.6 jit_solution(4649161764601219937)
XLA Ops:
  0.7 82.5 %shard_map.297 = (bf16[2,128,512]{2,1,0:T(8,128)(2,1)S(1)}, bf16[2,128,512]{2,1,0:T(8,128)(2,1)S(1)}, bf16[9,2,2,2,4,16,512]{6,5,4,3,2,1,0:T(8,128)(2,1)S(1)}, b...) custom-call(bf16[2,128,512]{2,1,0:T(8,128)(2,1)} %x_in.1, bf16[2,128,512]{2,1,0:T(8,128)(2,1)} %cot_in.1, ...), custom_call_target="tpu_custom_call" | custom-call | tf_op jit(solution)/shard_map/pallas_call | solution.py:1163
  83.1 5.3 %shard_map.298 = (f32[2,128,512]{2,1,0:T(8,128)}, f32[2,128,512]{2,1,0:T(8,128)}, f32[2048,512]{1,0:T(8,128)}, f32[512,2048]{1,0:T(8,128)}, f32[512,512]{1,0:T(8...) custom-call(bf16[2,128,512]{2,1,0:T(8,128)(2,1)S(1)} %get-tuple-elem, ...), custom_call_target="tpu_custom_call" | custom-call | tf_op jit(solution)/shard_map/pallas_call | solution.py:1176

commit v6 on v5

--- a/solution.py
+++ b/solution.py
@@ -598,19 +598,23 @@
             there = pl.ds(pl.multiple_of(256 * xx, 256), 256)
             qt[there, :] = (mm(low, wqkv[:, 0:512]) + qb[...]).astype(bf16) * eighth
             q[rows, :] = qt[there, mine]
-        else:
-            q[rows, :] = (mm(low, wq[:, 0:128]) + qb[:, mine]).astype(bf16) * eighth
         k[rows, :] = jnp.where(usable, mm(low, wqkv[:, 512:1024]), 0.0).astype(bf16)
         value = jnp.where(usable, mm(low, wqkv[:, 1024:1536]) + vb[...], 0.0).astype(bf16)
         one = jnp.broadcast_to(jnp.where(usable, 1.0, 0.0), (256, 128))
         for pair in range(4):
             vaug[pair, rows, 0:128] = value[:, 128 * pair : 128 * pair + 128]
             vaug[pair, rows, 128:256] = one.astype(bf16)
-        own_value = vaug[me, rows, 0:128].astype(f32)
-        for h in range(2):
-            edge = 64 * (1 - h)
-            extra = jnp.where((lane == edge) | (lane == edge + 1), one, 0.0)
-            vback[h, rows, :] = jnp.where(head_lanes[h], own_value, extra).astype(bf16)
+
+    def backward_values():
+        for xx in (0, 1):
+            for cc in (0, 1):
+                rows = pl.ds(512 * xx + 256 * cc, 256)
+                own_value = vaug[me, rows, 0:128].astype(f32)
+                one = vaug[me, rows, 128:256].astype(f32)
+                for h in range(2):
+                    edge = 64 * (1 - h)
+                    extra = jnp.where((lane == edge) | (lane == edge + 1), one, 0.0)
+                    vback[h, rows, :] = jnp.where(head_lanes[h], own_value, extra).astype(bf16)
 
     def attend(q_rows, pair, h, keys, probs_rows):
         columns = pl.ds(pl.multiple_of(128 * pair, 128), 128)
@@ -681,6 +685,8 @@
 
     def other_probs(xx):
         rows = rows_of(xx, 1 - c)
+        projected = mm(lowb[rows, :], wq[:, 0:128]) + qb[:, mine]
+        q[rows, :] = projected.astype(bf16) * jnp.asarray(0.125, bf16)
         attended_of([attend(q[rows, :], me, h, every, [rows]) for h in range(2)], rows)
 
     def norm(hidden):
@@ -916,6 +922,7 @@
             attn_grad[there, :] = low
             second[there, :] = second[there, :] + first_grad
         res[...] = second[own_half, :]
+        backward_values()
         low = attn_grad[...]
 
         def heads(cc):

time: 88.7 us -> 88.7 us (level)
  no operation moved by 1% of the time
where the time goes in v6:
time: 88.7 us; the launch traced here: 88.6 us
  Pallas kernels  87.7 us (99%)
    pallas_call x1, Pallas kernels, fused_local(): pl.pallas_call(fused, out_shape=out_shape, in_specs=in_specs, out_specs=[...  82.4 us
    pallas_call x1, Pallas kernels, fused_local(): pl.pallas_call(finish, out_shape=[jax.ShapeDtypeStruct(shape, f32) for sh...  5.27 us

profile of v6, /device:TPU:1, one launch (start us, length us, event | category | flops | bytes accessed | tf_op | source)
XLA Modules:
  0.0 88.6 jit_solution(10570735072035363315)
XLA Ops:
  0.7 82.4 %shard_map.297 = (bf16[2,128,512]{2,1,0:T(8,128)(2,1)S(1)}, bf16[2,128,512]{2,1,0:T(8,128)(2,1)S(1)}, bf16[9,2,2,2,4,16,512]{6,5,4,3,2,1,0:T(8,128)(2,1)S(1)}, b...) custom-call(bf16[2,128,512]{2,1,0:T(8,128)(2,1)} %x_in.1, bf16[2,128,512]{2,1,0:T(8,128)(2,1)} %cot_in.1, ...), custom_call_target="tpu_custom_call" | custom-call | tf_op jit(solution)/shard_map/pallas_call | solution.py:1170
  83.1 5.3 %shard_map.298 = (f32[2,128,512]{2,1,0:T(8,128)}, f32[2,128,512]{2,1,0:T(8,128)}, f32[2048,512]{1,0:T(8,128)}, f32[512,2048]{1,0:T(8,128)}, f32[512,512]{1,0:T(8...) custom-call(bf16[2,128,512]{2,1,0:T(8,128)(2,1)S(1)} %get-tuple-elem, ...), custom_call_target="tpu_custom_call" | custom-call | tf_op jit(solution)/shard_map/pallas_call | solution.py:1183
